TPU v7x, 32 devices: a whole 2x2x4 slice. The times are simulated.
32 devices in a mesh: dp: 8 (over y, x, core), expert: 4 (over z).
Axes of the slice: x: 2, y: 2, z: 4, core: 2. Of those that a mesh axis runs over, the one named last changes fastest.
Arguments:
- tokens: bfloat16 [8192, 1536], P(('dp', 'expert')), may hold values from -6 to 6
- cotangent: bfloat16 [8192, 1536], P(('dp', 'expert')), may hold values from -6 to 6
- norm_attn: bfloat16 [1536], P('dp'), may hold values from 0.5 to 1.5
- norm_moe: bfloat16 [1536], P('dp'), may hold values from 0.5 to 1.5
- w_query: bfloat16 [1536, 1536], P('dp'), may hold values from -0.3984375 to 0.3984375
- w_key: bfloat16 [1536, 512], P('dp'), may hold values from -0.3984375 to 0.3984375
- w_value: bfloat16 [1536, 512], P('dp'), may hold values from -0.15625 to 0.15625
- w_out: bfloat16 [1536, 1536], P('dp'), may hold values from -3 to 3
- w_router: bfloat16 [1536, 32], P('dp'), may hold values from -0.078125 to 0.078125
- w_gate: bfloat16 [1536, 32, 512], P(None, 'expert'), may hold values from -0.15625 to 0.15625
- w_up: bfloat16 [1536, 32, 512], P(None, 'expert'), may hold values from -0.15625 to 0.15625
- w_down: bfloat16 [1536, 32, 512], P(None, 'expert'), may hold values from -6 to 6
- routes: int32 [8192, 8], P(('dp', 'expert')), may hold values from 0 to 31, all different within a row; in each aligned block of 256 rows (0 to 255, 256 to 511, ...) at most 112 rows name the same one
Outputs:
- output: bfloat16 [8192, 1536], P(('dp', 'expert'))
- grad_tokens: bfloat16 [8192, 1536], P(('dp', 'expert'))
- grad_norm_attn: float32 [1536], P(('dp', 'expert'))
- grad_norm_moe: float32 [1536], P(('dp', 'expert'))
- grad_query: float32 [1536, 1536], P(('dp', 'expert'))
- grad_key: float32 [1536, 512], P(('dp', 'expert'))
- grad_value: float32 [1536, 512], P(('dp', 'expert'))
- grad_out: float32 [1536, 1536], P(('dp', 'expert'))
- grad_router: float32 [1536, 32], P(('dp', 'expert'))
- grad_gate: float32 [1536, 32, 512], P('dp', 'expert')
- grad_up: float32 [1536, 32, 512], P('dp', 'expert')
- grad_down: float32 [1536, 32, 512], P('dp', 'expert')
Inputs may be any that keep to these rules, and one draw needn't show every extreme that they name: `routes`: each row names 8 different experts. Within the rows of one device (aligned blocks of 256 rows) no expert is named by more than 112 rows, and in every draw some expert is named by exactly 112 rows of some block.
All inputs are finite; a program needn't handle non-finite values.
Results may differ from a plain program's by a relative error of at most 0.02.
Values may be sent and summed in bfloat16 or wider, within the bound.
No kernel may reach another device: no remote copies, remote signals or barrier semaphores. Data moves between devices by JAX's collectives and lax.ppermute only.
A program may use at most 384 MiB of HBM per device.

v0:
```python
import jax
import jax.numpy as jnp
from jax import lax
from jax.sharding import PartitionSpec as P

HEADS = 24
KV_HEADS = 8
HEAD_DIM = 64
FF = 512
TOP = 8


RES_MULT = 0.22
ATT_MULT = 0.015625
NORM_EPS = 1e-06
ROPE_BASE = 10000.0


def inverse_rms(hidden):
    return lax.rsqrt(jnp.mean(hidden * hidden, axis=-1, keepdims=True) + NORM_EPS)


def norm_back(hidden, inverse, gain_vector, grad_normed):
    weighted = grad_normed * gain_vector
    return inverse * weighted - hidden * inverse**3 * jnp.mean(
        weighted * hidden, axis=-1, keepdims=True
    )


def rope_tables(positions, head_width):
    half_width = head_width // 2
    frequency = ROPE_BASE ** (-(jnp.arange(half_width, dtype=jnp.float32) * 2.0 / head_width))
    angles = positions.astype(jnp.float32)[:, None] * frequency[None, :]
    angles = jnp.concatenate([angles, angles], axis=1)
    return (jnp.cos(angles)[:, None, :], jnp.sin(angles)[:, None, :])


def rotate_half(values):
    half_width = values.shape[-1] // 2
    return jnp.concatenate([-values[..., half_width:], values[..., :half_width]], axis=-1)


def apply_rope(values, cos_table, sin_table):
    return values * cos_table + rotate_half(values) * sin_table


def undo_rope(grad_values, cos_table, sin_table):
    return grad_values * cos_table - rotate_half(grad_values * sin_table)


def route_slots(routes, experts):
    flat_routes = routes.reshape(-1)
    onehot = (flat_routes[:, None] == jnp.arange(experts, dtype=jnp.int32)[None, :]).astype(
        jnp.int32
    )
    earlier = jnp.cumsum(onehot, axis=0) - onehot
    return jnp.sum(earlier * onehot, axis=1).reshape(routes.shape)


def body(
    tokens,
    cotangent,
    norm_attn,
    norm_moe,
    w_query,
    w_key,
    w_value,
    w_out,
    w_router,
    w_gate,
    w_up,
    w_down,
    routes,
):
    local_rows = tokens.shape[0]
    model_width = tokens.shape[1]
    expert_count = lax.axis_size("expert")
    local_experts = w_gate.shape[1]
    expert_total = local_experts * expert_count
    capacity = min(local_rows, max(2, local_rows * TOP * 7 // (4 * expert_total)))
    query_width = w_query.shape[1]
    key_width = w_key.shape[1]
    group_size = HEADS // KV_HEADS
    seq_length = local_rows * expert_count
    offset = lax.axis_index("expert") * local_rows
    query_pos = offset + jnp.arange(local_rows, dtype=jnp.int32)
    key_pos = jnp.arange(seq_length, dtype=jnp.int32)
    causal = key_pos[None, :] <= query_pos[:, None]
    cos_table, sin_table = rope_tables(query_pos, HEAD_DIM)
    qkv_shard = jnp.concatenate([w_query, w_key, w_value], axis=1)
    gain_attn, gain_moe, qkv_full, out_full, router_full = (
        lax.all_gather(norm_attn, "dp", axis=0, tiled=True),
        lax.all_gather(norm_moe, "dp", axis=0, tiled=True),
        lax.all_gather(qkv_shard, "dp", axis=0, tiled=True),
        lax.all_gather(w_out, "dp", axis=0, tiled=True),
        lax.all_gather(w_router, "dp", axis=0, tiled=True),
    )
    gain_one = gain_attn.astype(jnp.float32)
    gain_two = gain_moe.astype(jnp.float32)
    hidden = tokens.astype(jnp.float32)
    inverse_one = inverse_rms(hidden)
    normed_one = (hidden * inverse_one * gain_one).astype(jnp.bfloat16)
    projected = jnp.dot(normed_one, qkv_full, preferred_element_type=jnp.float32)
    query_rope = apply_rope(
        projected[:, :query_width].reshape(local_rows, HEADS, HEAD_DIM), cos_table, sin_table
    )
    query_rope = query_rope.astype(jnp.bfloat16).reshape(local_rows, query_width)
    key_rope = apply_rope(
        projected[:, query_width : query_width + key_width].reshape(local_rows, KV_HEADS, HEAD_DIM),
        cos_table,
        sin_table,
    )
    key_rope = key_rope.astype(jnp.bfloat16).reshape(local_rows, key_width)
    value_rows = projected[:, query_width + key_width :].astype(jnp.bfloat16)
    keys_all, values_all = (
        lax.all_gather(key_rope, "expert", axis=0, tiled=True),
        lax.all_gather(value_rows, "expert", axis=0, tiled=True),
    )

    def head_inputs(head_index):
        query_head = lax.dynamic_slice_in_dim(
            query_rope, head_index * group_size * HEAD_DIM, group_size * HEAD_DIM, 1
        )
        key_head = lax.dynamic_slice_in_dim(keys_all, head_index * HEAD_DIM, HEAD_DIM, 1)
        value_head = lax.dynamic_slice_in_dim(values_all, head_index * HEAD_DIM, HEAD_DIM, 1)
        return (query_head.reshape(local_rows, group_size, HEAD_DIM), key_head, value_head)

    def head_forward(head_index):
        query_head, key_head, value_head = head_inputs(head_index)
        scores = (
            jnp.einsum("rgd,nd->grn", query_head, key_head, preferred_element_type=jnp.float32)
            * ATT_MULT
        )
        masked = jnp.where(causal[None], scores, -1e30)
        row_peak = jnp.max(masked, axis=-1, keepdims=True)
        exponent = jnp.where(causal[None], jnp.exp(masked - row_peak), 0.0)
        row_total = jnp.sum(exponent, axis=-1, keepdims=True)
        probability = (exponent / row_total).astype(jnp.bfloat16)
        mixed_head = jnp.einsum(
            "grn,nd->rgd", probability, value_head, preferred_element_type=jnp.float32
        )
        return (
            mixed_head.reshape(local_rows, group_size * HEAD_DIM),
            (row_peak + jnp.log(row_total))[..., 0],
        )

    mixed_heads, log_totals = lax.map(head_forward, jnp.arange(KV_HEADS, dtype=jnp.int32))
    attended = (
        jnp.transpose(mixed_heads, (1, 0, 2)).reshape(local_rows, query_width).astype(jnp.bfloat16)
    )
    middle = hidden + RES_MULT * jnp.dot(attended, out_full, preferred_element_type=jnp.float32)
    inverse_two = inverse_rms(middle)
    normed_two = (middle * inverse_two * gain_two).astype(jnp.bfloat16)
    logits = jnp.dot(normed_two, router_full, preferred_element_type=jnp.float32)
    gate_probs = jax.nn.softmax(jnp.take_along_axis(logits, routes, axis=1), axis=1)
    slot_pos = route_slots(routes, expert_total)
    target = routes * capacity + slot_pos
    slot_ids = jnp.arange(expert_total * capacity, dtype=jnp.int32)
    slot_match = slot_ids[:, None, None] == target[None, :, :]
    placement = jnp.any(slot_match, axis=2).astype(jnp.bfloat16)
    slot_gate = jnp.sum(jnp.where(slot_match, gate_probs[None], 0.0), axis=(1, 2))
    slot_token = jnp.sum(
        jnp.where(slot_match, jnp.arange(local_rows, dtype=jnp.int32)[None, :, None], 0),
        axis=(1, 2),
    )
    dispatched = jnp.dot(placement, normed_two, preferred_element_type=jnp.float32).astype(
        jnp.bfloat16
    )
    dispatched = dispatched.reshape(expert_count, local_experts, capacity, model_width)
    expert_received = lax.all_to_all(dispatched, "expert", split_axis=0, concat_axis=0, tiled=True)
    gate_pre = jnp.einsum(
        "secd,def->secf", expert_received, w_gate, preferred_element_type=jnp.float32
    )
    up_pre = jnp.einsum("secd,def->secf", expert_received, w_up, preferred_element_type=jnp.float32)
    expert_active = (jax.nn.silu(gate_pre) * up_pre).astype(jnp.bfloat16)
    expert_out = jnp.einsum(
        "secf,def->secd", expert_active, w_down, preferred_element_type=jnp.float32
    ).astype(jnp.bfloat16)
    returned = lax.all_to_all(expert_out, "expert", split_axis=0, concat_axis=0, tiled=True)
    returned, received, gate_pre, up_pre, active = (
        returned,
        expert_received,
        gate_pre,
        up_pre,
        expert_active,
    )
    expert_rows = returned.reshape(expert_total * capacity, model_width)
    picked = (
        jnp.take(expert_rows, target.reshape(-1), axis=0)
        .reshape(local_rows, TOP, model_width)
        .astype(jnp.float32)
    )
    output = middle + RES_MULT * jnp.sum(picked * gate_probs[:, :, None], axis=1)
    grad_output = cotangent.astype(jnp.float32)
    grad_mix = RES_MULT * grad_output
    grad_gp = jnp.sum(picked * grad_mix[:, None, :], axis=2)
    grad_chosen = gate_probs * (grad_gp - jnp.sum(gate_probs * grad_gp, axis=1, keepdims=True))
    route_hot = (
        routes[:, :, None] == jnp.arange(expert_total, dtype=jnp.int32)[None, None, :]
    ).astype(jnp.float32)
    grad_logits = jnp.sum(route_hot * grad_chosen[:, :, None], axis=1).astype(jnp.bfloat16)
    slot_grads = (slot_gate[:, None] * jnp.take(grad_mix, slot_token, axis=0)).astype(jnp.bfloat16)
    slot_grads = slot_grads.reshape(expert_count, local_experts, capacity, model_width)
    arrived = lax.all_to_all(slot_grads, "expert", split_axis=0, concat_axis=0, tiled=True)
    grad_active = jnp.einsum("secd,def->secf", arrived, w_down, preferred_element_type=jnp.float32)
    sigmoid_gate = jax.nn.sigmoid(gate_pre)
    gate_back = (
        grad_active * up_pre * sigmoid_gate * (1.0 + gate_pre * (1.0 - sigmoid_gate))
    ).astype(jnp.bfloat16)
    up_back = (grad_active * gate_pre * sigmoid_gate).astype(jnp.bfloat16)
    slot_back = (
        jnp.einsum("secf,def->secd", gate_back, w_gate, preferred_element_type=jnp.float32)
        + jnp.einsum("secf,def->secd", up_back, w_up, preferred_element_type=jnp.float32)
    ).astype(jnp.bfloat16)
    grad_slots = lax.all_to_all(
        slot_back, "expert", split_axis=0, concat_axis=0, tiled=True
    ).reshape(expert_total * capacity, model_width)
    grad_normed_two = jnp.einsum(
        "sr,sd->rd", placement, grad_slots, preferred_element_type=jnp.float32
    ) + jnp.einsum("rx,dx->rd", grad_logits, router_full, preferred_element_type=jnp.float32)
    grad_router = jnp.einsum(
        "rd,rx->dx", normed_two, grad_logits, preferred_element_type=jnp.float32
    )
    grad_gain_two = jnp.sum(grad_normed_two * middle * inverse_two, axis=0)
    grad_middle = grad_output + norm_back(middle, inverse_two, gain_two, grad_normed_two)
    branch_back = (RES_MULT * grad_middle).astype(jnp.bfloat16)
    grad_wout = jnp.einsum("rq,rd->qd", attended, branch_back, preferred_element_type=jnp.float32)
    attended_back = jnp.einsum(
        "rd,qd->rq",
        branch_back,
        lax.all_gather(w_out, "dp", axis=0, tiled=True),
        preferred_element_type=jnp.float32,
    )
    attended_back = attended_back.astype(jnp.bfloat16)

    def head_backward(head_index):
        query_head, key_head, value_head = head_inputs(head_index)
        grad_head = lax.dynamic_slice_in_dim(
            attended_back, head_index * group_size * HEAD_DIM, group_size * HEAD_DIM, 1
        )
        grad_head = grad_head.reshape(local_rows, group_size, HEAD_DIM)
        scores = (
            jnp.einsum("rgd,nd->grn", query_head, key_head, preferred_element_type=jnp.float32)
            * ATT_MULT
        )
        shifted = jnp.where(causal[None], scores - log_totals[head_index][..., None], -1e30)
        probs_full = jnp.where(causal[None], jnp.exp(shifted), 0.0)
        probs_back = jnp.einsum(
            "rgd,nd->grn", grad_head, value_head, preferred_element_type=jnp.float32
        )
        row_delta = jnp.sum(probs_full * probs_back, axis=-1, keepdims=True)
        scores_back = (probs_full * (probs_back - row_delta)).astype(jnp.bfloat16)
        query_back = (
            jnp.einsum("grn,nd->rgd", scores_back, key_head, preferred_element_type=jnp.float32)
            * ATT_MULT
        )
        return (
            scores_back,
            probs_full.astype(jnp.bfloat16),
            query_back.reshape(local_rows, group_size * HEAD_DIM),
        )

    scores_all, probs_all, query_backs = lax.map(
        head_backward, jnp.arange(KV_HEADS, dtype=jnp.int32)
    )
    query_four = query_rope.reshape(local_rows, KV_HEADS, group_size, HEAD_DIM)
    grad_four = attended_back.reshape(local_rows, KV_HEADS, group_size, HEAD_DIM)
    key_term = (
        jnp.einsum("hgrn,rhgd->nhd", scores_all, query_four, preferred_element_type=jnp.float32)
        * ATT_MULT
    )
    value_term = jnp.einsum(
        "hgrn,rhgd->nhd", probs_all, grad_four, preferred_element_type=jnp.float32
    )
    key_value_back = lax.psum_scatter(
        jnp.concatenate(
            [
                key_term.reshape(lax.axis_size("expert") * local_rows, key_width),
                value_term.reshape(lax.axis_size("expert") * local_rows, key_width),
            ],
            axis=1,
        ).astype(jnp.bfloat16),
        "expert",
        scatter_dimension=0,
        tiled=True,
    ).astype(jnp.float32)
    key_grad_pre = undo_rope(
        key_value_back[:, :key_width].reshape(local_rows, KV_HEADS, HEAD_DIM), cos_table, sin_table
    )
    value_back = key_value_back[:, key_width:]
    query_back = jnp.transpose(query_backs, (1, 0, 2)).reshape(local_rows, HEADS, HEAD_DIM)
    query_grad_pre = undo_rope(query_back, cos_table, sin_table)
    grad_project = jnp.concatenate(
        [
            query_grad_pre.reshape(local_rows, query_width),
            key_grad_pre.reshape(local_rows, key_width),
            value_back,
        ],
        axis=1,
    ).astype(jnp.bfloat16)
    grad_qkv = jnp.einsum("rd,rq->dq", normed_one, grad_project, preferred_element_type=jnp.float32)
    grad_normed_one = jnp.einsum(
        "rq,dq->rd",
        grad_project,
        lax.all_gather(qkv_shard, "dp", axis=0, tiled=True),
        preferred_element_type=jnp.float32,
    )
    grad_gain_one = jnp.sum(grad_normed_one * hidden * inverse_one, axis=0)
    grad_tokens = (grad_middle + norm_back(hidden, inverse_one, gain_one, grad_normed_one)).astype(
        jnp.bfloat16
    )
    gate_term = jnp.einsum(
        "secd,secf->def", received, gate_back, preferred_element_type=jnp.float32
    )
    up_term = jnp.einsum("secd,secf->def", received, up_back, preferred_element_type=jnp.float32)
    down_term = jnp.einsum("secd,secf->def", arrived, active, preferred_element_type=jnp.float32)
    expert_owned = lax.psum_scatter(
        jnp.concatenate([gate_term, up_term, down_term], axis=2).astype(jnp.bfloat16),
        "dp",
        scatter_dimension=0,
        tiled=True,
    ).astype(jnp.float32)
    gain_one_sum, gain_two_sum, qkv_sum, wout_sum, router_sum = (
        lax.psum_scatter(grad_gain_one, ("dp", "expert"), scatter_dimension=0, tiled=True),
        lax.psum_scatter(grad_gain_two, ("dp", "expert"), scatter_dimension=0, tiled=True),
        lax.psum_scatter(grad_qkv, ("dp", "expert"), scatter_dimension=0, tiled=True),
        lax.psum_scatter(grad_wout, ("dp", "expert"), scatter_dimension=0, tiled=True),
        lax.psum_scatter(grad_router, ("dp", "expert"), scatter_dimension=0, tiled=True),
    )
    return (
        output.astype(jnp.bfloat16),
        grad_tokens,
        gain_one_sum,
        gain_two_sum,
        qkv_sum[:, :query_width],
        qkv_sum[:, query_width : query_width + key_width],
        qkv_sum[:, query_width + key_width :],
        wout_sum,
        router_sum,
        expert_owned[:, :, :FF],
        expert_owned[:, :, FF : 2 * FF],
        expert_owned[:, :, 2 * FF :],
    )


def solution(mesh):
    in_specs = (
        P(("dp", "expert"), None),
        P(("dp", "expert"), None),
        P("dp"),
        P("dp"),
        P("dp", None),
        P("dp", None),
        P("dp", None),
        P("dp", None),
        P("dp", None),
        P(None, "expert", None),
        P(None, "expert", None),
        P(None, "expert", None),
        P(("dp", "expert"), None),
    )
    out_specs = (
        P(("dp", "expert"), None),
        P(("dp", "expert"), None),
        P(("dp", "expert")),
        P(("dp", "expert")),
        P(("dp", "expert"), None),
        P(("dp", "expert"), None),
        P(("dp", "expert"), None),
        P(("dp", "expert"), None),
        P(("dp", "expert"), None),
        P("dp", "expert", None),
        P("dp", "expert", None),
        P("dp", "expert", None),
    )
    return jax.shard_map(body, mesh=mesh, in_specs=in_specs, out_specs=out_specs, check_vma=False)
```

profile of v0, /device:TPU:0, one launch (start us, length us, event | category | flops | bytes accessed | tf_op | source)
XLA Modules:
  0.0 2233.2 jit_solution(9880201080715032938)
XLA Ops:
  13.3 15.8 all-reduce.5
  29.9 35.6 %all-gather.6.cloned.1.call-done = bf16[1536,2560]{1,0:T(8,128)(2,1)} async-done(((bf16[192,2560]{1,0:T(8,128)(2,1)}), bf16[1536,2560]{1,0:T(8,128)(2,1)}) %all-gather.6.cloned.1.call-update) | async-done | bytes 7864336 | tf_op jit(solution)/shard_map/all_gather | solution.py:94
  65.5 5.5 fusion.97
  79.5 9.3 reduce-window.6
  89.8 20.1 fusion.33
  125.7 5.3 all-gather.10.cloned.1.call-done
  133.3 57.6 %while.34 = (s32[]{:T(128)}, bf16[8,256,192]{1,2,0:T(8,128)(2,1)S(1)}, f32[8,3,256]{2,1,0:T(4,128)}, s32[8]{0:T(128)S(1)}, bf16[1024,512]{0,1:T(8,128)(2,1)S(1)}...) while((s32[]{:T(128)}, ...), condition=%wide.region_4.5_spmd.clone.clone, body=%wide.region_1.4_spmd.clone.sunk.clone | while | flops 212598016 | bytes 11366633 | solution.py:147
  200.1 243.6 %all_to_all.20 = bf16[4,8,112,1536]{3,2,1,0:T(8,128)(2,1)} all-to-all(bf16[4,8,112,1536]{3,2,1,0:T(8,128)(2,1)S(1)} %bitcast.329), channel_id=1, replica_groups=mesh['dp'=8,'expert'=4] {'expert'}, dimensions={0} | all-to-all | bytes 22020096 | tf_op jit(solution)/shard_map/all_to_all | solution.py:170
  443.7 14.0 fusion.43
  457.7 24.6 %fusion.61 = (bf16[4,8,112,512]{3,2,0,1:T(8,128)(2,1)}, f32[8,4,112,512]{3,2,1,0:T(8,128)}) fusion(f32[8,4,112,512]{3,2,1,0:T(8,128)} %fusion.43, bf16[1536,8,512,1]{2,1,0,3:T(8,128)(2,1)} %bitcast.339, bf16[4,8,112,1536]{3,2,1,0:T(8,128)(2,1)} %all_to_all.20), kind=kOutput, calls=%fused_computation.92 | convolution fusion | flops 5648154624 | bytes 41943040 | tf_op jit(solution)/shard_map/secd,def->secf/dot_general | solution.py:174
  482.3 20.3 fusion.48
  502.5 9.8 copy.229
  512.3 6.2 all-to-all-start.1
  519.1 9.2 all-gather
  528.8 64.8 %select_reduce_fusion = s32[3584]{0:T(1024)S(1)} fusion(s32[256,8]{0,1:T(8,128)S(1)} %get-tuple-element.472), kind=kLoop, calls=%fused_computation.53 | loop fusion | flops 22016512 | bytes 22528 | tf_op jit(solution)/shard_map/reduce_sum | solution.py:162
  593.9 14.0 gather_fusion.1
  608.2 16.8 gather_fusion.2
  625.3 132.0 %all-to-all-done.1 = bf16[4,8,112,1536]{3,2,1,0:T(8,128)(2,1)} async-done(((bf16[4,8,112,1536]{3,2,1,0:T(8,128)(2,1)}), bf16[4,8,112,1536]{3,2,1,0:T(8,128)(2,1)}, u32[]{:S(2)}, u32[]{:S(2)}) %all-to-all-start.1) | async-done | bytes 11010080 | tf_op jit(solution)/shard_map/all_to_all | solution.py:179
  757.3 18.8 gather_fusion
  776.2 5.0 fusion.34
  781.4 27.3 %select_reduce_fusion.1 = f32[3584]{0:T(1024)S(1)} fusion(f32[256,8]{0,1:T(8,128)S(1)} %get-tuple-element.470, s32[256,8]{0,1:T(8,128)S(1)} %get-tuple-element.472), kind=kLoop, calls=%fused_computation.54 | loop fusion | flops 22016512 | bytes 30720 | tf_op jit(solution)/shard_map/reduce_sum | solution.py:161
  808.7 9.1 multiply_convert_fusion
  817.8 243.2 %all_to_all.21 = bf16[4,8,112,1536]{3,2,1,0:T(8,128)(2,1)} all-to-all(bf16[4,8,112,1536]{3,2,1,0:T(8,128)(2,1)S(1)} %multiply_convert_fusion), channel_id=1, replica_groups=mesh['dp'=8,'expert'=4] {'expert'}, dimensions={0} | all-to-all | bytes 22020096 | tf_op jit(solution)/shard_map/all_to_all | solution.py:204
  1061.0 33.5 %fusion.60 = (bf16[4,8,112,512]{3,2,0,1:T(8,128)(2,1)}, bf16[4,8,112,512]{3,2,0,1:T(8,128)(2,1)}) fusion(f32[8,4,112,512]{3,2,1,0:T(8,128)} %fusion.43, f32[8,4,112,512]{3,2,1,0:T(8,128)} %get-tuple-element.508, bf16[1536,8,512,1]{2,1,0,3:T(8,128)(2,1)} %bitcast.362, bf16[4,8,112,1536]{3,2,1,0:T(8,128)(2,1)} %all_to_all.21), kind=kOutput, calls=%fused_computation.90 | convolution fusion | flops 5660999680 | bytes 45613056 | tf_op jit(solution)/shard_map/secd,def->secf/dot_general | solution.py:205
  1094.5 22.3 fusion.41
  1116.8 22.4 %fusion.51 = bf16[4,8,112,1536]{3,2,0,1:T(8,128)(2,1)} fusion(f32[8,4,112,1536]{3,2,1,0:T(8,128)} %fusion.41, bf16[4,8,112,512]{3,2,0,1:T(8,128)(2,1)} %get-tuple-element.480, bf16[1536,8,512,1]{2,1,0,3:T(8,128)(2,1)} %bitcast.340), kind=kOutput, calls=%fused_computation.81 | convolution fusion | flops 5648154624 | bytes 49283072 | tf_op jit(solution)/shard_map/secf,def->secd/dot_general | solution.py:213
  1139.2 9.8 copy.239
  1148.9 6.2 all-to-all-start.3
  1155.4 16.2 multiply_reduce_fusion
  1171.6 221.8 %all-to-all-done.3 = bf16[4,8,112,1536]{3,2,1,0:T(8,128)(2,1)} async-done(((bf16[4,8,112,1536]{3,2,1,0:T(8,128)(2,1)}), bf16[4,8,112,1536]{3,2,1,0:T(8,128)(2,1)}, u32[]{:S(2)}, u32[]{:S(2)}) %all-to-all-start.3) | async-done | bytes 11010080 | tf_op jit(solution)/shard_map/all_to_all | solution.py:215
  1393.5 6.1 fusion.119
  1406.1 109.8 %while.35 = (s32[]{:T(128)}, bf16[8,3,256,1024]{2,3,1,0:T(8,128)(2,1)}, bf16[8,3,256,1024]{2,3,1,0:T(8,128)(2,1)}, f32[8,256,192]{1,2,0:T(8,128)}, s32[8]{0:T(12...) while((s32[]{:T(128)}, ...), condition=%wide.region_21.22_spmd.clone.clone, body=%wide.region_19.21_spmd.clone.sunk.clone | while | flops 310164736 | bytes 24133916 | solution.py:263
  1516.0 8.8 bitcast_convert_fusion.3
  1524.9 8.5 fusion.70
  1537.3 40.7 %reduce-scatter.8.cloned.1.call-done = bf16[256,1024]{0,1:T(8,128)(2,1)} async-done(((bf16[1024,1024]{0,1:T(8,128)(2,1)}), bf16[256,1024]{0,1:T(8,128)(2,1)}) %reduce-scatter.8.cloned.1.call-update) | async-done | bytes 524304 | tf_op jit(solution)/shard_map/reduce_scatter | solution.py:275
  1579.4 7.9 fusion.88
  1587.4 14.6 fusion.47
  1602.0 14.4 fusion.46
  1616.4 14.4 fusion.45
  1630.8 25.4 %pad_maximum_fusion = bf16[1536,8,1536]{0,2,1:T(8,128)(2,1)} fusion(bf16[1536,8,512]{0,2,1:T(8,128)(2,1)} %fusion.47, bf16[1536,8,512]{0,2,1:T(8,128)(2,1)} %fusion.46, bf16[1536,8,512]{0,2,1:T(8,128)(2,1)} %fusion.45), kind=kLoop, calls=%fused_computation.52 | loop fusion | flops 113246208 | bytes 75497472 | tf_op jit(solution)/shard_map/concatenate | solution.py:318
  1656.2 49.0 %copy.254 = bf16[1536,8,1536]{2,1,0:T(8,128)(2,1)} copy(bf16[1536,8,1536]{0,2,1:T(8,128)(2,1)} %pad_maximum_fusion) | data formatting | bytes 75497472 | tf_op jit(solution)/shard_map/concatenate | solution.py:318
  1707.1 5.3 fusion.91
  1713.9 7.4 fusion.80
  1721.3 41.4 %all-reduce.4 = (f32[1536]{0:T(1024)S(1)}, f32[1536]{0:T(1024)S(1)}) all-reduce(f32[1536]{0:T(1024)S(1)} %get-tuple-element.423, f32[1536]{0:T(1024)S(1)} %copy-done.40), channel_id=3, replica_groups=mesh['dp'=8,'expert'=4] {'dp','expert'}, use_global_device_ids=true, to_apply=%region_25.26.clone | all-reduce | flops 3072 | bytes 24576
  1766.7 89.2 %reduce-scatter.10.cloned.1.call-done = f32[48,2560]{1,0:T(8,128)} async-done(((f32[1536,2560]{1,0:T(8,128)}), f32[48,2560]{1,0:T(8,128)}) %reduce-scatter.10.cloned.1.call-update) | async-done | bytes 491536 | tf_op jit(solution)/shard_map/reduce_scatter | solution.py:326
  1859.2 224.9 %reduce-scatter.14.cloned.1.call-done = bf16[192,8,1536]{2,1,0:T(8,128)(2,1)} async-done(((bf16[1536,8,1536]{2,1,0:T(8,128)(2,1)}), bf16[192,8,1536]{2,1,0:T(8,128)(2,1)}) %reduce-scatter.14.cloned.1.call-update) | async-done | bytes 4718608 | tf_op jit(solution)/shard_map/reduce_scatter | solution.py:317
  2084.1 6.6 fusion.116
  2090.6 135.6 %reduce-scatter.12.cloned.1.call-done = f32[48,1536]{1,0:T(8,128)} async-done(((f32[1536,1536]{1,0:T(8,128)}), f32[48,1536]{1,0:T(8,128)}) %reduce-scatter.12.cloned.1.call-update) | async-done | bytes 294928 | tf_op jit(solution)/shard_map/reduce_scatter | solution.py:327
  (368 shorter events, 197.6 us)
Async XLA Ops:
  7.2 21.9 copy-start.4
  7.2 58.3 %all-gather.6.cloned.1.call-start = ((), (), s32[]{:S(2)}) async-start(), calls=%async_computation.9 | async-start | bytes 8847360 | tf_op jit(solution)/shard_map/all_gather | solution.py:94
  9.6 114.6 %all-gather.8.cloned.1.call-start = ((), (), s32[]{:S(2)}) async-start(), calls=%async_computation.10 | async-start | bytes 1310720 | tf_op jit(solution)/shard_map/all_gather | solution.py:117
  29.1 41.9 %copy-start.34 = (f32[1536]{0:T(1024)}, f32[1536]{0:T(1024)S(1)}, u32[]{:S(2)}) copy-start(f32[1536]{0:T(1024)S(1)} %convert_element_type.132) | copy-start | bytes 18436
  29.9 41.1 %copy-start.41 = (f32[256]{0:T(256)}, f32[256]{0:T(256)S(1)}, u32[]{:S(2)}) copy-start(f32[256]{0:T(256)S(1)} %get-tuple-element.502) | copy-start | bytes 3076
  73.3 57.7 %all-gather.10.cloned.1.call-start = ((), (), s32[]{:S(2)}) async-start(), calls=%async_computation.11 | async-start | bytes 1310720 | tf_op jit(solution)/shard_map/all_gather | solution.py:116
  73.6 4.2 copy-start.20
  73.6 41.1 %copy-start.22 = (f32[256,64]{0,1:T(8,128)}, f32[256,64]{0,1:T(8,128)S(1)}, u32[]{:S(2)}) copy-start(f32[256,64]{0,1:T(8,128)S(1)} %get-tuple-element.500) | copy-start | bytes 196612
  74.5 2.9 copy-start.31
  76.7 114.2 %all-gather.12.cloned.1.call-start = ((), (), s32[]{:S(2)}) async-start(), calls=%async_computation.12 | async-start | bytes 5308416 | tf_op jit(solution)/shard_map/all_gather | solution.py:95
  79.5 116.6 %copy-start.36 = (f32[1536]{0:T(1024)}, f32[1536]{0:T(1024)S(1)}, u32[]{:S(2)}) copy-start(f32[1536]{0:T(1024)S(1)} %convert_element_type.142) | copy-start | bytes 18436
  114.5 2.4 copy-start.2
  190.9 4.6 copy-start.8
  190.9 4.6 copy-start.28
  190.9 4.6 copy-start.38
  190.9 5.9 copy-start.18
  196.1 4.0 copy-start.44
  196.9 411.1 %copy-start.10 = (bf16[256,1536]{1,0:T(8,128)(2,1)}, bf16[256,1536]{1,0:T(8,128)(2,1)S(1)}, u32[]{:S(2)}) copy-start(bf16[256,1536]{1,0:T(8,128)(2,1)S(1)} %multiply_convert_fusion.2) | copy-start | bytes 2359300
  512.3 6.8 copy-start.43
  512.3 81.4 %copy-start.26 = (bf16[256,1536]{1,0:T(8,128)(2,1)S(1)}, bf16[256,1536]{1,0:T(8,128)(2,1)}, u32[]{:S(2)}) copy-start(bf16[256,1536]{1,0:T(8,128)(2,1)} %param.18) | copy-start | bytes 2359300
  512.3 245.0 %all-to-all-start.1 = ((bf16[4,8,112,1536]{3,2,1,0:T(8,128)(2,1)}), bf16[4,8,112,1536]{3,2,1,0:T(8,128)(2,1)}, u32[]{:S(2)}, u32[]{:S(2)}) async-start(bf16[4,8,112,1536]{3,2,1,0:T(8,128)(2,1)} %copy.229), calls=%async_computation.1 | async-start | bytes 22020096 | tf_op jit(solution)/shard_map/all_to_all | solution.py:179
  519.0 9.3 copy-start.32
  1148.9 6.4 copy-start.33
  1148.9 244.5 %all-to-all-start.3 = ((bf16[4,8,112,1536]{3,2,1,0:T(8,128)(2,1)}), bf16[4,8,112,1536]{3,2,1,0:T(8,128)(2,1)}, u32[]{:S(2)}, u32[]{:S(2)}) async-start(bf16[4,8,112,1536]{3,2,1,0:T(8,128)(2,1)} %copy.239), calls=%async_computation.3 | async-start | bytes 22020096 | tf_op jit(solution)/shard_map/all_to_all | solution.py:215
  1155.1 422.9 %reduce-scatter.8.cloned.1.call-start = ((), (), s32[]{:S(2)}) async-start(), calls=%async_computation.13 | async-start | bytes 2621440 | tf_op jit(solution)/shard_map/reduce_scatter | solution.py:275
  1155.4 238.1 %copy-start.19 = (pred[3584,256]{1,0:T(8,128)(4,1)S(1)}, pred[3584,256]{1,0:T(8,128)(4,1)}, u32[]{:S(2)}) copy-start(pred[3584,256]{1,0:T(8,128)(4,1)} %fusion.33) | copy-start | bytes 2752516
  1155.4 248.2 %slice-start = ((s8[4718592]{0:T(1024)(128)(4,1)}), s8[524288]{0:T(1024)(128)(4,1)S(1)}, s32[]{:S(2)}) async-start(s8[4718592]{0:T(1024)(128)(4,1)} %bitcast.333), calls=%async_computation.18 | async-start | bytes 1048576
  1393.4 6.1 copy-start.1
  1393.4 6.1 copy-start.37
  1393.4 6.1 copy-start.45
  1393.4 10.1 slice-start.1
  1403.5 2.6 copy-start.39
  1515.9 8.9 copy-start.3
  1515.9 8.9 copy-start.14
  1516.0 8.9 copy-start.16
  1516.0 8.9 copy-start.21
  1516.0 8.9 copy-start.23
  1534.9 177.5 %reduce-scatter.16.cloned.1.call-start = ((), (), s32[]{:S(2)}) async-start(), calls=%async_computation.17 | async-start | bytes 811008
  1536.3 319.5 %reduce-scatter.10.cloned.1.call-start = ((), (), s32[]{:S(2)}) async-start(), calls=%async_computation.14 | async-start | bytes 16220160 | tf_op jit(solution)/shard_map/reduce_scatter | solution.py:326
  1537.2 50.1 %copy-start.24 = (bf16[256,1536]{0,1:T(8,128)(2,1)}, bf16[256,1536]{0,1:T(8,128)(2,1)S(1)}, u32[]{:S(2)}) copy-start(bf16[256,1536]{0,1:T(8,128)(2,1)S(1)} %fusion.84) | copy-start | bytes 2359300
  1537.2 42.1 %copy-start.5 = (bf16[256,1536]{1,0:T(8,128)(2,1)S(1)}, bf16[256,1536]{1,0:T(8,128)(2,1)}, u32[]{:S(2)}) copy-start(bf16[256,1536]{1,0:T(8,128)(2,1)} %param.17) | copy-start | bytes 2359300
  1537.2 42.1 %copy-start.35 = (f32[1536]{0:T(1024)S(1)}, f32[1536]{0:T(1024)}, u32[]{:S(2)}) copy-start(f32[1536]{0:T(1024)} %copy-done.34) | copy-start | bytes 18436
  1537.2 42.1 %copy-start.42 = (f32[256]{0:T(256)S(1)}, f32[256]{0:T(256)}, u32[]{:S(2)}) copy-start(f32[256]{0:T(256)} %copy-done.41) | copy-start | bytes 3076
  1579.4 8.0 copy-start.30
  1587.3 496.7 %reduce-scatter.14.cloned.1.call-start = ((), (), s32[]{:S(2)}) async-start(), calls=%async_computation.16 | async-start | bytes 42467328 | tf_op jit(solution)/shard_map/reduce_scatter | solution.py:317
  1705.3 520.9 %reduce-scatter.12.cloned.1.call-start = ((), (), s32[]{:S(2)}) async-start(), calls=%async_computation.15 | async-start | bytes 9732096 | tf_op jit(solution)/shard_map/reduce_scatter | solution.py:327
  1713.9 7.4 copy-start.40
  1713.9 50.0 %copy-start.46 = (f32[256]{0:T(256)S(1)}, f32[256]{0:T(256)}, u32[]{:S(2)}) copy-start(f32[256]{0:T(256)} %get-tuple-element.501) | copy-start | bytes 3076
  (14 other events, 20.0 us)
Sparse Core Ops, SparseCore 0:
  10.5 54.9 all-gather.5
  73.4 27.9 all-gather.7
  103.5 27.4 all-gather.9
  132.7 38.3 all-gather.11
  1535.0 42.8 reduce-scatter.7
  1583.7 94.8 reduce-scatter.15
  1685.7 170.1 reduce-scatter.9
  1859.9 224.1 reduce-scatter.13
  2090.5 135.6 reduce-scatter.11
where the time goes:
time: 2240 us; the launch traced here: 2230 us
  waiting for transfers between devices  886 us (40%)
  blocking collectives  553 us (25%)
  matrix products  304 us (14%)
  other arithmetic  230 us (10%)
  local copies, waits for them, and re-layouts  195 us (9%)
  loops' own time  37.1 us (2%)
    all_to_all x1, blocking collectives, body(): lax.all_to_all(dispatched, 'expert', split_axis=0, concat_axis=0, tiled=T...  244 us
    all_to_all x1, blocking collectives, body(): lax.all_to_all(slot_grads, 'expert', split_axis=0, concat_axis=0, tiled=T...  243 us
    reduce_scatter x1, waiting for transfers between devices, body(): lax.psum_scatter(jnp.concatenate([gate_term, up_term, down_term], axis=2)...  225 us
    all_to_all x1, waiting for transfers between devices, body(): lax.all_to_all(slot_back, 'expert', split_axis=0, concat_axis=0, tiled=True)  222 us
    reduce_scatter x1, waiting for transfers between devices, body(): lax.psum_scatter(grad_wout, ('dp', 'expert'), scatter_dimension=0, tiled=...  136 us
    all_to_all x1, waiting for transfers between devices, body(): lax.all_to_all(expert_out, 'expert', split_axis=0, concat_axis=0, tiled=T...  132 us
    reduce_scatter x1, waiting for transfers between devices, body(): lax.psum_scatter(grad_qkv, ('dp', 'expert'), scatter_dimension=0, tiled=T...  89.2 us
    reduce_sum x1, other arithmetic, body(): jnp.sum(jnp.where(slot_match, jnp.arange(local_rows, dtype=jnp.int32)[Non...  64.8 us
  transfers between devices with their start and end apart: 11, of which 8 were waited for; matrix products, arithmetic and copies ran while one was open for 17% of the time, Pallas kernels for 0%

commit v1 on v0

v1 whole, which is shorter than its diff:
```python
import functools

import jax
import jax.numpy as jnp
from jax import lax
from jax.experimental import pallas as pl
from jax.experimental.pallas import tpu as pltpu
from jax.sharding import PartitionSpec as P

HEADS = 24
KV_HEADS = 8
HEAD_DIM = 64
TOP = 8
GROUP = HEADS // KV_HEADS
PAD = 128
PAIR = 2 * HEAD_DIM


RES_MULT = 0.22
ATT_MULT = 0.015625
NORM_EPS = 1e-06
ROPE_BASE = 10000.0
BF = jnp.bfloat16
F32 = jnp.float32


def dot(a, b, ca=1, cb=0):
    return lax.dot_general(a, b, (((ca,), (cb,)), ((), ())), preferred_element_type=F32)


def inverse_rms(hidden):
    return lax.rsqrt(jnp.mean(hidden * hidden, axis=-1, keepdims=True) + NORM_EPS)


def norm_back(hidden, inverse, gain_vector, grad_normed):
    weighted = grad_normed * gain_vector
    return inverse * weighted - hidden * inverse**3 * jnp.mean(
        weighted * hidden, axis=-1, keepdims=True
    )


def rope_tables(positions):
    half = HEAD_DIM // 2
    frequency = ROPE_BASE ** (-(jnp.arange(half, dtype=F32) * 2.0 / HEAD_DIM))
    angles = positions.astype(F32)[:, None] * frequency[None, :]
    cos, sin = jnp.cos(angles), jnp.sin(angles)
    return jnp.concatenate([cos] * 4, axis=1), jnp.concatenate([-sin, sin] * 2, axis=1)


def swap_halves(x):
    half = HEAD_DIM // 2
    lane = lax.broadcasted_iota(jnp.int32, x.shape, 1)
    return jnp.where(
        lane % HEAD_DIM < half, pltpu.roll(x, PAIR - half, 1), pltpu.roll(x, half, 1)
    )


def rope(x, cos, sin):
    return jnp.concatenate(
        [
            x[:, i : i + PAIR] * cos + swap_halves(x[:, i : i + PAIR]) * sin
            for i in range(0, x.shape[1], PAIR)
        ],
        axis=1,
    )


def causal_bias(me, count, rows):
    query = me * rows + lax.broadcasted_iota(jnp.int32, (rows, count * rows), 0)
    key = lax.broadcasted_iota(jnp.int32, (rows, count * rows), 1)
    source = me - key // rows
    source = jnp.where(source < 0, source + count, source)
    return jnp.where(source * rows + key % rows <= query, 0.0, -1e30)


def front_kernel(count, gain_at, me_ref, *refs):
    token_refs = refs[:count]
    wq_ref, wk_ref, wv_ref, side_ref, cos_ref, sin_ref = refs[count : count + 6]
    normed_ref, side_out, q_ref, k_ref, v_ref, att_ref, lse_ref, bias_ref = refs[count + 6 :]
    rows = token_refs[0].shape[0]

    @pl.when(pl.program_id(0) == 0)
    def _():
        side = side_ref[...].astype(F32).T
        side_out[...] = side
        for s in range(count):
            hidden = token_refs[s][...].astype(F32)
            normed = hidden * inverse_rms(hidden) * side[gain_at : gain_at + 1]
            normed_ref[s * rows : (s + 1) * rows] = normed.astype(BF)
        bias_ref[...] = causal_bias(me_ref[0], count, rows)

    cos, sin = cos_ref[...], sin_ref[...]
    query = rope(dot(normed_ref[:rows], wq_ref[...]), cos[:rows], sin[:rows]).astype(BF)
    query = query * ATT_MULT
    q_ref[...] = query
    both = dot(normed_ref[...], jnp.concatenate([wk_ref[...], wv_ref[...]], axis=1))
    key = rope(both[:, :PAIR], cos, sin).astype(BF)
    value = both[:, PAIR:].astype(BF)
    k_ref[...] = key
    v_ref[...] = value
    lse_ref[...] = jnp.zeros_like(lse_ref)
    for head in range(2 * GROUP):
        at = slice(head * HEAD_DIM, (head + 1) * HEAD_DIM)
        kv_at = slice(head // GROUP * HEAD_DIM, (head // GROUP + 1) * HEAD_DIM)
        scores = dot(query[:, at], key[:, kv_at], 1, 1) + bias_ref[...]
        peak = jnp.max(scores, axis=1, keepdims=True)
        weight = jnp.exp(scores - peak)
        total = jnp.sum(weight, axis=1, keepdims=True)
        probs = (weight * (1.0 / total)).astype(BF)
        att_ref[:, at] = dot(probs, value[:, kv_at]).astype(BF)
        lse_ref[:, head : head + 1] = peak + jnp.log(total)


def run_front(me, tokens, full, cos, sin, query_width, key_width, gain_at):
    count, (rows, width) = len(tokens), tokens[0].shape
    length, pairs, wide = count * rows, key_width // PAIR, GROUP * PAIR
    whole = lambda shape: pl.BlockSpec(shape, lambda p, i: (0, 0))
    column = lambda r, w, first: pl.BlockSpec((r, w), lambda p, i: (0, first + p))
    flops = 2 * width * (rows * query_width + 2 * length * key_width)
    flops += 4 * rows * length * query_width
    return pl.pallas_call(
        functools.partial(front_kernel, count, gain_at),
        grid_spec=pltpu.PrefetchScalarGridSpec(
            num_scalar_prefetch=1,
            grid=(pairs,),
            in_specs=[whole((rows, width))] * count
            + [
                column(width, wide, 0),
                column(width, PAIR, query_width // PAIR),
                column(width, PAIR, (query_width + key_width) // PAIR),
                pl.BlockSpec(
                    (width, PAIR), lambda p, i: (0, (query_width + 2 * key_width) // PAIR)
                ),
                whole((length, PAIR)),
                whole((length, PAIR)),
            ],
            out_specs=[
                whole((length, width)),
                whole((PAIR, width)),
                column(rows, wide, 0),
                column(length, PAIR, 0),
                column(length, PAIR, 0),
                column(rows, wide, 0),
                column(rows, PAIR, 0),
            ],
            scratch_shapes=[pltpu.VMEM((rows, length), F32)],
        ),
        out_shape=[
            jax.ShapeDtypeStruct((length, width), BF),
            jax.ShapeDtypeStruct((PAIR, width), F32),
            jax.ShapeDtypeStruct((rows, query_width), BF),
            jax.ShapeDtypeStruct((length, key_width), BF),
            jax.ShapeDtypeStruct((length, key_width), BF),
            jax.ShapeDtypeStruct((rows, query_width), BF),
            jax.ShapeDtypeStruct((rows, pairs * PAIR), F32),
        ],
        compiler_params=pltpu.CompilerParams(
            dimension_semantics=("arbitrary",), vmem_limit_bytes=56 * 2**20
        ),
        cost_estimate=pl.CostEstimate(
            flops=flops,
            bytes_accessed=4 * (length * width + full.size),
            transcendentals=rows * length * query_width // HEAD_DIM,
        ),
        name="front",
    )(me, *tokens, full, full, full, full, cos, sin)


def back_kernel(count, me_ref, *refs):
    branch_ref, wo_ref, q_ref, k_ref, v_ref, lse_ref, cos_ref, sin_ref, normed_ref = refs[:9]
    dq_ref, dk_ref, dv_ref, keep_ref, send_ref, bias_ref = refs[9:]
    rows = branch_ref.shape[0]

    @pl.when(pl.program_id(0) == 0)
    def _():
        bias_ref[...] = causal_bias(me_ref[0], count, rows)

    grad = dot(branch_ref[...], wo_ref[...], 1, 1).astype(BF)
    query, key, value = q_ref[...], k_ref[...], v_ref[...]
    dqs, dks, dvs = [], [], []
    for head in range(2 * GROUP):
        at = slice(head * HEAD_DIM, (head + 1) * HEAD_DIM)
        kv_at = slice(head // GROUP * HEAD_DIM, (head // GROUP + 1) * HEAD_DIM)
        scores = dot(query[:, at], key[:, kv_at], 1, 1) + bias_ref[...]
        probs = jnp.exp(scores - lse_ref[:, head : head + 1])
        probs_back = dot(grad[:, at], value[:, kv_at], 1, 1)
        delta = jnp.sum(probs * probs_back, axis=1, keepdims=True)
        scores_back = (probs * (probs_back - delta)).astype(BF)
        dqs.append(dot(scores_back, key[:, kv_at]) * ATT_MULT)
        dk = dot(scores_back, query[:, at], 0, 0)
        dv = dot(probs.astype(BF), grad[:, at], 0, 0)
        if head % GROUP == 0:
            dks.append(dk)
            dvs.append(dv)
        else:
            dks[-1] = dks[-1] + dk
            dvs[-1] = dvs[-1] + dv
    cos, sin = cos_ref[...], sin_ref[...]
    dq = rope(jnp.concatenate(dqs, axis=1), cos[:rows], -sin[:rows]).astype(BF)
    dk = rope(jnp.concatenate(dks, axis=1), cos, -sin).astype(BF)
    dv = jnp.concatenate(dvs, axis=1).astype(BF)
    dq_ref[...] = dq
    dk_ref[...] = dk
    dv_ref[...] = dv
    wide = dq.shape[1]
    grad_q = dot(normed_ref[:, :rows], dq).astype(BF)
    grad_kv = dot(normed_ref[...], jnp.concatenate([dk, dv], axis=1)).astype(BF)
    store_slabs(keep_ref, send_ref, me_ref[1], slice(0, wide), grad_q)
    store_slabs(keep_ref, send_ref, me_ref[1], slice(wide, wide + 2 * PAIR), grad_kv)


def out_kernel(total, me_ref, att_ref, branch_ref, normed_ref, logit_ref, gain_ref, *grad_refs):
    width = branch_ref.shape[1]
    router = dot(normed_ref[...].T, logit_ref[...])
    gain = jnp.broadcast_to(gain_ref[0:1], (PAD, width)).T
    lane = lax.broadcasted_iota(jnp.int32, (width, PAD), 1)
    side = jnp.where(lane == total, gain, router).astype(BF)
    main = dot(att_ref[...].T, branch_ref[...]).astype(BF)
    store_slabs(*grad_refs, me_ref[1], slice(0, width), main)
    store_slabs(*grad_refs, me_ref[1], slice(width, width + PAD), side)


def run_out(me, attended, branch, normed, logits, gain, slabs, total):
    rows, width = branch.shape
    inner = attended.shape[1]
    spec = pl.BlockSpec(memory_space=pltpu.VMEM)
    return pl.pallas_call(
        functools.partial(out_kernel, total),
        in_specs=[pl.BlockSpec(memory_space=pltpu.SMEM)] + [spec] * 5,
        out_specs=[spec] * 2,
        out_shape=[jax.ShapeDtypeStruct((slabs // 2, inner // slabs, width + PAD), BF)] * 2,
        compiler_params=pltpu.CompilerParams(vmem_limit_bytes=48 * 2**20),
        cost_estimate=pl.CostEstimate(
            flops=2 * rows * inner * (width + PAD),
            bytes_accessed=2 * (3 * rows * width + inner * (width + PAD)),
            transcendentals=0,
        ),
        name="out_grad",
    )(me, attended, branch, normed, logits, gain)


def run_back(me, branch, out_full, query, key, value, lse, cos, sin, normed_t, slabs):
    (rows, width), (length, key_width) = branch.shape, key.shape
    count, pairs, wide = length // rows, key_width // PAIR, GROUP * PAIR
    whole = lambda shape: pl.BlockSpec(shape, lambda p, i: (0, 0))
    column = lambda r, w: pl.BlockSpec((r, w), lambda p, i: (0, p))
    flops = 2 * width * (2 * rows * query.shape[1] + 2 * length * key_width)
    flops += 10 * rows * length * query.shape[1]
    return pl.pallas_call(
        functools.partial(back_kernel, count),
        grid_spec=pltpu.PrefetchScalarGridSpec(
            num_scalar_prefetch=1,
            grid=(pairs,),
            in_specs=[
                whole((rows, width)),
                pl.BlockSpec((wide, width), lambda p, i: (p, 0)),
                column(rows, wide),
                column(length, PAIR),
                column(length, PAIR),
                column(rows, PAIR),
                whole((length, PAIR)),
                whole((length, PAIR)),
                whole((width, length)),
            ],
            out_specs=[
                column(rows, wide),
                column(length, PAIR),
                column(length, PAIR),
            ]
            + [pl.BlockSpec((slabs // 2, width // slabs, wide + 2 * PAIR), lambda p, i: (0, 0, p))]
            * 2,
            scratch_shapes=[pltpu.VMEM((rows, length), F32)],
        ),
        out_shape=[
            jax.ShapeDtypeStruct(query.shape, BF),
            jax.ShapeDtypeStruct(key.shape, BF),
            jax.ShapeDtypeStruct(key.shape, BF),
        ]
        + [jax.ShapeDtypeStruct((slabs // 2, width // slabs, pairs * (wide + 2 * PAIR)), BF)] * 2,
        compiler_params=pltpu.CompilerParams(
            dimension_semantics=("arbitrary",), vmem_limit_bytes=56 * 2**20
        ),
        cost_estimate=pl.CostEstimate(
            flops=flops,
            bytes_accessed=2 * (length * width + 2 * width * query.shape[1]),
            transcendentals=rows * length * query.shape[1] // HEAD_DIM,
        ),
        name="back",
    )(me, branch, out_full, query, key, value, lse, cos, sin, normed_t)


def line_gather(block, axis, count):
    right, left = [block], [block]
    for step in range(1, count):
        right.append(
            lax.ppermute(right[-1], axis, [(i, i + 1) for i in range(step - 1, count - 1)])
        )
        left.append(lax.ppermute(left[-1], axis, [(i, i - 1) for i in range(1, count - step + 1)]))
    return [block] + [right[s] + left[count - s] for s in range(1, count)]


def line_scatter(parts, axis, count):
    if count == 1:
        return parts[0].astype(F32)
    right, left = parts[1], parts[count - 1]
    for step in range(1, count):
        right = lax.ppermute(right, axis, [(i, i + 1) for i in range(step)])
        left = lax.ppermute(left, axis, [(i, i - 1) for i in range(count - step, count)])
        if step < count - 1:
            right = parts[step + 1] + right
            left = parts[count - 1 - step] + left
    return parts[0].astype(F32) + right.astype(F32) + left.astype(F32)


def upward(block, axis, count, distance=1, first=0):
    pairs = [(i, i + distance) for i in range(first, count - distance)]
    return lax.ppermute(block, axis, pairs)


def downward(block, axis, count, distance=1, last=0):
    pairs = [(i, i - distance) for i in range(distance, count - last)]
    return lax.ppermute(block, axis, pairs)


def send_parts(parts, axis, count):
    return [
        lax.ppermute(parts[s], axis, [(i, (i + count - s) % count) for i in range(count)])
        for s in range(1, count)
    ]


def send_near(parts, axis, count):
    shifts = [s for s in {1: 1, count - 1: 1} if 0 < s < count]
    return [
        lax.ppermute(parts[s], axis, [(i, (i + count - s) % count) for i in range(count)])
        for s in shifts
    ]


def send_far(parts, axis, count):
    return [
        lax.ppermute(part, axis, [(i, (i + count - s) % count) for i in range(count)])
        for s, part in enumerate(parts, 2)
    ]


def add_up(parts):
    total = parts[0].astype(F32)
    for part in parts[1:]:
        total = total + part.astype(F32)
    return total


def trade(keep, send, bit, slabs):
    return keep + lax.ppermute(send, "dp", [(i, i ^ (1 << bit)) for i in range(slabs)])


def halve(x, bits, bit, slabs):
    at = bits.index(bit)
    keep, send = (lax.index_in_dim(x, i, at, False) for i in (0, 1))
    return trade(keep, send, bit, slabs), [b for b in bits if b != bit]


def slab_stages(x, slabs):
    top = slabs.bit_length() - 1
    bits = list(range(top - 1, 0, -1))
    x = x.reshape((2,) * (top - 1) + x.shape[1:])
    one, two = jnp.split(x, 2, axis=len(bits))
    bits_one, bits_two = bits, bits
    for k in range(len(bits)):
        one, bits_one = halve(one, bits_one, k + 1, slabs)
        two, bits_two = halve(two, bits_two, len(bits) - k, slabs)
        one, two = yield one, two


def own_parts(one, two, me, count):
    x = jnp.concatenate([one, two], axis=0)
    own = x.shape[0] // count
    return [
        lax.dynamic_slice_in_dim(x, lax.rem(me + count - s, count) * own, own, 0)
        for s in range(count)
    ]


def store_slabs(keep_ref, send_ref, own, at, value):
    half, slab, _ = keep_ref.shape
    for odd in (0, 1):

        @pl.when(lax.rem(own, 2) == odd)
        def _():
            for d in range(2 * half):
                ref = keep_ref if d % 2 == odd else send_ref
                place = lax.bitwise_xor(jnp.int32(d), own) // 2
                ref[place, :, at] = value[d * slab : (d + 1) * slab]


def expert_kernel(count, total, ei_ref, *refs):
    x_refs, g_refs, p_refs = refs[:count], refs[count : 2 * count], refs[2 * count : 3 * count]
    gate_ref, wg_ref, wu_ref, wd_ref = refs[3 * count : 3 * count + 4]
    outs = refs[3 * count + 4 :]
    out_refs, back_refs, grads_ref = outs[:count], outs[count : 2 * count], outs[2 * count]
    capacity, width = x_refs[0].shape
    expert = ei_ref[0] * pl.num_programs(0) + pl.program_id(0)
    x = jnp.concatenate([r[...] for r in x_refs], axis=0)
    g = jnp.concatenate([r[...] for r in g_refs], axis=0)
    gate = jnp.concatenate(
        [
            jnp.sum(p_refs[s][...].astype(F32) * gate_ref[0, s : s + 1, :], axis=1, keepdims=True)
            for s in range(count)
        ],
        axis=0,
    )
    wg, wu, wd = wg_ref[0], wu_ref[0], wd_ref[0]
    gate_pre = dot(x, wg)
    up_pre = dot(x, wu)
    back_active = dot(g, wd)
    sig = 1.0 / (1.0 + jnp.exp(-gate_pre))
    silu = gate_pre * sig
    active = silu * up_pre
    slot_gate = RES_MULT * gate
    gate_grad = slot_gate * jnp.sum(active * back_active, axis=1, keepdims=True)
    active_low = (active * slot_gate).astype(BF)
    back_active = back_active * slot_gate
    gate_back = (back_active * up_pre * sig * (1.0 + gate_pre * (1.0 - sig))).astype(BF)
    up_back = (back_active * silu).astype(BF)
    out = dot(active_low, wd, 1, 1).astype(BF)
    back = (dot(gate_back, wg, 1, 1) + dot(up_back, wu, 1, 1)).astype(BF)
    lane = lax.broadcasted_iota(jnp.int32, (gate_grad.shape[0], PAD), 1)
    high = gate_grad.astype(BF).astype(F32)
    extra = jnp.where(
        lane == expert, high, jnp.where(lane == total + expert, gate_grad - high, 0.0)
    ).astype(BF)
    for s in range(count):
        rows = slice(s * capacity, (s + 1) * capacity)
        out_refs[s][...] = out[rows]
        back_refs[s][:, :width] = back[rows]
        back_refs[s][:, width:] = extra[rows]
    slabs, rows = grads_ref.shape[0], grads_ref.shape[3]
    for k, (a, b) in enumerate(((x, gate_back), (x, up_back), (g, active_low))):
        grads_ref[:, k, 0] = dot(a, b, 0, 0).astype(BF).reshape(slabs, rows, b.shape[1])


def run_experts(index, xs, gs, places, gates, wg, wu, wd, slabs, total):
    count = len(xs)
    experts, width, hidden = wg.shape
    capacity = xs[0].shape[0] // experts
    block = lambda w: pl.BlockSpec((capacity, w), lambda e, i: (e, 0))
    weight = pl.BlockSpec((1, width, hidden), lambda e, i: (e, 0, 0))
    rows = width // slabs
    flops = 2 * 9 * count * experts * capacity * width * hidden
    return pl.pallas_call(
        functools.partial(expert_kernel, count, total),
        grid_spec=pltpu.PrefetchScalarGridSpec(
            num_scalar_prefetch=1,
            grid=(experts,),
            in_specs=[block(width)] * (2 * count)
            + [block(places[0].shape[1])] * count
            + [pl.BlockSpec((1,) + gates.shape[1:], lambda e, i: (e, 0, 0))]
            + [weight] * 3,
            out_specs=[block(width)] * count
            + [block(width + PAD)] * count
            + [pl.BlockSpec((slabs, 3, 1, rows, hidden), lambda e, i: (0, 0, e, 0, 0))],
        ),
        out_shape=[jax.ShapeDtypeStruct((experts * capacity, width), BF)] * count
        + [jax.ShapeDtypeStruct((experts * capacity, width + PAD), BF)] * count
        + [jax.ShapeDtypeStruct((slabs, 3, experts, rows, hidden), BF)],
        compiler_params=pltpu.CompilerParams(
            dimension_semantics=("arbitrary",), vmem_limit_bytes=60 * 2**20
        ),
        cost_estimate=pl.CostEstimate(
            flops=flops,
            bytes_accessed=2 * (4 * count * experts * capacity * width + 6 * wg.size),
            transcendentals=count * experts * capacity * hidden,
        ),
        name="experts",
    )(index, *xs, *gs, *places, gates, wg, wu, wd)


def body(
    tokens,
    cotangent,
    norm_attn,
    norm_moe,
    w_query,
    w_key,
    w_value,
    w_out,
    w_router,
    w_gate,
    w_up,
    w_down,
    routes,
):
    local_rows, width = tokens.shape
    count = lax.axis_size("expert")
    slabs = lax.axis_size("dp")
    local_experts = w_gate.shape[1]
    expert_total = local_experts * count
    capacity = min(local_rows, max(2, local_rows * TOP * 7 // (4 * expert_total)))
    capacity = -(-capacity // 16) * 16
    query_width = w_query.shape[1]
    key_width = w_key.shape[1]
    qkv_width = query_width + 2 * key_width
    me = lax.axis_index("expert")

    pad = jnp.zeros((width // slabs, PAD - expert_total - 2), BF)
    packed = jnp.concatenate(
        [w_query, w_key, w_value, w_router, norm_attn[:, None], norm_moe[:, None], pad], axis=1
    )
    full = lax.all_gather(packed, "dp", axis=0, tiled=True)
    routes_low = jnp.concatenate(
        [routes.astype(BF), jnp.zeros((local_rows, PAD - TOP), BF)], axis=1
    )
    side_rows = jnp.concatenate([cotangent, routes_low], axis=1)
    sources = [lax.rem(me + count - s, count) for s in range(count)]
    key_pos = jnp.concatenate(
        [i * local_rows + jnp.arange(local_rows, dtype=jnp.int32) for i in sources]
    )
    cos, sin = rope_tables(key_pos)
    token_blocks, cot_down = [tokens], [side_rows]
    turned, weights = [], [w_gate, w_up, w_down]
    for step in range(1, count):
        up = upward(token_blocks[-1], "expert", count, 1, step - 1)
        down = downward(cot_down[-1], "expert", count, 1, step - 1)
        if weights:
            turned.append(jnp.transpose(weights.pop(0), (1, 0, 2)))
            up, down, turned, weights = lax.optimization_barrier((up, down, turned, weights))
        token_blocks.append(up)
        cot_down.append(down)
    wg, wu, wd = turned
    full, token_blocks, cot_down, w_out, cos, sin = lax.optimization_barrier(
        (full, token_blocks, cot_down, w_out, cos, sin)
    )
    out_full = lax.all_gather(w_out, "dp", axis=0, tiled=True)
    side_rows = cot_down[0]
    cot_up = [side_rows, upward(side_rows, "expert", count)]
    cot_up = cot_up + [upward(side_rows, "expert", count, s) for s in (2,) if count > 2]

    me_ref = jnp.stack([me, lax.axis_index("dp")]).astype(jnp.int32)
    normed_all, side, query, key, value, attended, lse = run_front(
        me_ref, token_blocks, full, cos, sin, query_width, key_width, expert_total
    )
    hidden = tokens.astype(F32)
    inverse_one = inverse_rms(hidden)
    gain_one = side[expert_total : expert_total + 1]
    gain_two = side[expert_total + 1 : expert_total + 2]
    router_full = full[:, qkv_width : qkv_width + expert_total]
    middle = hidden + RES_MULT * dot(attended, out_full)
    inverse_two = inverse_rms(middle)
    normed_two = (middle * inverse_two * gain_two).astype(BF)

    cot_up, cot_down, _ = lax.optimization_barrier((cot_up, cot_down, normed_two))
    while len(cot_up) < count:
        cot_up.append(upward(cot_up[-1], "expert", count, 1, len(cot_up) - 1))
    cot_blocks = [side_rows] + [cot_up[s] + cot_down[count - s] for s in range(1, count)]
    row = lax.broadcasted_iota(jnp.int32, (local_rows, local_rows), 0)
    col = lax.broadcasted_iota(jnp.int32, (local_rows, local_rows), 1)
    earlier = (row < col).astype(BF)
    all_ids = jnp.arange(expert_total, dtype=jnp.int32)
    own_ids = me * local_experts + jnp.arange(local_experts, dtype=jnp.int32)
    route_blocks, hots, hot_locals, places, cot_slots = [], [], [], [], []
    for s in range(count):
        named = cot_blocks[s][:, width : width + TOP].astype(F32).astype(jnp.int32)
        hot = jnp.any(named[:, :, None] == all_ids[None, None, :], axis=1)
        hot_local = jnp.any(
            named.T[None, :, :] == own_ids[:, None, None], axis=1
        )
        position = dot(hot_local.astype(BF), earlier).astype(jnp.int32)
        position = jnp.where(hot_local, position, -1)
        slots = jnp.arange(capacity, dtype=jnp.int32)
        place = (position[:, None, :] == slots[None, :, None]).astype(BF)
        place = place.reshape(local_experts * capacity, local_rows)
        hots.append(hot)
        hot_locals.append(hot_local)
        places.append(place)
        cot_slots.append(dot(place, cot_blocks[s][:, :width]).astype(BF))

    second_blocks = line_gather(normed_two, "expert", count)
    slot_rows, gates = [], []
    for s in range(count):
        logits = dot(second_blocks[s], router_full)
        masked = jnp.where(hots[s], logits, -1e30)
        exponent = jnp.where(
            hots[s], jnp.exp(masked - jnp.max(masked, axis=1, keepdims=True)), 0.0
        )
        gates.append(exponent / jnp.sum(exponent, axis=1, keepdims=True))
        slot_rows.append(dot(places[s], second_blocks[s]).astype(BF))
    gate_rows = jnp.stack(
        [lax.dynamic_slice_in_dim(g.T, me * local_experts, local_experts, 0) for g in gates],
        axis=1,
    )
    results = run_experts(
        me_ref,
        slot_rows,
        cot_slots,
        places,
        gate_rows,
        wg,
        wu,
        wd,
        slabs,
        expert_total,
    )
    slot_outs, slot_backs, expert_grads = (
        results[:count],
        results[count : 2 * count],
        results[2 * count],
    )
    back_sum = line_scatter(
        [dot(places[s], slot_backs[s], 0, 0).astype(BF) for s in range(count)], "expert", count
    )
    mix_parts = [dot(places[s], slot_outs[s], 0, 0).astype(BF) for s in range(count)]
    expert_owned = lax.psum_scatter(expert_grads, "dp", scatter_dimension=0, tiled=True)

    gate_own = gates[0]
    weighted = (
        back_sum[:, width : width + expert_total]
        + back_sum[:, width + expert_total : width + 2 * expert_total]
    )
    grad_logits = (weighted - gate_own * jnp.sum(weighted, axis=1, keepdims=True)).astype(BF)
    grad_normed_two = back_sum[:, :width] + dot(grad_logits, router_full, 1, 1)
    grad_gain_two = jnp.sum(grad_normed_two * middle * inverse_two, axis=0, keepdims=True)
    grad_middle = cotangent.astype(F32) + norm_back(middle, inverse_two, gain_two, grad_normed_two)
    branch_back = (RES_MULT * grad_middle).astype(BF)
    logits_wide = jnp.pad(grad_logits, ((0, 0), (0, PAD - expert_total)))
    out_keep, out_send = run_out(
        me_ref, attended, branch_back, normed_two, logits_wide, grad_gain_two, slabs, expert_total
    )
    out_state = trade(out_keep, out_send, 0, slabs)
    mix_parts, out_state, branch_back = lax.optimization_barrier(
        (mix_parts, out_state, branch_back)
    )
    near = send_near(mix_parts, "expert", count)
    out_stages = slab_stages(out_state, slabs)
    out_halves = next(out_stages)
    query_pre, key_pre, value_pre, *qkv_grads = run_back(
        me_ref, branch_back, out_full, query, key, value, lse, cos, sin, normed_all.T, slabs
    )
    qkv_grads, key_pre, value_pre, near, out_halves = lax.optimization_barrier(
        (qkv_grads, key_pre, value_pre, near, out_halves)
    )
    key_value_part = jnp.concatenate([key_pre, value_pre], axis=1)
    key_value_sum = [key_value_part[:local_rows]]
    key_value_came = [
        downward(key_value_part[s * local_rows : (s + 1) * local_rows], "expert", count, s)
        for s in range(1, count)
    ]
    qkv_state = trade(*qkv_grads, 0, slabs)
    qkv_state, came = lax.optimization_barrier((qkv_state, key_value_came[0]))
    key_value_sum.append(came)
    qkv_stages = slab_stages(qkv_state, slabs)
    qkv_halves = next(qkv_stages)
    for step in range(slabs.bit_length() - 3):
        out_halves = out_stages.send(out_halves)
        qkv_halves, out_halves, came = lax.optimization_barrier(
            (qkv_halves, out_halves, key_value_came[1 + step : 2 + step])
        )
        key_value_sum += came
        qkv_halves = qkv_stages.send(qkv_halves)
    left = key_value_came[len(key_value_sum) - 1 :]
    out_parts = own_parts(*out_halves, me, count)
    out_came = send_parts(out_parts, "expert", count)
    qkv_halves, left, out_came, far = lax.optimization_barrier(
        (qkv_halves, left, out_came, mix_parts[2:-1])
    )
    key_value_sum = add_up(key_value_sum + left).astype(BF)
    out_sum = add_up(out_parts[:1] + out_came)
    qkv_parts = own_parts(*qkv_halves, me, count)
    qkv_sum = add_up(qkv_parts[:1] + send_parts(qkv_parts, "expert", count))
    far = send_far(far, "expert", count)
    output = (middle + add_up(mix_parts[:1] + near + far)).astype(BF)
    pairs = key_width // PAIR
    qkv_sum = qkv_sum.reshape(qkv_sum.shape[0], pairs, (GROUP + 2) * PAIR)
    wide = GROUP * PAIR
    qkv_sum = jnp.concatenate(
        [
            part.reshape(qkv_sum.shape[0], -1)
            for part in (
                qkv_sum[:, :, :wide],
                qkv_sum[:, :, wide : wide + PAIR],
                qkv_sum[:, :, wide + PAIR :],
            )
        ],
        axis=1,
    )
    grad_normed_one = dot(query_pre, full[:, :query_width], 1, 1) + dot(
        key_value_sum, full[:, query_width:qkv_width], 1, 1
    )
    grad_tokens = (grad_middle + norm_back(hidden, inverse_one, gain_one, grad_normed_one)).astype(
        BF
    )
    own = qkv_sum.shape[0]
    own_packed = lax.dynamic_slice_in_dim(packed, me * own, own, 0).astype(F32)
    gain_one_sum = (
        jnp.sum(own_packed[:, :qkv_width] * qkv_sum, axis=1)
        / own_packed[:, qkv_width + expert_total]
    )
    owned = [jnp.transpose(expert_owned[0, k], (1, 0, 2)).astype(F32) for k in range(3)]
    return (
        output,
        grad_tokens,
        gain_one_sum,
        out_sum[:, width + expert_total],
        qkv_sum[:, :query_width],
        qkv_sum[:, query_width : query_width + key_width],
        qkv_sum[:, query_width + key_width :],
        out_sum[:, :width],
        out_sum[:, width : width + expert_total],
        *owned,
    )


def solution(mesh):
    rows = P(("dp", "expert"), None)
    in_specs = (
        [rows, rows, P("dp"), P("dp")]
        + [P("dp", None)] * 5
        + [P(None, "expert", None)] * 3
        + [rows]
    )
    out_specs = (
        [rows, rows, P(("dp", "expert")), P(("dp", "expert"))]
        + [rows] * 5
        + [P("dp", "expert", None)] * 3
    )
    return jax.shard_map(
        body, mesh=mesh, in_specs=tuple(in_specs), out_specs=tuple(out_specs), check_vma=False
    )
```

time: 2240 us -> 626 us (0.28)
  waiting for transfers between devices: 886 us -> 219 us
  blocking collectives: 553 us -> 0 us
  matrix products: 304 us -> 57.9 us
  other arithmetic: 230 us -> 34.5 us
  Pallas kernels: 0 us -> 140 us
  local copies, waits for them, and re-layouts: 195 us -> 69.3 us
  starting transfers between devices: 13 us -> 82.6 us
  loops' own time: 37.1 us -> 0 us
    reduce_scatter x4 -> x1, waiting for transfers between devices: 490 us -> 0.02 us  [body(): lax.psum_scatter(expert_grads, 'dp', scatter_dimension=0, tiled=True)]
    all_to_all x2 -> x0, blocking collectives: 487 us -> none  [the longest x1 244 us: body(): lax.all_to_all(dispatched, 'expert', split_axis=0, concat_axis=0, tiled=T...]
    all_to_all x2 -> x0, waiting for transfers between devices: 354 us -> none  [the longest x1 222 us: body(): lax.all_to_all(slot_back, 'expert', split_axis=0, concat_axis=0, tiled=True)]
    dot_general x61 -> x28, matrix products: 302 us -> 57.9 us  [dot(): lax.dot_general(a, b, (((ca,), (cb,)), ((), ())), preferred_element_type=...]
    ppermute x0 -> x43, waiting for transfers between devices: none -> 219 us  [the longest x10 92.6 us: trade(): lax.ppermute(send, 'dp', [(i, i ^ 1 << bit) for i in range(slabs)])]
    pallas_call x0 -> x4, Pallas kernels: none -> 140 us  [the longest x1 65 us: run_experts(): pl.pallas_call(functools.partial(expert_kernel, count, total), grid_spec=...]
    reduce_sum x17 -> x6, other arithmetic: 120 us -> 1.13 us  [the longest x4 0.78 us: body(): gates.append(exponent / jnp.sum(exponent, axis=1, keepdims=True))]
    ppermute x0 -> x43, starting transfers between devices: none -> 82.5 us  [the longest x3 22.5 us: line_scatter(): right = lax.ppermute(right, axis, [(i, i + 1) for i in range(step)])]
  transfers between devices with their start and end apart: 11 -> 46, of which waited for: 8 -> 18; matrix products, arithmetic and copies ran while one was open for 17% -> 21% of each run, Pallas kernels for 0% -> 12%
where the time goes in v1:
time: 626 us; the launch traced here: 619 us
  waiting for transfers between devices  219 us (35%)
  Pallas kernels  140 us (22%)
  starting transfers between devices  82.6 us (13%)
  local copies, waits for them, and re-layouts  69.3 us (11%)
  matrix products  57.9 us (9%)
  other arithmetic  34.5 us (6%)
  between operations  15.6 us (2%)
    ppermute x10, waiting for transfers between devices, trade(): lax.ppermute(send, 'dp', [(i, i ^ 1 << bit) for i in range(slabs)])  92.6 us
    pallas_call x1, Pallas kernels, run_experts(): pl.pallas_call(functools.partial(expert_kernel, count, total), grid_spec=...  65 us
    dot_general x28, matrix products, dot(): lax.dot_general(a, b, (((ca,), (cb,)), ((), ())), preferred_element_type=...  57.9 us
    ppermute x3, waiting for transfers between devices, line_scatter(): right = lax.ppermute(right, axis, [(i, i + 1) for i in range(step)])  38.6 us
    pallas_call x1, Pallas kernels, run_back(): pl.pallas_call(functools.partial(back_kernel, count), grid_spec=pltpu.Pre...  37.7 us
    pallas_call x1, Pallas kernels, run_front(): pl.pallas_call(functools.partial(front_kernel, count, gain_at), grid_spec...  33.4 us
    ppermute x6, waiting for transfers between devices, send_parts(): lax.ppermute(parts[s], axis, [(i, (i + count - s) % count) for i in range...  28.2 us
    unnamed x109, local copies, waits for them, and re-layouts  26.7 us
  transfers between devices with their start and end apart: 46, of which 18 were waited for; matrix products, arithmetic and copies ran while one was open for 21% of the time, Pallas kernels for 12%

profile of v1, /device:TPU:0, one launch (start us, length us, event | category | flops | bytes accessed | tf_op | source)
XLA Modules:
  0.0 619.1 jit_solution(15240980412722535015)
XLA Ops:
  9.7 3.1 concatenate.31
  14.9 5.6 collective-permute-start
  20.5 13.2 %copy.215 = bf16[1536,8,512]{2,0,1:T(8,128)(2,1)} copy(bf16[1536,8,512]{2,1,0:T(8,128)(2,1)} %param.22) | data formatting | bytes 25165824 | tf_op args[9]
  33.7 3.5 collective-permute-done.refs_1_
  40.4 13.3 %copy.214 = bf16[1536,8,512]{2,0,1:T(8,128)(2,1)} copy(bf16[1536,8,512]{2,1,0:T(8,128)(2,1)} %param.23) | data formatting | bytes 25165824 | tf_op jit(solution)/shard_map/optimization_barrier | solution.py:527
  53.7 6.3 %collective-permute-done.3 = bf16[256,1664]{0,1:T(8,128)(2,1)S(1)} collective-permute-done((bf16[256,1664]{0,1:T(8,128)(2,1)}, bf16[256,1664]{0,1:T(8,128)(2,1)S(1)}, u32[]{:S(2)}, u32[]{:S(2)}) %collective-permute-start.3) | collective-permute-done | bytes 852000 | tf_op jit(solution)/shard_map/ppermute | solution.py:322
  67.3 12.9 %copy.213 = bf16[1536,8,512]{2,0,1:T(8,128)(2,1)} copy(bf16[1536,8,512]{2,1,0:T(8,128)(2,1)} %param.24) | data formatting | bytes 25165824 | tf_op jit(solution)/shard_map/optimization_barrier | solution.py:527
  80.3 2.7 collective-permute-done.5
  83.7 5.8 collective-permute-start.7
  92.0 33.4 %front.1 = (bf16[1024,1536]{1,0:T(8,128)(2,1)}, f32[128,1536]{1,0:T(8,128)}, bf16[256,1536]{1,0:T(8,128)(2,1)}, bf16[1024,512]{1,0:T(8,128)(2,1)}, bf16[1024,512...) custom-call(s32[2]{0:T(128)} %pad_add_fusion.me_ref.ei_ref, bf16[256,1536]{1,0:T(8,128)(2,1)} %refs_0_, ...), custom_call_target="tpu_custom_call" | custom-call | flops 6039797760 | bytes 22806528 | tf_op jit(solution)/shard_map/front/pallas_call | solution.py:121
  126.4 4.1 multiply_reduce_fusion.2
  132.1 4.6 collective-permute-start.8
  142.8 6.7 %collective-permute-done.9 = bf16[256,1536]{1,0:T(8,128)(2,1)S(1)} collective-permute-done((bf16[256,1536]{1,0:T(8,128)(2,1)S(1)}, bf16[256,1536]{1,0:T(8,128)(2,1)S(1)}, u32[]{:S(2)}, u32[]{:S(2)}) %collective-permute-start.9) | collective-permute-done | bytes 786464 | tf_op jit(solution)/shard_map/ppermute | solution.py:298
  155.9 2.4 convolution_convert_fusion.3.refs_4_
  158.3 2.5 convolution_convert_fusion.7.refs_0_
  160.9 2.5 convolution_convert_fusion.refs_7_
  163.4 2.4 convolution_convert_fusion.1.refs_6_
  171.9 2.4 convolution_convert_fusion.5.refs_2_
  174.5 19.2 %collective-permute-done.11 = bf16[256,1536]{1,0:T(8,128)(2,1)S(1)} collective-permute-done((bf16[256,1536]{1,0:T(8,128)(2,1)S(1)}, bf16[256,1536]{1,0:T(8,128)(2,1)S(1)}, u32[]{:S(2)}, u32[]{:S(2)}) %collective-permute-start.11) | collective-permute-done | bytes 786464 | tf_op jit(solution)/shard_map/ppermute | solution.py:298
  198.8 4.1 convolution_convert_fusion.4.refs_3_
  202.8 2.4 convolution_convert_fusion.6.refs_1_
  205.3 65.0 %experts.1 = (bf16[896,1536]{1,0:T(8,128)(2,1)}, bf16[896,1536]{1,0:T(8,128)(2,1)}, bf16[896,1536]{1,0:T(8,128)(2,1)}, bf16[896,1536]{1,0:T(8,128)(2,1)}, bf16[8...) custom-call(s32[2]{0:T(128)} %pad_add_fusion.me_ref.ei_ref, ...), custom_call_target="tpu_custom_call" | custom-call | flops 50734301184 | bytes 119537664 | tf_op jit(solution)/shard_map/experts/pallas_call | solution.py:451
  270.3 3.1 convolution_convert_fusion.12
  276.9 14.8 %collective-permute-done.15 = bf16[256,1664]{1,0:T(8,128)(2,1)S(1)} collective-permute-done((bf16[256,1664]{1,0:T(8,128)(2,1)S(1)}, bf16[256,1664]{1,0:T(8,128)(2,1)S(1)}, u32[]{:S(2)}, u32[]{:S(2)}) %collective-permute-start.15) | collective-permute-done | bytes 852000 | tf_op jit(solution)/shard_map/ppermute | solution.py:307
  292.9 4.4 collective-permute-start.16
  298.2 13.0 %collective-permute-done.16 = bf16[256,1664]{1,0:T(8,128)(2,1)S(1)} collective-permute-done((bf16[256,1664]{1,0:T(8,128)(2,1)S(1)}, bf16[256,1664]{1,0:T(8,128)(2,1)S(1)}, u32[]{:S(2)}, u32[]{:S(2)}) %collective-permute-start.16) | collective-permute-done | bytes 852000 | tf_op jit(solution)/shard_map/ppermute | solution.py:307
  311.4 16.5 %collective-permute-start.17 = (bf16[256,1664]{1,0:T(8,128)(2,1)S(1)}, bf16[256,1664]{1,0:T(8,128)(2,1)S(1)}, u32[]{:S(2)}, u32[]{:S(2)}) collective-permute-start(bf16[256,1664]{1,0:T(8,128)(2,1)S(1)} %add.260), channel_id=1, source_target_pairs={{0,1},{1,2},{2,3},{4,5},{5,6},{6,7},{8,9},{9,10},{10,11},{12,13},{... | collective-permute-start | bytes 2555912 | tf_op jit(solution)/shard_map/ppermute | solution.py:307
  330.7 10.9 %collective-permute-done.17 = bf16[256,1664]{1,0:T(8,128)(2,1)S(1)} collective-permute-done((bf16[256,1664]{1,0:T(8,128)(2,1)S(1)}, bf16[256,1664]{1,0:T(8,128)(2,1)S(1)}, u32[]{:S(2)}, u32[]{:S(2)}) %collective-permute-start.17) | collective-permute-done | bytes 852000 | tf_op jit(solution)/shard_map/ppermute | solution.py:307
  341.6 5.1 collective-permute-done.20
  350.9 4.2 out_grad.1
  355.0 4.8 copy.190
  359.8 3.9 convolution_convert_fusion.11
  376.2 37.7 %back.1 = (bf16[256,1536]{1,0:T(8,128)(2,1)}, bf16[1024,512]{1,0:T(8,128)(2,1)}, bf16[1024,512]{1,0:T(8,128)(2,1)}, bf16[4,192,2560]{2,1,0:T(8,128)(2,1)}, bf16[4,192,2560]{2,1,0:T(8,128)(2,1)}) custom-call(s32[2]{0:T(128)} %pad_add_fusion.me_ref.ei_ref, bf16[256,1536]{1,0:T(8,128)(2,1)} %copy-done, bf16[1536,1536]{1,0:T(8,128)(2,1)} %all-gather.5.cloned.1.call-done.refs_1_, ...), custom_call_target="tpu_custom_call" | custom-call | flops 9663676416 | bytes 12582912 | tf_op jit(solution)/shard_map/back/pallas_call | solution.py:249
  418.3 4.2 fusion
  424.0 3.1 add.273
  427.1 6.0 collective-permute-done.27
  441.2 46.2 %collective-permute-done.30 = bf16[96,1664]{1,0:T(8,128)(2,1)S(1)} collective-permute-done((bf16[96,1664]{1,0:T(8,128)(2,1)S(1)}, bf16[96,1664]{1,0:T(8,128)(2,1)S(1)}, u32[]{:S(2)}, u32[]{:S(2)}) %collective-permute-start.30) | collective-permute-done | bytes 319520 | tf_op jit(solution)/shard_map/ppermute | solution.py:355
  495.0 21.3 %collective-permute-done.34 = bf16[96,2560]{1,0:T(8,128)(2,1)S(1)} collective-permute-done((bf16[96,2560]{1,0:T(8,128)(2,1)S(1)}, bf16[96,2560]{1,0:T(8,128)(2,1)S(1)}, u32[]{:S(2)}, u32[]{:S(2)}) %collective-permute-start.34) | collective-permute-done | bytes 491552 | tf_op jit(solution)/shard_map/ppermute | solution.py:355
  516.6 23.2 %collective-permute-done.33 = bf16[96,2560]{1,0:T(8,128)(2,1)S(1)} collective-permute-done((bf16[96,2560]{1,0:T(8,128)(2,1)S(1)}, bf16[96,2560]{1,0:T(8,128)(2,1)S(1)}, u32[]{:S(2)}, u32[]{:S(2)}) %collective-permute-start.33) | collective-permute-done | bytes 491552 | tf_op jit(solution)/shard_map/ppermute | solution.py:355
  542.8 3.5 fusion.11
  549.1 2.8 collective-permute-start.39
  552.8 27.9 %collective-permute-done.41 = bf16[48,2560]{1,0:T(8,128)(2,1)} collective-permute-done((bf16[48,2560]{1,0:T(8,128)(2,1)}, bf16[48,2560]{1,0:T(8,128)(2,1)}, u32[]{:S(2)}, u32[]{:S(2)}) %collective-permute-start.41) | collective-permute-done | bytes 245792 | tf_op jit(solution)/shard_map/ppermute | solution.py:327
  584.9 9.8 %collective-permute-done.39 = bf16[256,1536]{1,0:T(8,128)(2,1)} collective-permute-done((bf16[256,1536]{1,0:T(8,128)(2,1)}, bf16[256,1536]{1,0:T(8,128)(2,1)}, u32[]{:S(2)}, u32[]{:S(2)}) %collective-permute-start.39) | collective-permute-done | bytes 786464 | tf_op jit(solution)/shard_map/ppermute | solution.py:342
  594.7 3.2 add_convert_fusion
  597.9 3.7 convert_bitcast_fusion
  601.6 3.5 copy.197
  605.1 3.5 copy.196
  608.6 3.5 copy.195
  (289 shorter events, 101.8 us)
Async XLA Ops:
  7.2 75.7 %all-gather.3.cloned.1.call-start = ((), (), s32[]{:S(2)}) async-start(), calls=%async_computation.1 | async-start | bytes 9289728 | tf_op jit(solution)/shard_map/all_gather | solution.py:510
  12.8 113.5 %all-gather.5.cloned.1.call-start = ((), (), s32[]{:S(2)}) async-start(), calls=%async_computation.2 | async-start | bytes 5308416 | tf_op jit(solution)/shard_map/all_gather | solution.py:534
  13.6 24.0 %collective-permute-start.1 = (bf16[256,1664]{0,1:T(8,128)(2,1)S(1)}, bf16[256,1664]{0,1:T(8,128)(2,1)}, u32[]{:S(2)}, u32[]{:S(2)}) collective-permute-start(bf16[256,1664]{0,1:T(8,128)(2,1)S(1)} %maximum_maximum_fusion), channel_id=1, source_target_pairs={{1,0},{2,1},{3,2},{5,4},{6,5},{7,6},{9,8},{10,9},{11,10},{13,12},{... | collective-permute-start | bytes 2555912 | tf_op jit(solution)/shard_map/ppermute | solution.py:322
  14.9 22.3 %collective-permute-start = (bf16[256,1536]{1,0:T(8,128)(2,1)S(1)}, bf16[256,1536]{1,0:T(8,128)(2,1)S(1)}, u32[]{:S(2)}, u32[]{:S(2)}) collective-permute-start(bf16[256,1536]{1,0:T(8,128)(2,1)S(1)} %copy-done.21), channel_id=1, source_target_pairs={{0,1},{1,2},{2,3},{4,5},{5,6},{6,7},{8,9},{9,10},{10,11},{12,13},{... | collective-permute-start | bytes 2359304 | tf_op jit(solution)/shard_map/ppermute | solution.py:317
  37.5 22.4 %collective-permute-start.3 = (bf16[256,1664]{0,1:T(8,128)(2,1)}, bf16[256,1664]{0,1:T(8,128)(2,1)S(1)}, u32[]{:S(2)}, u32[]{:S(2)}) collective-permute-start(bf16[256,1664]{0,1:T(8,128)(2,1)} %collective-permute-done.1), channel_id=1, source_target_pairs={{1,0},{2,1},{5,4},{6,5},{9,8},{10,9},{13,12},{14,13},{17,16},{18,1... | collective-permute-start | bytes 2555912 | tf_op jit(solution)/shard_map/ppermute | solution.py:322
  38.8 14.8 %collective-permute-start.2 = (bf16[256,1536]{1,0:T(8,128)(2,1)S(1)}, bf16[256,1536]{1,0:T(8,128)(2,1)}, u32[]{:S(2)}, u32[]{:S(2)}) collective-permute-start(bf16[256,1536]{1,0:T(8,128)(2,1)S(1)} %collective-permute-done.refs_1_), channel_id=1, source_target_pairs={{1,2},{2,3},{5,6},{6,7},{9,10},{10,11},{13,14},{14,15},{17,18},{18... | collective-permute-start | bytes 2359304 | tf_op jit(solution)/shard_map/ppermute | solution.py:317
  60.0 20.3 %collective-permute-start.4 = (bf16[256,1536]{1,0:T(8,128)(2,1)}, bf16[256,1536]{1,0:T(8,128)(2,1)}, u32[]{:S(2)}, u32[]{:S(2)}) collective-permute-start(bf16[256,1536]{1,0:T(8,128)(2,1)} %collective-permute-done.2.refs_2_), channel_id=1, source_target_pairs={{2,3},{6,7},{10,11},{14,15},{18,19},{22,23},{26,27},{30,31}} | collective-permute-start | bytes 2359304 | tf_op jit(solution)/shard_map/ppermute | solution.py:317
  61.6 21.4 %collective-permute-start.5 = (bf16[256,1664]{0,1:T(8,128)(2,1)S(1)}, bf16[256,1664]{0,1:T(8,128)(2,1)}, u32[]{:S(2)}, u32[]{:S(2)}) collective-permute-start(bf16[256,1664]{0,1:T(8,128)(2,1)S(1)} %collective-permute-done.3), channel_id=1, source_target_pairs={{1,0},{5,4},{9,8},{13,12},{17,16},{21,20},{25,24},{29,28}} | collective-permute-start | bytes 2555912 | tf_op jit(solution)/shard_map/ppermute | solution.py:322
  83.0 515.0 %reduce-scatter.2.cloned.1.call-start = ((), (), s32[]{:S(2)}) async-start(), calls=%async_computation.3 | async-start | bytes 42467328 | tf_op jit(solution)/shard_map/reduce_scatter | solution.py:613
  83.7 53.1 %collective-permute-start.7 = (bf16[256,1664]{0,1:T(8,128)(2,1)S(1)}, bf16[256,1664]{0,1:T(8,128)(2,1)}, u32[]{:S(2)}, u32[]{:S(2)}) collective-permute-start(bf16[256,1664]{0,1:T(8,128)(2,1)S(1)} %maximum_maximum_fusion), channel_id=1, source_target_pairs={{0,2},{1,3},{4,6},{5,7},{8,10},{9,11},{12,14},{13,15},{16,18},{17,... | collective-permute-start | bytes 2555912 | tf_op jit(solution)/shard_map/ppermute | solution.py:317
  89.5 47.3 %collective-permute-start.6 = (bf16[256,1664]{0,1:T(8,128)(2,1)S(1)}, bf16[256,1664]{0,1:T(8,128)(2,1)}, u32[]{:S(2)}, u32[]{:S(2)}) collective-permute-start(bf16[256,1664]{0,1:T(8,128)(2,1)S(1)} %maximum_maximum_fusion), channel_id=1, source_target_pairs={{0,1},{1,2},{2,3},{4,5},{5,6},{6,7},{8,9},{9,10},{10,11},{12,13},{... | collective-permute-start | bytes 2555912 | tf_op jit(solution)/shard_map/ppermute | solution.py:317
  130.5 218.6 %copy-start.3 = (f32[256,1536]{1,0:T(8,128)}, f32[256,1536]{1,0:T(8,128)S(1)}, u32[]{:S(2)}) copy-start(f32[256,1536]{1,0:T(8,128)S(1)} %get-tuple-element.318) | copy-start | bytes 4718596
  130.7 18.7 %collective-permute-start.9 = (bf16[256,1536]{1,0:T(8,128)(2,1)S(1)}, bf16[256,1536]{1,0:T(8,128)(2,1)S(1)}, u32[]{:S(2)}, u32[]{:S(2)}) collective-permute-start(bf16[256,1536]{1,0:T(8,128)(2,1)S(1)} %multiply_convert_fusion.1.normed_ref), channel_id=1, source_target_pairs={{1,0},{2,1},{3,2},{5,4},{6,5},{7,6},{9,8},{10,9},{11,10},{13,12},{... | collective-permute-start | bytes 2359304 | tf_op jit(solution)/shard_map/ppermute | solution.py:298
  132.1 18.6 %collective-permute-start.8 = (bf16[256,1536]{1,0:T(8,128)(2,1)S(1)}, bf16[256,1536]{1,0:T(8,128)(2,1)S(1)}, u32[]{:S(2)}, u32[]{:S(2)}) collective-permute-start(bf16[256,1536]{1,0:T(8,128)(2,1)S(1)} %multiply_convert_fusion.1.normed_ref), channel_id=1, source_target_pairs={{0,1},{1,2},{2,3},{4,5},{5,6},{6,7},{8,9},{9,10},{10,11},{12,13},{... | collective-permute-start | bytes 2359304 | tf_op jit(solution)/shard_map/ppermute | solution.py:296
  138.4 13.3 %collective-permute-start.13 = (bf16[256,1664]{0,1:T(8,128)(2,1)}, bf16[256,1664]{0,1:T(8,128)(2,1)S(1)}, u32[]{:S(2)}, u32[]{:S(2)}) collective-permute-start(bf16[256,1664]{0,1:T(8,128)(2,1)} %collective-permute-done.7), channel_id=1, source_target_pairs={{2,3},{6,7},{10,11},{14,15},{18,19},{22,23},{26,27},{30,31}} | collective-permute-start | bytes 2555912 | tf_op jit(solution)/shard_map/ppermute | solution.py:317
  149.5 18.8 %collective-permute-start.10 = (bf16[256,1536]{1,0:T(8,128)(2,1)S(1)}, bf16[256,1536]{1,0:T(8,128)(2,1)S(1)}, u32[]{:S(2)}, u32[]{:S(2)}) collective-permute-start(bf16[256,1536]{1,0:T(8,128)(2,1)S(1)} %collective-permute-done.9), channel_id=1, source_target_pairs={{1,0},{2,1},{5,4},{6,5},{9,8},{10,9},{13,12},{14,13},{17,16},{18,1... | collective-permute-start | bytes 2359304 | tf_op jit(solution)/shard_map/ppermute | solution.py:298
  150.8 18.8 %collective-permute-start.12 = (bf16[256,1536]{1,0:T(8,128)(2,1)S(1)}, bf16[256,1536]{1,0:T(8,128)(2,1)S(1)}, u32[]{:S(2)}, u32[]{:S(2)}) collective-permute-start(bf16[256,1536]{1,0:T(8,128)(2,1)S(1)} %collective-permute-done.8), channel_id=1, source_target_pairs={{1,2},{2,3},{5,6},{6,7},{9,10},{10,11},{13,14},{14,15},{17,18},{18... | collective-permute-start | bytes 2359304 | tf_op jit(solution)/shard_map/ppermute | solution.py:296
  155.8 173.7 %copy-start.9 = (pred[896,256]{1,0:T(32,128)(4,1)}, pred[896,256]{1,0:T(32,128)(4,1)S(1)}, u32[]{:S(2)}) copy-start(pred[896,256]{1,0:T(32,128)(4,1)S(1)} %get-tuple-element.311) | copy-start | bytes 688132
  168.3 25.4 %collective-permute-start.11 = (bf16[256,1536]{1,0:T(8,128)(2,1)S(1)}, bf16[256,1536]{1,0:T(8,128)(2,1)S(1)}, u32[]{:S(2)}, u32[]{:S(2)}) collective-permute-start(bf16[256,1536]{1,0:T(8,128)(2,1)S(1)} %collective-permute-done.10), channel_id=1, source_target_pairs={{1,0},{5,4},{9,8},{13,12},{17,16},{21,20},{25,24},{29,28}} | collective-permute-start | bytes 2359304 | tf_op jit(solution)/shard_map/ppermute | solution.py:298
  169.6 26.2 %collective-permute-start.14 = (bf16[256,1536]{1,0:T(8,128)(2,1)S(1)}, bf16[256,1536]{1,0:T(8,128)(2,1)S(1)}, u32[]{:S(2)}, u32[]{:S(2)}) collective-permute-start(bf16[256,1536]{1,0:T(8,128)(2,1)S(1)} %collective-permute-done.12), channel_id=1, source_target_pairs={{2,3},{6,7},{10,11},{14,15},{18,19},{22,23},{26,27},{30,31}} | collective-permute-start | bytes 2359304 | tf_op jit(solution)/shard_map/ppermute | solution.py:296
  274.6 2.2 collective-permute-start.18
  275.4 16.3 %collective-permute-start.15 = (bf16[256,1664]{1,0:T(8,128)(2,1)S(1)}, bf16[256,1664]{1,0:T(8,128)(2,1)S(1)}, u32[]{:S(2)}, u32[]{:S(2)}) collective-permute-start(bf16[256,1664]{1,0:T(8,128)(2,1)S(1)} %convolution_convert_fusion.12), channel_id=1, source_target_pairs={{0,1},{4,5},{8,9},{12,13},{16,17},{20,21},{24,25},{28,29}} | collective-permute-start | bytes 2555912 | tf_op jit(solution)/shard_map/ppermute | solution.py:307
  292.9 18.3 %collective-permute-start.16 = (bf16[256,1664]{1,0:T(8,128)(2,1)S(1)}, bf16[256,1664]{1,0:T(8,128)(2,1)S(1)}, u32[]{:S(2)}, u32[]{:S(2)}) collective-permute-start(bf16[256,1664]{1,0:T(8,128)(2,1)S(1)} %get-tuple-element.281), channel_id=1, source_target_pairs={{0,1},{1,2},{4,5},{5,6},{8,9},{9,10},{12,13},{13,14},{16,17},{17,1... | collective-permute-start | bytes 2555912 | tf_op jit(solution)/shard_map/ppermute | solution.py:307
  297.3 30.6 %collective-permute-start.19 = (bf16[256,1664]{1,0:T(8,128)(2,1)S(1)}, bf16[256,1664]{1,0:T(8,128)(2,1)S(1)}, u32[]{:S(2)}, u32[]{:S(2)}) collective-permute-start(bf16[256,1664]{1,0:T(8,128)(2,1)S(1)} %get-tuple-element.282), channel_id=1, source_target_pairs={{2,1},{3,2},{6,5},{7,6},{10,9},{11,10},{14,13},{15,14},{18,17},{19... | collective-permute-start | bytes 2555912 | tf_op jit(solution)/shard_map/ppermute | solution.py:308
  311.4 30.3 %collective-permute-start.17 = (bf16[256,1664]{1,0:T(8,128)(2,1)S(1)}, bf16[256,1664]{1,0:T(8,128)(2,1)S(1)}, u32[]{:S(2)}, u32[]{:S(2)}) collective-permute-start(bf16[256,1664]{1,0:T(8,128)(2,1)S(1)} %add.260), channel_id=1, source_target_pairs={{0,1},{1,2},{2,3},{4,5},{5,6},{6,7},{8,9},{9,10},{10,11},{12,13},{... | collective-permute-start | bytes 2555912 | tf_op jit(solution)/shard_map/ppermute | solution.py:307
  328.1 18.6 %collective-permute-start.20 = (bf16[256,1664]{1,0:T(8,128)(2,1)S(1)}, bf16[256,1664]{1,0:T(8,128)(2,1)S(1)}, u32[]{:S(2)}, u32[]{:S(2)}) collective-permute-start(bf16[256,1664]{1,0:T(8,128)(2,1)S(1)} %add.263), channel_id=1, source_target_pairs={{1,0},{2,1},{3,2},{5,4},{6,5},{7,6},{9,8},{10,9},{11,10},{13,12},{... | collective-permute-start | bytes 2555912 | tf_op jit(solution)/shard_map/ppermute | solution.py:308
  355.0 14.5 %collective-permute-start.21 = (bf16[4,192,1664]{2,1,0:T(8,128)(2,1)}, bf16[4,192,1664]{2,1,0:T(8,128)(2,1)}, u32[]{:S(2)}, u32[]{:S(2)}) collective-permute-start(bf16[4,192,1664]{2,1,0:T(8,128)(2,1)} %get-tuple-element.138), channel_id=1, source_target_pairs={{0,4},{4,0},{8,12},{12,8},{16,20},{20,16},{24,28},{28,24},{1,5},{5... | collective-permute-start | bytes 7667720 | tf_op jit(solution)/shard_map/ppermute | solution.py:355
  371.9 42.1 %collective-permute-start.25 = (bf16[2,96,1664]{2,1,0:T(8,128)(2,1)S(1)}, bf16[2,96,1664]{2,1,0:T(8,128)(2,1)S(1)}, u32[]{:S(2)}, u32[]{:S(2)}) collective-permute-start(bf16[2,96,1664]{2,1,0:T(8,128)(2,1)S(1)} %slice_bitcast_fusion.7), channel_id=1, source_target_pairs={{0,16},{4,20},{8,24},{12,28},{16,0},{20,4},{24,8},{28,12},{1,17},{... | collective-permute-start | bytes 1916936 | tf_op jit(solution)/shard_map/ppermute | solution.py:355
  373.1 40.8 %collective-permute-start.24 = (bf16[2,96,1664]{2,1,0:T(8,128)(2,1)S(1)}, bf16[2,96,1664]{2,1,0:T(8,128)(2,1)S(1)}, u32[]{:S(2)}, u32[]{:S(2)}) collective-permute-start(bf16[2,96,1664]{2,1,0:T(8,128)(2,1)S(1)} %slice_bitcast_fusion.9), channel_id=1, source_target_pairs={{0,8},{4,12},{8,0},{12,4},{16,24},{20,28},{24,16},{28,20},{1,9},{5... | collective-permute-start | bytes 1916936 | tf_op jit(solution)/shard_map/ppermute | solution.py:355
  373.9 40.2 %collective-permute-start.22 = (bf16[256,1536]{1,0:T(8,128)(2,1)}, bf16[256,1536]{1,0:T(8,128)(2,1)}, u32[]{:S(2)}, u32[]{:S(2)}) collective-permute-start(bf16[256,1536]{1,0:T(8,128)(2,1)} %convolution_convert_fusion.10), channel_id=1, source_target_pairs={{0,3},{1,0},{2,1},{3,2},{4,7},{5,4},{6,5},{7,6},{8,11},{9,8},{10,9... | collective-permute-start | bytes 2359304 | tf_op jit(solution)/shard_map/ppermute | solution.py:335
  374.8 39.3 %collective-permute-start.23 = (bf16[256,1536]{1,0:T(8,128)(2,1)}, bf16[256,1536]{1,0:T(8,128)(2,1)}, u32[]{:S(2)}, u32[]{:S(2)}) collective-permute-start(bf16[256,1536]{1,0:T(8,128)(2,1)} %convolution_convert_fusion.8), channel_id=1, source_target_pairs={{0,1},{1,2},{2,3},{3,0},{4,5},{5,6},{6,7},{7,4},{8,9},{9,10},{10,1... | collective-permute-start | bytes 2359304 | tf_op jit(solution)/shard_map/ppermute | solution.py:335
  414.1 9.9 %collective-permute-start.26 = (bf16[4,192,2560]{2,1,0:T(8,128)(2,1)}, bf16[4,192,2560]{2,1,0:T(8,128)(2,1)}, u32[]{:S(2)}, u32[]{:S(2)}) collective-permute-start(bf16[4,192,2560]{2,1,0:T(8,128)(2,1)} %get-tuple-element.156), channel_id=1, source_target_pairs={{0,4},{4,0},{8,12},{12,8},{16,20},{20,16},{24,28},{28,24},{1,5},{5... | collective-permute-start | bytes 11796488 | tf_op jit(solution)/shard_map/ppermute | solution.py:355
  416.9 16.3 %collective-permute-start.27 = (bf16[256,1024]{1,0:T(8,128)(2,1)S(1)}, bf16[256,1024]{1,0:T(8,128)(2,1)S(1)}, u32[]{:S(2)}, u32[]{:S(2)}) collective-permute-start(bf16[256,1024]{1,0:T(8,128)(2,1)S(1)} %get-tuple-element.277), channel_id=1, source_target_pairs={{1,0},{2,1},{3,2},{5,4},{6,5},{7,6},{9,8},{10,9},{11,10},{13,12},{... | collective-permute-start | bytes 1572872 | tf_op jit(solution)/shard_map/ppermute | solution.py:322
  422.5 17.3 %collective-permute-start.31 = (bf16[96,1664]{1,0:T(8,128)(2,1)S(1)}, bf16[96,1664]{1,0:T(8,128)(2,1)S(1)}, u32[]{:S(2)}, u32[]{:S(2)}) collective-permute-start(bf16[96,1664]{1,0:T(8,128)(2,1)S(1)} %slice_bitcast_fusion.13), channel_id=1, source_target_pairs={{0,8},{4,12},{8,0},{12,4},{16,24},{20,28},{24,16},{28,20},{1,9},{5... | collective-permute-start | bytes 958472 | tf_op jit(solution)/shard_map/ppermute | solution.py:355
  433.2 54.2 %collective-permute-start.28 = (bf16[2,96,2560]{2,1,0:T(8,128)(2,1)S(1)}, bf16[2,96,2560]{2,1,0:T(8,128)(2,1)S(1)}, u32[]{:S(2)}, u32[]{:S(2)}) collective-permute-start(bf16[2,96,2560]{2,1,0:T(8,128)(2,1)S(1)} %slice_bitcast_fusion.5), channel_id=1, source_target_pairs={{0,8},{4,12},{8,0},{12,4},{16,24},{20,28},{24,16},{28,20},{1,9},{5... | collective-permute-start | bytes 2949128 | tf_op jit(solution)/shard_map/ppermute | solution.py:355
  434.4 53.0 %collective-permute-start.29 = (bf16[2,96,2560]{2,1,0:T(8,128)(2,1)S(1)}, bf16[2,96,2560]{2,1,0:T(8,128)(2,1)S(1)}, u32[]{:S(2)}, u32[]{:S(2)}) collective-permute-start(bf16[2,96,2560]{2,1,0:T(8,128)(2,1)S(1)} %slice_bitcast_fusion.3), channel_id=1, source_target_pairs={{0,16},{4,20},{8,24},{12,28},{16,0},{20,4},{24,8},{28,12},{1,17},{... | collective-permute-start | bytes 2949128 | tf_op jit(solution)/shard_map/ppermute | solution.py:355
  435.5 51.8 %collective-permute-start.30 = (bf16[96,1664]{1,0:T(8,128)(2,1)S(1)}, bf16[96,1664]{1,0:T(8,128)(2,1)S(1)}, u32[]{:S(2)}, u32[]{:S(2)}) collective-permute-start(bf16[96,1664]{1,0:T(8,128)(2,1)S(1)} %slice_bitcast_fusion.14), channel_id=1, source_target_pairs={{0,16},{4,20},{8,24},{12,28},{16,0},{20,4},{24,8},{28,12},{1,17},{... | collective-permute-start | bytes 958472 | tf_op jit(solution)/shard_map/ppermute | solution.py:355
  436.6 103.2 %collective-permute-start.35 = (bf16[256,1024]{1,0:T(8,128)(2,1)S(1)}, bf16[256,1024]{1,0:T(8,128)(2,1)S(1)}, u32[]{:S(2)}, u32[]{:S(2)}) collective-permute-start(bf16[256,1024]{1,0:T(8,128)(2,1)S(1)} %get-tuple-element.275), channel_id=1, source_target_pairs={{3,0},{7,4},{11,8},{15,12},{19,16},{23,20},{27,24},{31,28}} | collective-permute-start | bytes 1572872 | tf_op jit(solution)/shard_map/ppermute | solution.py:322
  439.8 47.8 %collective-permute-start.32 = (bf16[256,1024]{1,0:T(8,128)(2,1)S(1)}, bf16[256,1024]{1,0:T(8,128)(2,1)S(1)}, u32[]{:S(2)}, u32[]{:S(2)}) collective-permute-start(bf16[256,1024]{1,0:T(8,128)(2,1)S(1)} %get-tuple-element.276), channel_id=1, source_target_pairs={{2,0},{3,1},{6,4},{7,5},{10,8},{11,9},{14,12},{15,13},{18,16},{19,... | collective-permute-start | bytes 1572872 | tf_op jit(solution)/shard_map/ppermute | solution.py:322
  487.8 52.0 %collective-permute-start.38 = (bf16[48,1664]{1,0:T(8,128)(2,1)S(1)}, bf16[48,1664]{1,0:T(8,128)(2,1)S(1)}, u32[]{:S(2)}, u32[]{:S(2)}) collective-permute-start(bf16[48,1664]{1,0:T(8,128)(2,1)S(1)} %get-tuple-element.291), channel_id=1, source_target_pairs={{0,1},{1,2},{2,3},{3,0},{4,5},{5,6},{6,7},{7,4},{8,9},{9,10},{10,1... | collective-permute-start | bytes 479240 | tf_op jit(solution)/shard_map/ppermute | solution.py:327
  489.6 50.2 %collective-permute-start.37 = (bf16[48,1664]{1,0:T(8,128)(2,1)S(1)}, bf16[48,1664]{1,0:T(8,128)(2,1)S(1)}, u32[]{:S(2)}, u32[]{:S(2)}) collective-permute-start(bf16[48,1664]{1,0:T(8,128)(2,1)S(1)} %get-tuple-element.292), channel_id=1, source_target_pairs={{0,2},{1,3},{2,0},{3,1},{4,6},{5,7},{6,4},{7,5},{8,10},{9,11},{10,... | collective-permute-start | bytes 479240 | tf_op jit(solution)/shard_map/ppermute | solution.py:327
  492.0 47.9 %collective-permute-start.36 = (bf16[48,1664]{1,0:T(8,128)(2,1)S(1)}, bf16[48,1664]{1,0:T(8,128)(2,1)S(1)}, u32[]{:S(2)}, u32[]{:S(2)}) collective-permute-start(bf16[48,1664]{1,0:T(8,128)(2,1)S(1)} %get-tuple-element.293), channel_id=1, source_target_pairs={{0,3},{1,0},{2,1},{3,2},{4,7},{5,4},{6,5},{7,6},{8,11},{9,8},{10,9... | collective-permute-start | bytes 479240 | tf_op jit(solution)/shard_map/ppermute | solution.py:327
  493.4 22.8 %collective-permute-start.34 = (bf16[96,2560]{1,0:T(8,128)(2,1)S(1)}, bf16[96,2560]{1,0:T(8,128)(2,1)S(1)}, u32[]{:S(2)}, u32[]{:S(2)}) collective-permute-start(bf16[96,2560]{1,0:T(8,128)(2,1)S(1)} %slice_bitcast_fusion.11), channel_id=1, source_target_pairs={{0,8},{4,12},{8,0},{12,4},{16,24},{20,28},{24,16},{28,20},{1,9},{5... | collective-permute-start | bytes 1474568 | tf_op jit(solution)/shard_map/ppermute | solution.py:355
  516.3 23.5 %collective-permute-start.33 = (bf16[96,2560]{1,0:T(8,128)(2,1)S(1)}, bf16[96,2560]{1,0:T(8,128)(2,1)S(1)}, u32[]{:S(2)}, u32[]{:S(2)}) collective-permute-start(bf16[96,2560]{1,0:T(8,128)(2,1)S(1)} %slice_bitcast_fusion.12), channel_id=1, source_target_pairs={{0,16},{4,20},{8,24},{12,28},{16,0},{20,4},{24,8},{28,12},{1,17},{... | collective-permute-start | bytes 1474568 | tf_op jit(solution)/shard_map/ppermute | solution.py:355
  540.8 11.8 %collective-permute-start.40 = (bf16[48,2560]{1,0:T(8,128)(2,1)}, bf16[48,2560]{1,0:T(8,128)(2,1)}, u32[]{:S(2)}, u32[]{:S(2)}) collective-permute-start(bf16[48,2560]{1,0:T(8,128)(2,1)} %get-tuple-element.278), channel_id=1, source_target_pairs={{0,3},{1,0},{2,1},{3,2},{4,7},{5,4},{6,5},{7,6},{8,11},{9,8},{10,9... | collective-permute-start | bytes 737288 | tf_op jit(solution)/shard_map/ppermute | solution.py:327
  540.8 12.0 %collective-permute-start.42 = (bf16[48,2560]{1,0:T(8,128)(2,1)}, bf16[48,2560]{1,0:T(8,128)(2,1)}, u32[]{:S(2)}, u32[]{:S(2)}) collective-permute-start(bf16[48,2560]{1,0:T(8,128)(2,1)} %get-tuple-element.279), channel_id=1, source_target_pairs={{0,1},{1,2},{2,3},{3,0},{4,5},{5,6},{6,7},{7,4},{8,9},{9,10},{10,1... | collective-permute-start | bytes 737288 | tf_op jit(solution)/shard_map/ppermute | solution.py:327
  542.8 37.9 %collective-permute-start.41 = (bf16[48,2560]{1,0:T(8,128)(2,1)}, bf16[48,2560]{1,0:T(8,128)(2,1)}, u32[]{:S(2)}, u32[]{:S(2)}) collective-permute-start(bf16[48,2560]{1,0:T(8,128)(2,1)} %get-tuple-element.280), channel_id=1, source_target_pairs={{0,2},{1,3},{2,0},{3,1},{4,6},{5,7},{6,4},{7,5},{8,10},{9,11},{10,... | collective-permute-start | bytes 737288 | tf_op jit(solution)/shard_map/ppermute | solution.py:327
  549.1 45.6 %collective-permute-start.39 = (bf16[256,1536]{1,0:T(8,128)(2,1)}, bf16[256,1536]{1,0:T(8,128)(2,1)}, u32[]{:S(2)}, u32[]{:S(2)}) collective-permute-start(bf16[256,1536]{1,0:T(8,128)(2,1)} %convolution_convert_fusion.9), channel_id=1, source_target_pairs={{0,2},{1,3},{2,0},{3,1},{4,6},{5,7},{6,4},{7,5},{8,10},{9,11},{10,... | collective-permute-start | bytes 2359304 | tf_op jit(solution)/shard_map/ppermute | solution.py:342
  (46 other events, 692.4 us)
Sparse Core Ops, SparseCore 0:
  12.9 56.5 all-gather.2
  83.1 39.5 all-gather.4
  270.4 289.7 reduce-scatter.1

commit v2 on v1

--- a/solution.py
+++ b/solution.py
@@ -394,13 +394,13 @@
                 ref[place, :, at] = value[d * slab : (d + 1) * slab]
 
 
-def expert_kernel(count, total, ei_ref, *refs):
+def expert_kernel(count, total, experts, first, me_ref, *refs):
     x_refs, g_refs, p_refs = refs[:count], refs[count : 2 * count], refs[2 * count : 3 * count]
     gate_ref, wg_ref, wu_ref, wd_ref = refs[3 * count : 3 * count + 4]
-    outs = refs[3 * count + 4 :]
+    outs = refs[-2 * count - 1 :]
     out_refs, back_refs, grads_ref = outs[:count], outs[count : 2 * count], outs[2 * count]
     capacity, width = x_refs[0].shape
-    expert = ei_ref[0] * pl.num_programs(0) + pl.program_id(0)
+    expert = me_ref[0] * experts + first + pl.program_id(0)
     x = jnp.concatenate([r[...] for r in x_refs], axis=0)
     g = jnp.concatenate([r[...] for r in g_refs], axis=0)
     gate = jnp.concatenate(
@@ -440,40 +440,76 @@
         grads_ref[:, k, 0] = dot(a, b, 0, 0).astype(BF).reshape(slabs, rows, b.shape[1])
 
 
-def run_experts(index, xs, gs, places, gates, wg, wu, wd, slabs, total):
+def run_experts(index, xs, gs, places, gates, wg, wu, wd, slabs, total, first, number, earlier):
     count = len(xs)
     experts, width, hidden = wg.shape
     capacity = xs[0].shape[0] // experts
-    block = lambda w: pl.BlockSpec((capacity, w), lambda e, i: (e, 0))
-    weight = pl.BlockSpec((1, width, hidden), lambda e, i: (e, 0, 0))
+    block = lambda w: pl.BlockSpec((capacity, w), lambda e, i: (first + e, 0))
+    weight = pl.BlockSpec((1, width, hidden), lambda e, i: (first + e, 0, 0))
     rows = width // slabs
-    flops = 2 * 9 * count * experts * capacity * width * hidden
+    slots = count * number * capacity
+    inputs = [*xs, *gs, *places, gates, wg, wu, wd, *earlier]
     return pl.pallas_call(
-        functools.partial(expert_kernel, count, total),
+        functools.partial(expert_kernel, count, total, experts, first),
         grid_spec=pltpu.PrefetchScalarGridSpec(
             num_scalar_prefetch=1,
-            grid=(experts,),
+            grid=(number,),
             in_specs=[block(width)] * (2 * count)
             + [block(places[0].shape[1])] * count
-            + [pl.BlockSpec((1,) + gates.shape[1:], lambda e, i: (e, 0, 0))]
-            + [weight] * 3,
+            + [pl.BlockSpec((1,) + gates.shape[1:], lambda e, i: (first + e, 0, 0))]
+            + [weight] * 3
+            + [pl.BlockSpec(memory_space=pl.ANY)] * len(earlier),
             out_specs=[block(width)] * count
             + [block(width + PAD)] * count
             + [pl.BlockSpec((slabs, 3, 1, rows, hidden), lambda e, i: (0, 0, e, 0, 0))],
         ),
         out_shape=[jax.ShapeDtypeStruct((experts * capacity, width), BF)] * count
         + [jax.ShapeDtypeStruct((experts * capacity, width + PAD), BF)] * count
-        + [jax.ShapeDtypeStruct((slabs, 3, experts, rows, hidden), BF)],
+        + [jax.ShapeDtypeStruct((slabs, 3, number, rows, hidden), BF)],
+        input_output_aliases={1 + len(inputs) - len(earlier) + i: i for i in range(len(earlier))},
         compiler_params=pltpu.CompilerParams(
             dimension_semantics=("arbitrary",), vmem_limit_bytes=60 * 2**20
         ),
         cost_estimate=pl.CostEstimate(
-            flops=flops,
-            bytes_accessed=2 * (4 * count * experts * capacity * width + 6 * wg.size),
-            transcendentals=count * experts * capacity * hidden,
+            flops=18 * slots * width * hidden,
+            bytes_accessed=2 * (4 * slots * width + 6 * number * width * hidden),
+            transcendentals=slots * hidden,
         ),
         name="experts",
-    )(index, *xs, *gs, *places, gates, wg, wu, wd)
+    )(index, *inputs)
+
+
+def owned_kernel(*refs):
+    owned, sums = refs[-3:], refs[:-3]
+    experts = sum(ref.shape[2] for ref in sums)
+    at = 0
+    for ref in sums:
+        for e in range(ref.shape[2]):
+            for k, out in enumerate(owned):
+                out[pl.ds(at, ref.shape[3], stride=experts), :] = ref[0, k, e].astype(F32)
+            at += 1
+
+
+def run_owned(sums):
+    rows, hidden = sums[0].shape[3:]
+    experts = sum(x.shape[2] for x in sums)
+    lanes = 128
+    return pl.pallas_call(
+        owned_kernel,
+        grid=(hidden // lanes,),
+        in_specs=[
+            pl.BlockSpec((1, 3, x.shape[2], rows, lanes), lambda i: (0, 0, 0, 0, i)) for x in sums
+        ],
+        out_specs=[pl.BlockSpec((rows * experts, lanes), lambda i: (0, i))] * 3,
+        out_shape=[jax.ShapeDtypeStruct((rows * experts, hidden), F32)] * 3,
+        compiler_params=pltpu.CompilerParams(
+            dimension_semantics=("arbitrary",), vmem_limit_bytes=32 * 2**20
+        ),
+        cost_estimate=pl.CostEstimate(
+            flops=0, bytes_accessed=18 * rows * experts * hidden, transcendentals=0
+        ),
+        name="owned",
+    )(*sums)
 
 
 def body(
@@ -589,28 +625,30 @@
         [lax.dynamic_slice_in_dim(g.T, me * local_experts, local_experts, 0) for g in gates],
         axis=1,
     )
-    results = run_experts(
-        me_ref,
-        slot_rows,
-        cot_slots,
-        places,
-        gate_rows,
-        wg,
-        wu,
-        wd,
-        slabs,
-        expert_total,
-    )
-    slot_outs, slot_backs, expert_grads = (
-        results[:count],
-        results[count : 2 * count],
-        results[2 * count],
-    )
+    early = max(1, local_experts // 4)
+    results, expert_sums = [], []
+    for first, number in ((0, early), (early, local_experts - early)):
+        *results, grads = run_experts(
+            me_ref,
+            slot_rows,
+            cot_slots,
+            places,
+            gate_rows,
+            wg,
+            wu,
+            wd,
+            slabs,
+            expert_total,
+            first,
+            number,
+            results,
+        )
+        expert_sums.append(lax.psum_scatter(grads, "dp", scatter_dimension=0, tiled=True))
+    slot_outs, slot_backs = results[:count], results[count:]
     back_sum = line_scatter(
         [dot(places[s], slot_backs[s], 0, 0).astype(BF) for s in range(count)], "expert", count
     )
     mix_parts = [dot(places[s], slot_outs[s], 0, 0).astype(BF) for s in range(count)]
-    expert_owned = lax.psum_scatter(expert_grads, "dp", scatter_dimension=0, tiled=True)
 
     gate_own = gates[0]
     weighted = (
@@ -650,24 +688,23 @@
     key_value_sum.append(came)
     qkv_stages = slab_stages(qkv_state, slabs)
     qkv_halves = next(qkv_stages)
+    far, _ = lax.optimization_barrier((mix_parts[2:-1], qkv_state))
+    far = send_far(far, "expert", count)
     for step in range(slabs.bit_length() - 3):
         out_halves = out_stages.send(out_halves)
-        qkv_halves, out_halves, came = lax.optimization_barrier(
-            (qkv_halves, out_halves, key_value_came[1 + step : 2 + step])
+        qkv_halves, out_halves, far, came = lax.optimization_barrier(
+            (qkv_halves, out_halves, far, key_value_came[1 + step : 2 + step])
         )
         key_value_sum += came
         qkv_halves = qkv_stages.send(qkv_halves)
     left = key_value_came[len(key_value_sum) - 1 :]
     out_parts = own_parts(*out_halves, me, count)
     out_came = send_parts(out_parts, "expert", count)
-    qkv_halves, left, out_came, far = lax.optimization_barrier(
-        (qkv_halves, left, out_came, mix_parts[2:-1])
-    )
+    qkv_halves, left, out_came = lax.optimization_barrier((qkv_halves, left, out_came))
     key_value_sum = add_up(key_value_sum + left).astype(BF)
     out_sum = add_up(out_parts[:1] + out_came)
     qkv_parts = own_parts(*qkv_halves, me, count)
     qkv_sum = add_up(qkv_parts[:1] + send_parts(qkv_parts, "expert", count))
-    far = send_far(far, "expert", count)
     output = (middle + add_up(mix_parts[:1] + near + far)).astype(BF)
     pairs = key_width // PAIR
     qkv_sum = qkv_sum.reshape(qkv_sum.shape[0], pairs, (GROUP + 2) * PAIR)
@@ -695,7 +732,9 @@
         jnp.sum(own_packed[:, :qkv_width] * qkv_sum, axis=1)
         / own_packed[:, qkv_width + expert_total]
     )
-    owned = [jnp.transpose(expert_owned[0, k], (1, 0, 2)).astype(F32) for k in range(3)]
+    owned = [
+        x.reshape(width // slabs, local_experts, x.shape[1]) for x in run_owned(expert_sums)
+    ]
     return (
         output,
         grad_tokens,

time: 626 us -> 586 us (0.936)
  waiting for transfers between devices: 219 us -> 175 us
  Pallas kernels: 140 us -> 150 us
  local copies, waits for them, and re-layouts: 69.3 us -> 61.2 us
  starting transfers between devices: 82.6 us -> 90.4 us
  other arithmetic: 34.5 us -> 27.3 us
    ppermute x10, waiting for transfers between devices: 92.6 us -> 40.1 us  [trade(): lax.ppermute(send, 'dp', [(i, i ^ 1 << bit) for i in range(slabs)])]
    ppermute x1, waiting for transfers between devices: 9.76 us -> 34.2 us  [send_far(): lax.ppermute(part, axis, [(i, (i + count - s) % count) for i in range(cou...]
    ppermute x6, waiting for transfers between devices: 28.2 us -> 14.1 us  [send_parts(): lax.ppermute(parts[s], axis, [(i, (i + count - s) % count) for i in range...]
    pallas_call x1 -> x3, Pallas kernels: 65 us -> 75.5 us  [the longest x2 70.6 us: run_experts(): pl.pallas_call(functools.partial(expert_kernel, count, total, experts, fi...]
    unnamed x109 -> x114, local copies, waits for them, and re-layouts: 26.7 us -> 20.6 us
  transfers between devices with their start and end apart: 46 -> 47, of which waited for: 18 -> 18; matrix products, arithmetic and copies ran while one was open for 21% -> 22% of each run, Pallas kernels for 12% -> 22%
where the time goes in v2:
time: 586 us; the launch traced here: 578 us
  waiting for transfers between devices  175 us (30%)
  Pallas kernels  150 us (26%)
  starting transfers between devices  90.4 us (15%)
  local copies, waits for them, and re-layouts  61.2 us (10%)
  matrix products  57.6 us (10%)
  other arithmetic  27.3 us (5%)
  between operations  15.4 us (3%)
    pallas_call x2, Pallas kernels, run_experts(): pl.pallas_call(functools.partial(expert_kernel, count, total, experts, fi...  70.6 us
    dot_general x28, matrix products, dot(): lax.dot_general(a, b, (((ca,), (cb,)), ((), ())), preferred_element_type=...  57.6 us
    ppermute x10, waiting for transfers between devices, trade(): lax.ppermute(send, 'dp', [(i, i ^ 1 << bit) for i in range(slabs)])  40.1 us
    ppermute x3, waiting for transfers between devices, line_scatter(): right = lax.ppermute(right, axis, [(i, i + 1) for i in range(step)])  39.4 us
    pallas_call x1, Pallas kernels, run_back(): pl.pallas_call(functools.partial(back_kernel, count), grid_spec=pltpu.Pre...  37.4 us
    ppermute x1, waiting for transfers between devices, send_far(): lax.ppermute(part, axis, [(i, (i + count - s) % count) for i in range(cou...  34.2 us
    pallas_call x1, Pallas kernels, run_front(): pl.pallas_call(functools.partial(front_kernel, count, gain_at), grid_spec...  33.3 us
    optimization_barrier x2, local copies, waits for them, and re-layouts, body(): lax.optimization_barrier((up, down, turned, weights))  26.1 us
  transfers between devices with their start and end apart: 47, of which 18 were waited for; matrix products, arithmetic and copies ran while one was open for 22% of the time, Pallas kernels for 22%

profile of v2, /device:TPU:0, one launch (start us, length us, event | category | flops | bytes accessed | tf_op | source)
XLA Modules:
  0.0 577.7 jit_solution(583425696804825716)
XLA Ops:
  9.7 3.1 concatenate.31
  14.9 6.5 %collective-permute-start = (bf16[256,1536]{1,0:T(8,128)(2,1)S(1)}, bf16[256,1536]{1,0:T(8,128)(2,1)}, u32[]{:S(2)}, u32[]{:S(2)}) collective-permute-start(bf16[256,1536]{1,0:T(8,128)(2,1)S(1)} %copy-done.23), channel_id=1, source_target_pairs={{0,1},{1,2},{2,3},{4,5},{5,6},{6,7},{8,9},{9,10},{10,11},{12,13},{... | collective-permute-start | bytes 2359304 | tf_op jit(solution)/shard_map/ppermute | solution.py:317
  21.4 13.1 %copy.211 = bf16[1536,8,512]{2,0,1:T(8,128)(2,1)} copy(bf16[1536,8,512]{2,1,0:T(8,128)(2,1)} %param.22) | data formatting | bytes 25165824 | tf_op args[9]
  34.5 2.7 collective-permute-done.refs_1_
  40.3 13.3 %copy.210 = bf16[1536,8,512]{2,0,1:T(8,128)(2,1)} copy(bf16[1536,8,512]{2,1,0:T(8,128)(2,1)} %param.23) | data formatting | bytes 25165824 | tf_op jit(solution)/shard_map/optimization_barrier | solution.py:563
  53.6 6.2 %collective-permute-done.3 = bf16[256,1664]{0,1:T(8,128)(2,1)S(1)} collective-permute-done((bf16[256,1664]{0,1:T(8,128)(2,1)S(1)}, bf16[256,1664]{0,1:T(8,128)(2,1)S(1)}, u32[]{:S(2)}, u32[]{:S(2)}) %collective-permute-start.3) | collective-permute-done | bytes 852000 | tf_op jit(solution)/shard_map/ppermute | solution.py:322
  67.1 12.8 %copy.209 = bf16[1536,8,512]{2,0,1:T(8,128)(2,1)} copy(bf16[1536,8,512]{2,1,0:T(8,128)(2,1)} %param.24) | data formatting | bytes 25165824 | tf_op jit(solution)/shard_map/optimization_barrier | solution.py:563
  80.0 2.5 collective-permute-done.5
  83.3 5.1 collective-permute-start.7
  90.9 33.3 %front.1 = (bf16[1024,1536]{1,0:T(8,128)(2,1)}, f32[128,1536]{1,0:T(8,128)}, bf16[256,1536]{1,0:T(8,128)(2,1)}, bf16[1024,512]{1,0:T(8,128)(2,1)}, bf16[1024,512...) custom-call(s32[2]{0:T(128)} %pad_add_fusion.me_ref, bf16[256,1536]{1,0:T(8,128)(2,1)} %refs_0_, ...), custom_call_target="tpu_custom_call" | custom-call | flops 6039797760 | bytes 22806528 | tf_op jit(solution)/shard_map/front/pallas_call | solution.py:121
  125.2 4.1 multiply_reduce_fusion.2
  131.1 4.6 collective-permute-start.8
  141.7 7.0 %collective-permute-done.9 = bf16[256,1536]{1,0:T(8,128)(2,1)S(1)} collective-permute-done((bf16[256,1536]{1,0:T(8,128)(2,1)S(1)}, bf16[256,1536]{1,0:T(8,128)(2,1)S(1)}, u32[]{:S(2)}, u32[]{:S(2)}) %collective-permute-start.9) | collective-permute-done | bytes 786464 | tf_op jit(solution)/shard_map/ppermute | solution.py:298
  156.5 2.6 convolution_convert_fusion.7.refs_0_
  159.2 2.5 convolution_convert_fusion.refs_7_
  161.7 2.5 convolution_convert_fusion.1.refs_6_
  164.2 2.5 convolution_convert_fusion.2.refs_5_
  173.4 18.7 %collective-permute-done.11 = bf16[256,1536]{1,0:T(8,128)(2,1)S(1)} collective-permute-done((bf16[256,1536]{1,0:T(8,128)(2,1)S(1)}, bf16[256,1536]{1,0:T(8,128)(2,1)S(1)}, u32[]{:S(2)}, u32[]{:S(2)}) %collective-permute-start.11) | collective-permute-done | bytes 786464 | tf_op jit(solution)/shard_map/ppermute | solution.py:298
  197.2 4.0 convolution_convert_fusion.4.refs_3_
  203.5 20.6 %experts.2 = (bf16[896,1536]{1,0:T(8,128)(2,1)}, bf16[896,1536]{1,0:T(8,128)(2,1)}, bf16[896,1536]{1,0:T(8,128)(2,1)}, bf16[896,1536]{1,0:T(8,128)(2,1)}, bf16[8...) custom-call(s32[2]{0:T(128)} %pad_add_fusion.me_ref, ...), custom_call_target="tpu_custom_call" | custom-call | flops 12683575296 | bytes 29884416 | tf_op jit(solution)/shard_map/experts/pallas_call | solution.py:452
  224.4 49.9 %experts.3 = (bf16[896,1536]{1,0:T(8,128)(2,1)}, bf16[896,1536]{1,0:T(8,128)(2,1)}, bf16[896,1536]{1,0:T(8,128)(2,1)}, bf16[896,1536]{1,0:T(8,128)(2,1)}, bf16[8...) custom-call(s32[2]{0:T(128)} %pad_add_fusion.me_ref, ...), custom_call_target="tpu_custom_call", output_to_operand_aliasing={{0}: (17, {}), {1}: (18, {}), {2}: (19, {}), {3}: (20, {}),... | custom-call | flops 38050725888 | bytes 89653248 | tf_op jit(solution)/shard_map/experts/pallas_call | solution.py:452
  274.4 3.2 convolution_convert_fusion.12
  281.0 14.9 %collective-permute-done.15 = bf16[256,1664]{1,0:T(8,128)(2,1)S(1)} collective-permute-done((bf16[256,1664]{1,0:T(8,128)(2,1)S(1)}, bf16[256,1664]{1,0:T(8,128)(2,1)S(1)}, u32[]{:S(2)}, u32[]{:S(2)}) %collective-permute-start.15) | collective-permute-done | bytes 852000 | tf_op jit(solution)/shard_map/ppermute | solution.py:307
  297.1 4.4 collective-permute-start.16
  302.4 13.1 %collective-permute-done.16 = bf16[256,1664]{1,0:T(8,128)(2,1)S(1)} collective-permute-done((bf16[256,1664]{1,0:T(8,128)(2,1)S(1)}, bf16[256,1664]{1,0:T(8,128)(2,1)S(1)}, u32[]{:S(2)}, u32[]{:S(2)}) %collective-permute-start.16) | collective-permute-done | bytes 852000 | tf_op jit(solution)/shard_map/ppermute | solution.py:307
  315.7 17.3 %collective-permute-start.17 = (bf16[256,1664]{1,0:T(8,128)(2,1)S(1)}, bf16[256,1664]{1,0:T(8,128)(2,1)S(1)}, u32[]{:S(2)}, u32[]{:S(2)}) collective-permute-start(bf16[256,1664]{1,0:T(8,128)(2,1)S(1)} %add.262), channel_id=1, source_target_pairs={{0,1},{1,2},{2,3},{4,5},{5,6},{6,7},{8,9},{9,10},{10,11},{12,13},{... | collective-permute-start | bytes 2555912 | tf_op jit(solution)/shard_map/ppermute | solution.py:307
  335.9 11.4 %collective-permute-done.17 = bf16[256,1664]{1,0:T(8,128)(2,1)S(1)} collective-permute-done((bf16[256,1664]{1,0:T(8,128)(2,1)S(1)}, bf16[256,1664]{1,0:T(8,128)(2,1)S(1)}, u32[]{:S(2)}, u32[]{:S(2)}) %collective-permute-start.17) | collective-permute-done | bytes 852000 | tf_op jit(solution)/shard_map/ppermute | solution.py:307
  347.3 5.1 collective-permute-done.20
  356.5 4.2 out_grad.1
  360.6 4.8 copy.189
  365.5 3.8 convolution_convert_fusion.11
  382.1 37.4 %back.1 = (bf16[256,1536]{1,0:T(8,128)(2,1)}, bf16[1024,512]{1,0:T(8,128)(2,1)}, bf16[1024,512]{1,0:T(8,128)(2,1)}, bf16[4,192,2560]{2,1,0:T(8,128)(2,1)}, bf16[4,192,2560]{2,1,0:T(8,128)(2,1)}) custom-call(s32[2]{0:T(128)} %pad_add_fusion.me_ref, bf16[256,1536]{1,0:T(8,128)(2,1)} %copy-done.2, bf16[1536,1536]{1,0:T(8,128)(2,1)} %all-gather.5.cloned.1.call-done.refs_1_, ...), custom_call_target="tpu_custom_call" | custom-call | flops 9663676416 | bytes 12582912 | tf_op jit(solution)/shard_map/back/pallas_call | solution.py:249
  424.0 3.9 fusion
  430.3 3.6 add.275
  433.9 5.1 collective-permute-done.27
  447.0 34.2 %collective-permute-done.30 = bf16[96,1664]{1,0:T(8,128)(2,1)S(1)} collective-permute-done((bf16[96,1664]{1,0:T(8,128)(2,1)S(1)}, bf16[96,1664]{1,0:T(8,128)(2,1)S(1)}, u32[]{:S(2)}, u32[]{:S(2)}) %collective-permute-start.30) | collective-permute-done | bytes 319520 | tf_op jit(solution)/shard_map/ppermute | solution.py:355
  481.3 2.5 collective-permute-start.32
  484.0 34.2 %collective-permute-done.32 = bf16[256,1536]{1,0:T(8,128)(2,1)S(1)} collective-permute-done((bf16[256,1536]{1,0:T(8,128)(2,1)S(1)}, bf16[256,1536]{1,0:T(8,128)(2,1)S(1)}, u32[]{:S(2)}, u32[]{:S(2)}) %collective-permute-start.32) | collective-permute-done | bytes 786464 | tf_op jit(solution)/shard_map/ppermute | solution.py:342
  521.1 3.4 collective-permute-start.38
  524.5 2.7 add_convert_fusion
  527.2 4.9 collective-permute-done.35
  532.1 3.3 collective-permute-start.37
  535.6 3.1 collective-permute-done.37
  538.9 4.3 collective-permute-start.40
  543.9 3.3 fusion.11
  550.7 4.8 collective-permute-done.42
  555.5 6.2 %collective-permute-done.41 = bf16[48,2560]{1,0:T(8,128)(2,1)S(1)} collective-permute-done((bf16[48,2560]{1,0:T(8,128)(2,1)S(1)}, bf16[48,2560]{1,0:T(8,128)(2,1)S(1)}, u32[]{:S(2)}, u32[]{:S(2)}) %collective-permute-start.41) | collective-permute-done | bytes 245792 | tf_op jit(solution)/shard_map/ppermute | solution.py:327
  566.1 4.9 owned.1
  (298 shorter events, 100.6 us)
Async XLA Ops:
  7.2 75.3 %all-gather.3.cloned.1.call-start = ((), (), s32[]{:S(2)}) async-start(), calls=%async_computation.2 | async-start | bytes 9289728 | tf_op jit(solution)/shard_map/all_gather | solution.py:546
  12.8 112.4 %all-gather.5.cloned.1.call-start = ((), (), s32[]{:S(2)}) async-start(), calls=%async_computation.3 | async-start | bytes 5308416 | tf_op jit(solution)/shard_map/all_gather | solution.py:570
  13.6 23.9 %collective-permute-start.1 = (bf16[256,1664]{0,1:T(8,128)(2,1)S(1)}, bf16[256,1664]{0,1:T(8,128)(2,1)S(1)}, u32[]{:S(2)}, u32[]{:S(2)}) collective-permute-start(bf16[256,1664]{0,1:T(8,128)(2,1)S(1)} %maximum_maximum_fusion), channel_id=1, source_target_pairs={{1,0},{2,1},{3,2},{5,4},{6,5},{7,6},{9,8},{10,9},{11,10},{13,12},{... | collective-permute-start | bytes 2555912 | tf_op jit(solution)/shard_map/ppermute | solution.py:322
  14.9 22.3 %collective-permute-start = (bf16[256,1536]{1,0:T(8,128)(2,1)S(1)}, bf16[256,1536]{1,0:T(8,128)(2,1)}, u32[]{:S(2)}, u32[]{:S(2)}) collective-permute-start(bf16[256,1536]{1,0:T(8,128)(2,1)S(1)} %copy-done.23), channel_id=1, source_target_pairs={{0,1},{1,2},{2,3},{4,5},{5,6},{6,7},{8,9},{9,10},{10,11},{12,13},{... | collective-permute-start | bytes 2359304 | tf_op jit(solution)/shard_map/ppermute | solution.py:317
  37.4 22.3 %collective-permute-start.3 = (bf16[256,1664]{0,1:T(8,128)(2,1)S(1)}, bf16[256,1664]{0,1:T(8,128)(2,1)S(1)}, u32[]{:S(2)}, u32[]{:S(2)}) collective-permute-start(bf16[256,1664]{0,1:T(8,128)(2,1)S(1)} %collective-permute-done.1), channel_id=1, source_target_pairs={{1,0},{2,1},{5,4},{6,5},{9,8},{10,9},{13,12},{14,13},{17,16},{18,1... | collective-permute-start | bytes 2555912 | tf_op jit(solution)/shard_map/ppermute | solution.py:322
  38.7 14.8 %collective-permute-start.2 = (bf16[256,1536]{1,0:T(8,128)(2,1)}, bf16[256,1536]{1,0:T(8,128)(2,1)}, u32[]{:S(2)}, u32[]{:S(2)}) collective-permute-start(bf16[256,1536]{1,0:T(8,128)(2,1)} %collective-permute-done.refs_1_), channel_id=1, source_target_pairs={{1,2},{2,3},{5,6},{6,7},{9,10},{10,11},{13,14},{14,15},{17,18},{18... | collective-permute-start | bytes 2359304 | tf_op jit(solution)/shard_map/ppermute | solution.py:317
  59.8 20.2 %collective-permute-start.4 = (bf16[256,1536]{1,0:T(8,128)(2,1)}, bf16[256,1536]{1,0:T(8,128)(2,1)}, u32[]{:S(2)}, u32[]{:S(2)}) collective-permute-start(bf16[256,1536]{1,0:T(8,128)(2,1)} %collective-permute-done.2.refs_2_), channel_id=1, source_target_pairs={{2,3},{6,7},{10,11},{14,15},{18,19},{22,23},{26,27},{30,31}} | collective-permute-start | bytes 2359304 | tf_op jit(solution)/shard_map/ppermute | solution.py:317
  61.3 21.2 %collective-permute-start.5 = (bf16[256,1664]{0,1:T(8,128)(2,1)S(1)}, bf16[256,1664]{0,1:T(8,128)(2,1)S(1)}, u32[]{:S(2)}, u32[]{:S(2)}) collective-permute-start(bf16[256,1664]{0,1:T(8,128)(2,1)S(1)} %collective-permute-done.3), channel_id=1, source_target_pairs={{1,0},{5,4},{9,8},{13,12},{17,16},{21,20},{25,24},{29,28}} | collective-permute-start | bytes 2555912 | tf_op jit(solution)/shard_map/ppermute | solution.py:322
  82.5 480.3 %reduce-scatter.3.cloned.1.call-start = ((), (), s32[]{:S(2)}) async-start(), calls=%async_computation.4 | async-start | bytes 10616832 | tf_op jit(solution)/shard_map/reduce_scatter | solution.py:646
  83.3 52.5 %collective-permute-start.7 = (bf16[256,1664]{0,1:T(8,128)(2,1)S(1)}, bf16[256,1664]{0,1:T(8,128)(2,1)}, u32[]{:S(2)}, u32[]{:S(2)}) collective-permute-start(bf16[256,1664]{0,1:T(8,128)(2,1)S(1)} %maximum_maximum_fusion), channel_id=1, source_target_pairs={{0,2},{1,3},{4,6},{5,7},{8,10},{9,11},{12,14},{13,15},{16,18},{17,... | collective-permute-start | bytes 2555912 | tf_op jit(solution)/shard_map/ppermute | solution.py:317
  88.4 47.4 %collective-permute-start.6 = (bf16[256,1664]{0,1:T(8,128)(2,1)S(1)}, bf16[256,1664]{0,1:T(8,128)(2,1)}, u32[]{:S(2)}, u32[]{:S(2)}) collective-permute-start(bf16[256,1664]{0,1:T(8,128)(2,1)S(1)} %maximum_maximum_fusion), channel_id=1, source_target_pairs={{0,1},{1,2},{2,3},{4,5},{5,6},{6,7},{8,9},{9,10},{10,11},{12,13},{... | collective-permute-start | bytes 2555912 | tf_op jit(solution)/shard_map/ppermute | solution.py:317
  129.3 225.4 %copy-start.5 = (f32[256,1536]{1,0:T(8,128)}, f32[256,1536]{1,0:T(8,128)S(1)}, u32[]{:S(2)}) copy-start(f32[256,1536]{1,0:T(8,128)S(1)} %get-tuple-element.341) | copy-start | bytes 4718596
  129.6 19.2 %collective-permute-start.9 = (bf16[256,1536]{1,0:T(8,128)(2,1)S(1)}, bf16[256,1536]{1,0:T(8,128)(2,1)S(1)}, u32[]{:S(2)}, u32[]{:S(2)}) collective-permute-start(bf16[256,1536]{1,0:T(8,128)(2,1)S(1)} %multiply_convert_fusion.1.normed_ref), channel_id=1, source_target_pairs={{1,0},{2,1},{3,2},{5,4},{6,5},{7,6},{9,8},{10,9},{11,10},{13,12},{... | collective-permute-start | bytes 2359304 | tf_op jit(solution)/shard_map/ppermute | solution.py:298
  131.1 18.9 %collective-permute-start.8 = (bf16[256,1536]{1,0:T(8,128)(2,1)S(1)}, bf16[256,1536]{1,0:T(8,128)(2,1)S(1)}, u32[]{:S(2)}, u32[]{:S(2)}) collective-permute-start(bf16[256,1536]{1,0:T(8,128)(2,1)S(1)} %multiply_convert_fusion.1.normed_ref), channel_id=1, source_target_pairs={{0,1},{1,2},{2,3},{4,5},{5,6},{6,7},{8,9},{9,10},{10,11},{12,13},{... | collective-permute-start | bytes 2359304 | tf_op jit(solution)/shard_map/ppermute | solution.py:296
  137.2 13.8 %collective-permute-start.13 = (bf16[256,1664]{0,1:T(8,128)(2,1)}, bf16[256,1664]{0,1:T(8,128)(2,1)S(1)}, u32[]{:S(2)}, u32[]{:S(2)}) collective-permute-start(bf16[256,1664]{0,1:T(8,128)(2,1)} %collective-permute-done.7), channel_id=1, source_target_pairs={{2,3},{6,7},{10,11},{14,15},{18,19},{22,23},{26,27},{30,31}} | collective-permute-start | bytes 2555912 | tf_op jit(solution)/shard_map/ppermute | solution.py:317
  148.7 18.0 %collective-permute-start.10 = (bf16[256,1536]{1,0:T(8,128)(2,1)S(1)}, bf16[256,1536]{1,0:T(8,128)(2,1)S(1)}, u32[]{:S(2)}, u32[]{:S(2)}) collective-permute-start(bf16[256,1536]{1,0:T(8,128)(2,1)S(1)} %collective-permute-done.9), channel_id=1, source_target_pairs={{1,0},{2,1},{5,4},{6,5},{9,8},{10,9},{13,12},{14,13},{17,16},{18,1... | collective-permute-start | bytes 2359304 | tf_op jit(solution)/shard_map/ppermute | solution.py:298
  150.1 18.0 %collective-permute-start.12 = (bf16[256,1536]{1,0:T(8,128)(2,1)S(1)}, bf16[256,1536]{1,0:T(8,128)(2,1)S(1)}, u32[]{:S(2)}, u32[]{:S(2)}) collective-permute-start(bf16[256,1536]{1,0:T(8,128)(2,1)S(1)} %collective-permute-done.8), channel_id=1, source_target_pairs={{1,2},{2,3},{5,6},{6,7},{9,10},{10,11},{13,14},{14,15},{17,18},{18... | collective-permute-start | bytes 2359304 | tf_op jit(solution)/shard_map/ppermute | solution.py:296
  166.7 25.4 %collective-permute-start.11 = (bf16[256,1536]{1,0:T(8,128)(2,1)S(1)}, bf16[256,1536]{1,0:T(8,128)(2,1)S(1)}, u32[]{:S(2)}, u32[]{:S(2)}) collective-permute-start(bf16[256,1536]{1,0:T(8,128)(2,1)S(1)} %collective-permute-done.10), channel_id=1, source_target_pairs={{1,0},{5,4},{9,8},{13,12},{17,16},{21,20},{25,24},{29,28}} | collective-permute-start | bytes 2359304 | tf_op jit(solution)/shard_map/ppermute | solution.py:298
  168.0 26.2 %collective-permute-start.14 = (bf16[256,1536]{1,0:T(8,128)(2,1)S(1)}, bf16[256,1536]{1,0:T(8,128)(2,1)S(1)}, u32[]{:S(2)}, u32[]{:S(2)}) collective-permute-start(bf16[256,1536]{1,0:T(8,128)(2,1)S(1)} %collective-permute-done.12), channel_id=1, source_target_pairs={{2,3},{6,7},{10,11},{14,15},{18,19},{22,23},{26,27},{30,31}} | collective-permute-start | bytes 2359304 | tf_op jit(solution)/shard_map/ppermute | solution.py:296
  224.2 338.6 %reduce-scatter.5.cloned.1.call-start = ((), (), s32[]{:S(2)}) async-start(), calls=%async_computation.5 | async-start | bytes 31850496 | tf_op jit(solution)/shard_map/reduce_scatter | solution.py:646
  278.8 2.2 collective-permute-start.18
  279.5 16.3 %collective-permute-start.15 = (bf16[256,1664]{1,0:T(8,128)(2,1)S(1)}, bf16[256,1664]{1,0:T(8,128)(2,1)S(1)}, u32[]{:S(2)}, u32[]{:S(2)}) collective-permute-start(bf16[256,1664]{1,0:T(8,128)(2,1)S(1)} %convolution_convert_fusion.12), channel_id=1, source_target_pairs={{0,1},{4,5},{8,9},{12,13},{16,17},{20,21},{24,25},{28,29}} | collective-permute-start | bytes 2555912 | tf_op jit(solution)/shard_map/ppermute | solution.py:307
  297.1 18.4 %collective-permute-start.16 = (bf16[256,1664]{1,0:T(8,128)(2,1)S(1)}, bf16[256,1664]{1,0:T(8,128)(2,1)S(1)}, u32[]{:S(2)}, u32[]{:S(2)}) collective-permute-start(bf16[256,1664]{1,0:T(8,128)(2,1)S(1)} %get-tuple-element.304), channel_id=1, source_target_pairs={{0,1},{1,2},{4,5},{5,6},{8,9},{9,10},{12,13},{13,14},{16,17},{17,1... | collective-permute-start | bytes 2555912 | tf_op jit(solution)/shard_map/ppermute | solution.py:307
  301.5 31.4 %collective-permute-start.19 = (bf16[256,1664]{1,0:T(8,128)(2,1)S(1)}, bf16[256,1664]{1,0:T(8,128)(2,1)S(1)}, u32[]{:S(2)}, u32[]{:S(2)}) collective-permute-start(bf16[256,1664]{1,0:T(8,128)(2,1)S(1)} %get-tuple-element.305), channel_id=1, source_target_pairs={{2,1},{3,2},{6,5},{7,6},{10,9},{11,10},{14,13},{15,14},{18,17},{19... | collective-permute-start | bytes 2555912 | tf_op jit(solution)/shard_map/ppermute | solution.py:308
  315.7 31.6 %collective-permute-start.17 = (bf16[256,1664]{1,0:T(8,128)(2,1)S(1)}, bf16[256,1664]{1,0:T(8,128)(2,1)S(1)}, u32[]{:S(2)}, u32[]{:S(2)}) collective-permute-start(bf16[256,1664]{1,0:T(8,128)(2,1)S(1)} %add.262), channel_id=1, source_target_pairs={{0,1},{1,2},{2,3},{4,5},{5,6},{6,7},{8,9},{9,10},{10,11},{12,13},{... | collective-permute-start | bytes 2555912 | tf_op jit(solution)/shard_map/ppermute | solution.py:307
  333.2 19.2 %collective-permute-start.20 = (bf16[256,1664]{1,0:T(8,128)(2,1)S(1)}, bf16[256,1664]{1,0:T(8,128)(2,1)S(1)}, u32[]{:S(2)}, u32[]{:S(2)}) collective-permute-start(bf16[256,1664]{1,0:T(8,128)(2,1)S(1)} %add.265), channel_id=1, source_target_pairs={{1,0},{2,1},{3,2},{5,4},{6,5},{7,6},{9,8},{10,9},{11,10},{13,12},{... | collective-permute-start | bytes 2555912 | tf_op jit(solution)/shard_map/ppermute | solution.py:308
  360.6 15.1 %collective-permute-start.21 = (bf16[4,192,1664]{2,1,0:T(8,128)(2,1)}, bf16[4,192,1664]{2,1,0:T(8,128)(2,1)}, u32[]{:S(2)}, u32[]{:S(2)}) collective-permute-start(bf16[4,192,1664]{2,1,0:T(8,128)(2,1)} %get-tuple-element.159), channel_id=1, source_target_pairs={{0,4},{4,0},{8,12},{12,8},{16,20},{20,16},{24,28},{28,24},{1,5},{5... | collective-permute-start | bytes 7667720 | tf_op jit(solution)/shard_map/ppermute | solution.py:355
  378.1 41.4 %collective-permute-start.25 = (bf16[2,96,1664]{2,1,0:T(8,128)(2,1)S(1)}, bf16[2,96,1664]{2,1,0:T(8,128)(2,1)S(1)}, u32[]{:S(2)}, u32[]{:S(2)}) collective-permute-start(bf16[2,96,1664]{2,1,0:T(8,128)(2,1)S(1)} %slice_bitcast_fusion.4), channel_id=1, source_target_pairs={{0,16},{4,20},{8,24},{12,28},{16,0},{20,4},{24,8},{28,12},{1,17},{... | collective-permute-start | bytes 1916936 | tf_op jit(solution)/shard_map/ppermute | solution.py:355
  379.5 40.0 %collective-permute-start.24 = (bf16[2,96,1664]{2,1,0:T(8,128)(2,1)S(1)}, bf16[2,96,1664]{2,1,0:T(8,128)(2,1)S(1)}, u32[]{:S(2)}, u32[]{:S(2)}) collective-permute-start(bf16[2,96,1664]{2,1,0:T(8,128)(2,1)S(1)} %slice_bitcast_fusion.6), channel_id=1, source_target_pairs={{0,8},{4,12},{8,0},{12,4},{16,24},{20,28},{24,16},{28,20},{1,9},{5... | collective-permute-start | bytes 1916936 | tf_op jit(solution)/shard_map/ppermute | solution.py:355
  379.7 40.0 %collective-permute-start.22 = (bf16[256,1536]{1,0:T(8,128)(2,1)}, bf16[256,1536]{1,0:T(8,128)(2,1)}, u32[]{:S(2)}, u32[]{:S(2)}) collective-permute-start(bf16[256,1536]{1,0:T(8,128)(2,1)} %convolution_convert_fusion.10), channel_id=1, source_target_pairs={{0,3},{1,0},{2,1},{3,2},{4,7},{5,4},{6,5},{7,6},{8,11},{9,8},{10,9... | collective-permute-start | bytes 2359304 | tf_op jit(solution)/shard_map/ppermute | solution.py:335
  379.8 39.9 %collective-permute-start.23 = (bf16[256,1536]{1,0:T(8,128)(2,1)}, bf16[256,1536]{1,0:T(8,128)(2,1)}, u32[]{:S(2)}, u32[]{:S(2)}) collective-permute-start(bf16[256,1536]{1,0:T(8,128)(2,1)} %convolution_convert_fusion.8), channel_id=1, source_target_pairs={{0,1},{1,2},{2,3},{3,0},{4,5},{5,6},{6,7},{7,4},{8,9},{9,10},{10,1... | collective-permute-start | bytes 2359304 | tf_op jit(solution)/shard_map/ppermute | solution.py:335
  419.7 10.7 %collective-permute-start.26 = (bf16[4,192,2560]{2,1,0:T(8,128)(2,1)}, bf16[4,192,2560]{2,1,0:T(8,128)(2,1)}, u32[]{:S(2)}, u32[]{:S(2)}) collective-permute-start(bf16[4,192,2560]{2,1,0:T(8,128)(2,1)} %get-tuple-element.177), channel_id=1, source_target_pairs={{0,4},{4,0},{8,12},{12,8},{16,20},{20,16},{24,28},{28,24},{1,5},{5... | collective-permute-start | bytes 11796488 | tf_op jit(solution)/shard_map/ppermute | solution.py:355
  422.7 16.3 %collective-permute-start.27 = (bf16[256,1024]{1,0:T(8,128)(2,1)S(1)}, bf16[256,1024]{1,0:T(8,128)(2,1)S(1)}, u32[]{:S(2)}, u32[]{:S(2)}) collective-permute-start(bf16[256,1024]{1,0:T(8,128)(2,1)S(1)} %get-tuple-element.300), channel_id=1, source_target_pairs={{1,0},{2,1},{3,2},{5,4},{6,5},{7,6},{9,8},{10,9},{11,10},{13,12},{... | collective-permute-start | bytes 1572872 | tf_op jit(solution)/shard_map/ppermute | solution.py:322
  428.0 17.6 %collective-permute-start.31 = (bf16[96,1664]{1,0:T(8,128)(2,1)S(1)}, bf16[96,1664]{1,0:T(8,128)(2,1)S(1)}, u32[]{:S(2)}, u32[]{:S(2)}) collective-permute-start(bf16[96,1664]{1,0:T(8,128)(2,1)S(1)} %slice_bitcast_fusion.10), channel_id=1, source_target_pairs={{0,8},{4,12},{8,0},{12,4},{16,24},{20,28},{24,16},{28,20},{1,9},{5... | collective-permute-start | bytes 958472 | tf_op jit(solution)/shard_map/ppermute | solution.py:355
  439.1 44.7 %collective-permute-start.28 = (bf16[2,96,2560]{2,1,0:T(8,128)(2,1)S(1)}, bf16[2,96,2560]{2,1,0:T(8,128)(2,1)S(1)}, u32[]{:S(2)}, u32[]{:S(2)}) collective-permute-start(bf16[2,96,2560]{2,1,0:T(8,128)(2,1)S(1)} %slice_bitcast_fusion.2), channel_id=1, source_target_pairs={{0,8},{4,12},{8,0},{12,4},{16,24},{20,28},{24,16},{28,20},{1,9},{5... | collective-permute-start | bytes 2949128 | tf_op jit(solution)/shard_map/ppermute | solution.py:355
  441.1 42.7 %collective-permute-start.29 = (bf16[2,96,2560]{2,1,0:T(8,128)(2,1)S(1)}, bf16[2,96,2560]{2,1,0:T(8,128)(2,1)S(1)}, u32[]{:S(2)}, u32[]{:S(2)}) collective-permute-start(bf16[2,96,2560]{2,1,0:T(8,128)(2,1)S(1)} %slice_bitcast_fusion), channel_id=1, source_target_pairs={{0,16},{4,20},{8,24},{12,28},{16,0},{20,4},{24,8},{28,12},{1,17},{... | collective-permute-start | bytes 2949128 | tf_op jit(solution)/shard_map/ppermute | solution.py:355
  442.0 39.3 %collective-permute-start.30 = (bf16[96,1664]{1,0:T(8,128)(2,1)S(1)}, bf16[96,1664]{1,0:T(8,128)(2,1)S(1)}, u32[]{:S(2)}, u32[]{:S(2)}) collective-permute-start(bf16[96,1664]{1,0:T(8,128)(2,1)S(1)} %slice_bitcast_fusion.11), channel_id=1, source_target_pairs={{0,16},{4,20},{8,24},{12,28},{16,0},{20,4},{24,8},{28,12},{1,17},{... | collective-permute-start | bytes 958472 | tf_op jit(solution)/shard_map/ppermute | solution.py:355
  443.3 92.3 %collective-permute-start.36 = (bf16[256,1024]{1,0:T(8,128)(2,1)S(1)}, bf16[256,1024]{1,0:T(8,128)(2,1)S(1)}, u32[]{:S(2)}, u32[]{:S(2)}) collective-permute-start(bf16[256,1024]{1,0:T(8,128)(2,1)S(1)} %get-tuple-element.298), channel_id=1, source_target_pairs={{3,0},{7,4},{11,8},{15,12},{19,16},{23,20},{27,24},{31,28}} | collective-permute-start | bytes 1572872 | tf_op jit(solution)/shard_map/ppermute | solution.py:322
  445.5 38.5 %collective-permute-start.33 = (bf16[256,1024]{1,0:T(8,128)(2,1)S(1)}, bf16[256,1024]{1,0:T(8,128)(2,1)S(1)}, u32[]{:S(2)}, u32[]{:S(2)}) collective-permute-start(bf16[256,1024]{1,0:T(8,128)(2,1)S(1)} %get-tuple-element.299), channel_id=1, source_target_pairs={{2,0},{3,1},{6,4},{7,5},{10,8},{11,9},{14,12},{15,13},{18,16},{19,... | collective-permute-start | bytes 1572872 | tf_op jit(solution)/shard_map/ppermute | solution.py:322
  481.3 36.9 %collective-permute-start.32 = (bf16[256,1536]{1,0:T(8,128)(2,1)S(1)}, bf16[256,1536]{1,0:T(8,128)(2,1)S(1)}, u32[]{:S(2)}, u32[]{:S(2)}) collective-permute-start(bf16[256,1536]{1,0:T(8,128)(2,1)S(1)} %copy-done.50), channel_id=1, source_target_pairs={{0,2},{1,3},{2,0},{3,1},{4,6},{5,7},{6,4},{7,5},{8,10},{9,11},{10,... | collective-permute-start | bytes 2359304 | tf_op jit(solution)/shard_map/ppermute | solution.py:342
  518.2 13.9 %collective-permute-start.35 = (bf16[96,2560]{1,0:T(8,128)(2,1)S(1)}, bf16[96,2560]{1,0:T(8,128)(2,1)S(1)}, u32[]{:S(2)}, u32[]{:S(2)}) collective-permute-start(bf16[96,2560]{1,0:T(8,128)(2,1)S(1)} %slice_bitcast_fusion.8), channel_id=1, source_target_pairs={{0,8},{4,12},{8,0},{12,4},{16,24},{20,28},{24,16},{28,20},{1,9},{5... | collective-permute-start | bytes 1474568 | tf_op jit(solution)/shard_map/ppermute | solution.py:355
  519.9 15.6 %collective-permute-start.34 = (bf16[96,2560]{1,0:T(8,128)(2,1)S(1)}, bf16[96,2560]{1,0:T(8,128)(2,1)S(1)}, u32[]{:S(2)}, u32[]{:S(2)}) collective-permute-start(bf16[96,2560]{1,0:T(8,128)(2,1)S(1)} %slice_bitcast_fusion.9), channel_id=1, source_target_pairs={{0,16},{4,20},{8,24},{12,28},{16,0},{20,4},{24,8},{28,12},{1,17},{... | collective-permute-start | bytes 1474568 | tf_op jit(solution)/shard_map/ppermute | solution.py:355
  520.6 15.0 %collective-permute-start.39 = (bf16[48,1664]{1,0:T(8,128)(2,1)S(1)}, bf16[48,1664]{1,0:T(8,128)(2,1)S(1)}, u32[]{:S(2)}, u32[]{:S(2)}) collective-permute-start(bf16[48,1664]{1,0:T(8,128)(2,1)S(1)} %get-tuple-element.314), channel_id=1, source_target_pairs={{0,1},{1,2},{2,3},{3,0},{4,5},{5,6},{6,7},{7,4},{8,9},{9,10},{10,1... | collective-permute-start | bytes 479240 | tf_op jit(solution)/shard_map/ppermute | solution.py:327
  521.1 14.5 %collective-permute-start.38 = (bf16[48,1664]{1,0:T(8,128)(2,1)S(1)}, bf16[48,1664]{1,0:T(8,128)(2,1)S(1)}, u32[]{:S(2)}, u32[]{:S(2)}) collective-permute-start(bf16[48,1664]{1,0:T(8,128)(2,1)S(1)} %get-tuple-element.315), channel_id=1, source_target_pairs={{0,2},{1,3},{2,0},{3,1},{4,6},{5,7},{6,4},{7,5},{8,10},{9,11},{10,... | collective-permute-start | bytes 479240 | tf_op jit(solution)/shard_map/ppermute | solution.py:327
  532.1 6.6 %collective-permute-start.37 = (bf16[48,1664]{1,0:T(8,128)(2,1)S(1)}, bf16[48,1664]{1,0:T(8,128)(2,1)S(1)}, u32[]{:S(2)}, u32[]{:S(2)}) collective-permute-start(bf16[48,1664]{1,0:T(8,128)(2,1)S(1)} %get-tuple-element.316), channel_id=1, source_target_pairs={{0,3},{1,0},{2,1},{3,2},{4,7},{5,4},{6,5},{7,6},{8,11},{9,8},{10,9... | collective-permute-start | bytes 479240 | tf_op jit(solution)/shard_map/ppermute | solution.py:327
  538.9 11.8 %collective-permute-start.40 = (bf16[48,2560]{1,0:T(8,128)(2,1)S(1)}, bf16[48,2560]{1,0:T(8,128)(2,1)S(1)}, u32[]{:S(2)}, u32[]{:S(2)}) collective-permute-start(bf16[48,2560]{1,0:T(8,128)(2,1)S(1)} %get-tuple-element.301), channel_id=1, source_target_pairs={{0,3},{1,0},{2,1},{3,2},{4,7},{5,4},{6,5},{7,6},{8,11},{9,8},{10,9... | collective-permute-start | bytes 737288 | tf_op jit(solution)/shard_map/ppermute | solution.py:327
  543.2 12.2 %collective-permute-start.42 = (bf16[48,2560]{1,0:T(8,128)(2,1)S(1)}, bf16[48,2560]{1,0:T(8,128)(2,1)S(1)}, u32[]{:S(2)}, u32[]{:S(2)}) collective-permute-start(bf16[48,2560]{1,0:T(8,128)(2,1)S(1)} %get-tuple-element.302), channel_id=1, source_target_pairs={{0,1},{1,2},{2,3},{3,0},{4,5},{5,6},{6,7},{7,4},{8,9},{9,10},{10,1... | collective-permute-start | bytes 737288 | tf_op jit(solution)/shard_map/ppermute | solution.py:327
  543.2 18.4 %collective-permute-start.41 = (bf16[48,2560]{1,0:T(8,128)(2,1)S(1)}, bf16[48,2560]{1,0:T(8,128)(2,1)S(1)}, u32[]{:S(2)}, u32[]{:S(2)}) collective-permute-start(bf16[48,2560]{1,0:T(8,128)(2,1)S(1)} %get-tuple-element.303), channel_id=1, source_target_pairs={{0,2},{1,3},{2,0},{3,1},{4,6},{5,7},{6,4},{7,5},{8,10},{9,11},{10,... | collective-permute-start | bytes 737288 | tf_op jit(solution)/shard_map/ppermute | solution.py:327
  (51 other events, 919.6 us)
Sparse Core Ops, SparseCore 0:
  12.9 56.5 all-gather.2
  82.6 38.6 all-gather.4
  224.3 87.6 reduce-scatter.2
  315.5 209.1 reduce-scatter.4

commit v3 on v2

--- a/solution.py
+++ b/solution.py
@@ -299,17 +299,20 @@
     return [block] + [right[s] + left[count - s] for s in range(1, count)]
 
 
-def line_scatter(parts, axis, count):
+def line_scatter(parts, axis, count, beside):
     if count == 1:
-        return parts[0].astype(F32)
-    right, left = parts[1], parts[count - 1]
+        return parts[0].astype(F32), beside
+    right, left, ready = parts[1], parts[count - 1], []
     for step in range(1, count):
         right = lax.ppermute(right, axis, [(i, i + 1) for i in range(step)])
         left = lax.ppermute(left, axis, [(i, i - 1) for i in range(count - step, count)])
+        if beside:
+            right, left, now = lax.optimization_barrier((right, left, beside.pop(0)))
+            ready.append(now)
         if step < count - 1:
             right = parts[step + 1] + right
             left = parts[count - 1 - step] + left
-    return parts[0].astype(F32) + right.astype(F32) + left.astype(F32)
+    return parts[0].astype(F32) + right.astype(F32) + left.astype(F32), ready + beside
 
 
 def upward(block, axis, count, distance=1, first=0):
@@ -625,9 +628,8 @@
         [lax.dynamic_slice_in_dim(g.T, me * local_experts, local_experts, 0) for g in gates],
         axis=1,
     )
-    early = max(1, local_experts // 4)
     results, expert_sums = [], []
-    for first, number in ((0, early), (early, local_experts - early)):
+    for first, number in ((0, local_experts),):
         *results, grads = run_experts(
             me_ref,
             slot_rows,
@@ -645,10 +647,13 @@
         )
         expert_sums.append(lax.psum_scatter(grads, "dp", scatter_dimension=0, tiled=True))
     slot_outs, slot_backs = results[:count], results[count:]
-    back_sum = line_scatter(
-        [dot(places[s], slot_backs[s], 0, 0).astype(BF) for s in range(count)], "expert", count
-    )
     mix_parts = [dot(places[s], slot_outs[s], 0, 0).astype(BF) for s in range(count)]
+    back_sum, (mix_parts, normed_t) = line_scatter(
+        [dot(places[s], slot_backs[s], 0, 0).astype(BF) for s in range(count)],
+        "expert",
+        count,
+        [mix_parts, normed_all.T],
+    )
 
     gate_own = gates[0]
     weighted = (
@@ -672,35 +677,36 @@
     out_stages = slab_stages(out_state, slabs)
     out_halves = next(out_stages)
     query_pre, key_pre, value_pre, *qkv_grads = run_back(
-        me_ref, branch_back, out_full, query, key, value, lse, cos, sin, normed_all.T, slabs
+        me_ref, branch_back, out_full, query, key, value, lse, cos, sin, normed_t, slabs
     )
     qkv_grads, key_pre, value_pre, near, out_halves = lax.optimization_barrier(
         (qkv_grads, key_pre, value_pre, near, out_halves)
     )
-    key_value_part = jnp.concatenate([key_pre, value_pre], axis=1)
-    key_value_sum = [key_value_part[:local_rows]]
-    key_value_came = [
-        downward(key_value_part[s * local_rows : (s + 1) * local_rows], "expert", count, s)
-        for s in range(1, count)
+    key_value_parts = [
+        jnp.concatenate(
+            [x[s * local_rows : (s + 1) * local_rows] for x in (key_pre, value_pre)], axis=1
+        )
+        for s in range(count)
     ]
+    key_value_came = [downward(key_value_parts[s], "expert", count, s) for s in range(1, count)]
+    key_value_sum = [key_value_parts[0]]
     qkv_state = trade(*qkv_grads, 0, slabs)
-    qkv_state, came = lax.optimization_barrier((qkv_state, key_value_came[0]))
-    key_value_sum.append(came)
     qkv_stages = slab_stages(qkv_state, slabs)
     qkv_halves = next(qkv_stages)
-    far, _ = lax.optimization_barrier((mix_parts[2:-1], qkv_state))
-    far = send_far(far, "expert", count)
     for step in range(slabs.bit_length() - 3):
         out_halves = out_stages.send(out_halves)
-        qkv_halves, out_halves, far, came = lax.optimization_barrier(
-            (qkv_halves, out_halves, far, key_value_came[1 + step : 2 + step])
+        at = len(key_value_sum) - 1
+        qkv_halves, out_halves, came = lax.optimization_barrier(
+            (qkv_halves, out_halves, key_value_came[at : at + 2])
         )
         key_value_sum += came
         qkv_halves = qkv_stages.send(qkv_halves)
     left = key_value_came[len(key_value_sum) - 1 :]
+    far, _ = lax.optimization_barrier((mix_parts[2:-1], key_value_sum[-1]))
+    far = send_far(far, "expert", count)
     out_parts = own_parts(*out_halves, me, count)
     out_came = send_parts(out_parts, "expert", count)
-    qkv_halves, left, out_came = lax.optimization_barrier((qkv_halves, left, out_came))
+    qkv_halves, left = lax.optimization_barrier((qkv_halves, left))
     key_value_sum = add_up(key_value_sum + left).astype(BF)
     out_sum = add_up(out_parts[:1] + out_came)
     qkv_parts = own_parts(*qkv_halves, me, count)

time: 586 us -> 577 us (0.985)
  waiting for transfers between devices: 175 us -> 161 us
  local copies, waits for them, and re-layouts: 61.2 us -> 68.4 us
  other arithmetic: 27.3 us -> 34.3 us
    ppermute x6, waiting for transfers between devices: 14.1 us -> 48.9 us  [send_parts(): lax.ppermute(parts[s], axis, [(i, (i + count - s) % count) for i in range...]
    ppermute x1, waiting for transfers between devices: 34.2 us -> 0.01 us  [send_far(): lax.ppermute(part, axis, [(i, (i + count - s) % count) for i in range(cou...]
    ppermute x3, waiting for transfers between devices: 39.4 us -> 13.4 us  [line_scatter(): right = lax.ppermute(right, axis, [(i, i + 1) for i in range(step)])]
    ppermute x3, starting transfers between devices: 6.63 us -> 18.6 us  [line_gather(): lax.ppermute(right[-1], axis, [(i, i + 1) for i in range(step - 1, count...]
    ppermute x3, starting transfers between devices: 23.1 us -> 12.2 us  [line_scatter(): right = lax.ppermute(right, axis, [(i, i + 1) for i in range(step)])]
    ppermute x10, waiting for transfers between devices: 40.1 us -> 50.7 us  [trade(): lax.ppermute(send, 'dp', [(i, i ^ 1 << bit) for i in range(slabs)])]
    pallas_call x2 -> x1, Pallas kernels: 70.6 us -> 64.5 us  [run_experts(): pl.pallas_call(functools.partial(expert_kernel, count, total, experts, fi...]
    unnamed x114 -> x127, local copies, waits for them, and re-layouts: 20.6 us -> 22.3 us
  transfers between devices with their start and end apart: 47 -> 46, of which waited for: 18 -> 20; matrix products, arithmetic and copies ran while one was open for 22% -> 24% of each run, Pallas kernels for 22% -> 13%
where the time goes in v3:
time: 577 us; the launch traced here: 568 us
  waiting for transfers between devices  161 us (28%)
  Pallas kernels  145 us (25%)
  starting transfers between devices  87.4 us (15%)
  local copies, waits for them, and re-layouts  68.4 us (12%)
  matrix products  56.8 us (10%)
  other arithmetic  34.3 us (6%)
  between operations  15.4 us (3%)
    pallas_call x1, Pallas kernels, run_experts(): pl.pallas_call(functools.partial(expert_kernel, count, total, experts, fi...  64.5 us
    dot_general x28, matrix products, dot(): lax.dot_general(a, b, (((ca,), (cb,)), ((), ())), preferred_element_type=...  56.8 us
    ppermute x10, waiting for transfers between devices, trade(): lax.ppermute(send, 'dp', [(i, i ^ 1 << bit) for i in range(slabs)])  50.7 us
    ppermute x6, waiting for transfers between devices, send_parts(): lax.ppermute(parts[s], axis, [(i, (i + count - s) % count) for i in range...  48.9 us
    pallas_call x1, Pallas kernels, run_back(): pl.pallas_call(functools.partial(back_kernel, count), grid_spec=pltpu.Pre...  37.5 us
    pallas_call x1, Pallas kernels, run_front(): pl.pallas_call(functools.partial(front_kernel, count, gain_at), grid_spec...  33.5 us
    optimization_barrier x2, local copies, waits for them, and re-layouts, body(): lax.optimization_barrier((up, down, turned, weights))  26 us
    ppermute x3, waiting for transfers between devices, line_gather(): lax.ppermute(left[-1], axis, [(i, i - 1) for i in range(1, count - step +...  25.8 us
  transfers between devices with their start and end apart: 46, of which 20 were waited for; matrix products, arithmetic and copies ran while one was open for 24% of the time, Pallas kernels for 13%

profile of v3, /device:TPU:0, one launch (start us, length us, event | category | flops | bytes accessed | tf_op | source)
XLA Modules:
  0.0 568.3 jit_solution(9358712818891939276)
XLA Ops:
  9.7 3.1 concatenate.40
  14.9 6.5 %collective-permute-start = (bf16[256,1536]{1,0:T(8,128)(2,1)S(1)}, bf16[256,1536]{1,0:T(8,128)(2,1)}, u32[]{:S(2)}, u32[]{:S(2)}) collective-permute-start(bf16[256,1536]{1,0:T(8,128)(2,1)S(1)} %copy-done.15), channel_id=1, source_target_pairs={{0,1},{1,2},{2,3},{4,5},{5,6},{6,7},{8,9},{9,10},{10,11},{12,13},{... | collective-permute-start | bytes 2359304 | tf_op jit(solution)/shard_map/ppermute | solution.py:320
  21.3 13.3 %copy.197 = bf16[1536,8,512]{2,0,1:T(8,128)(2,1)} copy(bf16[1536,8,512]{2,1,0:T(8,128)(2,1)} %param.22) | data formatting | bytes 25165824 | tf_op args[9]
  34.6 2.6 collective-permute-done.refs_1_
  40.3 13.2 %copy.196 = bf16[1536,8,512]{2,0,1:T(8,128)(2,1)} copy(bf16[1536,8,512]{2,1,0:T(8,128)(2,1)} %param.23) | data formatting | bytes 25165824 | tf_op jit(solution)/shard_map/optimization_barrier | solution.py:566
  53.5 6.2 %collective-permute-done.3 = bf16[256,1664]{0,1:T(8,128)(2,1)S(1)} collective-permute-done((bf16[256,1664]{0,1:T(8,128)(2,1)S(1)}, bf16[256,1664]{0,1:T(8,128)(2,1)S(1)}, u32[]{:S(2)}, u32[]{:S(2)}) %collective-permute-start.3) | collective-permute-done | bytes 852000 | tf_op jit(solution)/shard_map/ppermute | solution.py:325
  67.2 12.8 %copy.195 = bf16[1536,8,512]{2,0,1:T(8,128)(2,1)} copy(bf16[1536,8,512]{2,1,0:T(8,128)(2,1)} %param.24) | data formatting | bytes 25165824 | tf_op jit(solution)/shard_map/optimization_barrier | solution.py:566
  80.0 2.7 collective-permute-done.5
  83.4 5.8 %collective-permute-start.7 = (bf16[256,1664]{0,1:T(8,128)(2,1)S(1)}, bf16[256,1664]{0,1:T(8,128)(2,1)}, u32[]{:S(2)}, u32[]{:S(2)}) collective-permute-start(bf16[256,1664]{0,1:T(8,128)(2,1)S(1)} %maximum_maximum_fusion), channel_id=1, source_target_pairs={{0,2},{1,3},{4,6},{5,7},{8,10},{9,11},{12,14},{13,15},{16,18},{17,... | collective-permute-start | bytes 2555912 | tf_op jit(solution)/shard_map/ppermute | solution.py:320
  89.2 2.4 collective-permute-start.6
  91.8 33.5 %front.1 = (bf16[1024,1536]{1,0:T(8,128)(2,1)}, f32[128,1536]{1,0:T(8,128)}, bf16[256,1536]{1,0:T(8,128)(2,1)}, bf16[1024,512]{1,0:T(8,128)(2,1)}, bf16[1024,512...) custom-call(s32[2]{0:T(128)} %pad_add_fusion.me_ref, bf16[256,1536]{1,0:T(8,128)(2,1)} %refs_0_, ...), custom_call_target="tpu_custom_call" | custom-call | flops 6039797760 | bytes 22806528 | tf_op jit(solution)/shard_map/front/pallas_call | solution.py:121
  126.3 4.1 multiply_reduce_fusion.2
  132.0 4.6 collective-permute-start.8
  142.8 6.7 %collective-permute-done.9 = bf16[256,1536]{1,0:T(8,128)(2,1)S(1)} collective-permute-done((bf16[256,1536]{1,0:T(8,128)(2,1)S(1)}, bf16[256,1536]{1,0:T(8,128)(2,1)S(1)}, u32[]{:S(2)}, u32[]{:S(2)}) %collective-permute-start.9) | collective-permute-done | bytes 786464 | tf_op jit(solution)/shard_map/ppermute | solution.py:298
  150.8 13.3 %collective-permute-start.12 = (bf16[256,1536]{1,0:T(8,128)(2,1)S(1)}, bf16[256,1536]{1,0:T(8,128)(2,1)S(1)}, u32[]{:S(2)}, u32[]{:S(2)}) collective-permute-start(bf16[256,1536]{1,0:T(8,128)(2,1)S(1)} %collective-permute-done.8), channel_id=1, source_target_pairs={{1,2},{2,3},{5,6},{6,7},{9,10},{10,11},{13,14},{14,15},{17,18},{18... | collective-permute-start | bytes 2359304 | tf_op jit(solution)/shard_map/ppermute | solution.py:296
  167.1 2.5 convolution_convert_fusion.3.refs_4_
  169.6 2.5 convolution_convert_fusion.7.refs_0_
  172.2 2.5 convolution_convert_fusion.refs_7_
  174.7 2.4 convolution_convert_fusion.1.refs_6_
  177.1 2.4 convolution_convert_fusion.2.refs_5_
  183.2 2.4 convolution_convert_fusion.5.refs_2_
  185.8 19.1 %collective-permute-done.11 = bf16[256,1536]{1,0:T(8,128)(2,1)S(1)} collective-permute-done((bf16[256,1536]{1,0:T(8,128)(2,1)S(1)}, bf16[256,1536]{1,0:T(8,128)(2,1)S(1)}, u32[]{:S(2)}, u32[]{:S(2)}) %collective-permute-start.11) | collective-permute-done | bytes 786464 | tf_op jit(solution)/shard_map/ppermute | solution.py:298
  211.8 3.8 convolution_convert_fusion.4.refs_3_
  215.6 2.5 convolution_convert_fusion.6.refs_1_
  218.1 64.5 %experts.1 = (bf16[896,1536]{1,0:T(8,128)(2,1)}, bf16[896,1536]{1,0:T(8,128)(2,1)}, bf16[896,1536]{1,0:T(8,128)(2,1)}, bf16[896,1536]{1,0:T(8,128)(2,1)}, bf16[8...) custom-call(s32[2]{0:T(128)} %pad_add_fusion.me_ref, ...), custom_call_target="tpu_custom_call" | custom-call | flops 50734301184 | bytes 119537664 | tf_op jit(solution)/shard_map/experts/pallas_call | solution.py:455
  283.6 3.2 convolution_convert_fusion.14
  301.7 4.1 collective-permute-done.15
  308.7 5.1 collective-permute-start.17
  313.8 5.0 copy.175
  318.8 8.1 %collective-permute-done.17 = bf16[256,1664]{1,0:T(8,128)(2,1)} collective-permute-done((bf16[256,1664]{1,0:T(8,128)(2,1)}, bf16[256,1664]{1,0:T(8,128)(2,1)}, u32[]{:S(2)}, u32[]{:S(2)}) %collective-permute-start.17) | collective-permute-done | bytes 852000 | tf_op jit(solution)/shard_map/ppermute | solution.py:307
  331.7 5.3 collective-permute-start.19
  338.2 10.5 %collective-permute-done.20 = bf16[256,1664]{1,0:T(8,128)(2,1)S(1)} collective-permute-done((bf16[256,1664]{1,0:T(8,128)(2,1)S(1)}, bf16[256,1664]{1,0:T(8,128)(2,1)S(1)}, u32[]{:S(2)}, u32[]{:S(2)}) %collective-permute-start.20) | collective-permute-done | bytes 852000 | tf_op jit(solution)/shard_map/ppermute | solution.py:308
  353.9 4.4 out_grad.1
  358.3 5.0 collective-permute-done.21
  366.3 5.3 collective-permute-start.22
  371.6 37.5 %back.1 = (bf16[256,1536]{1,0:T(8,128)(2,1)}, bf16[1024,512]{1,0:T(8,128)(2,1)}, bf16[1024,512]{1,0:T(8,128)(2,1)}, bf16[4,192,2560]{2,1,0:T(8,128)(2,1)}, bf16[4,192,2560]{2,1,0:T(8,128)(2,1)}) custom-call(s32[2]{0:T(128)} %pad_add_fusion.me_ref, bf16[256,1536]{1,0:T(8,128)(2,1)} %copy-done.1, bf16[1536,1536]{1,0:T(8,128)(2,1)} %all-gather.5.cloned.1.call-done.refs_1_, ...), custom_call_target="tpu_custom_call" | custom-call | flops 9663676416 | bytes 12582912 | tf_op jit(solution)/shard_map/back/pallas_call | solution.py:249
  411.5 5.2 fusion
  423.7 3.4 add.273
  429.3 4.7 collective-permute-done.30
  437.0 39.0 %collective-permute-done.27 = bf16[2,96,2560]{2,1,0:T(8,128)(2,1)S(1)} collective-permute-done((bf16[2,96,2560]{2,1,0:T(8,128)(2,1)S(1)}, bf16[2,96,2560]{2,1,0:T(8,128)(2,1)S(1)}, u32[]{:S(2)}, u32[]{:S(2)}) %collective-permute-start.27) | collective-permute-done | bytes 983072 | tf_op jit(solution)/shard_map/ppermute | solution.py:358
  478.1 3.7 collective-permute-start.40
  487.3 3.3 collective-permute-done.42
  491.5 21.4 %collective-permute-done.41 = bf16[48,1664]{1,0:T(8,128)(2,1)S(1)} collective-permute-done((bf16[48,1664]{1,0:T(8,128)(2,1)S(1)}, bf16[48,1664]{1,0:T(8,128)(2,1)S(1)}, u32[]{:S(2)}, u32[]{:S(2)}) %collective-permute-start.41) | collective-permute-done | bytes 159776 | tf_op jit(solution)/shard_map/ppermute | solution.py:330
  522.1 3.5 fusion.11
  526.9 8.3 %collective-permute-done.37 = bf16[48,2560]{1,0:T(8,128)(2,1)S(1)} collective-permute-done((bf16[48,2560]{1,0:T(8,128)(2,1)S(1)}, bf16[48,2560]{1,0:T(8,128)(2,1)S(1)}, u32[]{:S(2)}, u32[]{:S(2)}) %collective-permute-start.37) | collective-permute-done | bytes 245792 | tf_op jit(solution)/shard_map/ppermute | solution.py:330
  535.2 14.4 %collective-permute-done.38 = bf16[48,2560]{1,0:T(8,128)(2,1)S(1)} collective-permute-done((bf16[48,2560]{1,0:T(8,128)(2,1)S(1)}, bf16[48,2560]{1,0:T(8,128)(2,1)S(1)}, u32[]{:S(2)}, u32[]{:S(2)}) %collective-permute-start.38) | collective-permute-done | bytes 245792 | tf_op jit(solution)/shard_map/ppermute | solution.py:330
  551.3 3.0 add_convert_fusion
  556.6 4.9 owned.1
  (311 shorter events, 109.2 us)
Async XLA Ops:
  7.2 75.4 %all-gather.3.cloned.1.call-start = ((), (), s32[]{:S(2)}) async-start(), calls=%async_computation.1 | async-start | bytes 9289728 | tf_op jit(solution)/shard_map/all_gather | solution.py:549
  12.8 113.4 %all-gather.5.cloned.1.call-start = ((), (), s32[]{:S(2)}) async-start(), calls=%async_computation.2 | async-start | bytes 5308416 | tf_op jit(solution)/shard_map/all_gather | solution.py:573
  13.6 23.9 %collective-permute-start.1 = (bf16[256,1664]{0,1:T(8,128)(2,1)S(1)}, bf16[256,1664]{0,1:T(8,128)(2,1)S(1)}, u32[]{:S(2)}, u32[]{:S(2)}) collective-permute-start(bf16[256,1664]{0,1:T(8,128)(2,1)S(1)} %maximum_maximum_fusion), channel_id=1, source_target_pairs={{1,0},{2,1},{3,2},{5,4},{6,5},{7,6},{9,8},{10,9},{11,10},{13,12},{... | collective-permute-start | bytes 2555912 | tf_op jit(solution)/shard_map/ppermute | solution.py:325
  14.9 22.3 %collective-permute-start = (bf16[256,1536]{1,0:T(8,128)(2,1)S(1)}, bf16[256,1536]{1,0:T(8,128)(2,1)}, u32[]{:S(2)}, u32[]{:S(2)}) collective-permute-start(bf16[256,1536]{1,0:T(8,128)(2,1)S(1)} %copy-done.15), channel_id=1, source_target_pairs={{0,1},{1,2},{2,3},{4,5},{5,6},{6,7},{8,9},{9,10},{10,11},{12,13},{... | collective-permute-start | bytes 2359304 | tf_op jit(solution)/shard_map/ppermute | solution.py:320
  37.4 22.3 %collective-permute-start.3 = (bf16[256,1664]{0,1:T(8,128)(2,1)S(1)}, bf16[256,1664]{0,1:T(8,128)(2,1)S(1)}, u32[]{:S(2)}, u32[]{:S(2)}) collective-permute-start(bf16[256,1664]{0,1:T(8,128)(2,1)S(1)} %collective-permute-done.1), channel_id=1, source_target_pairs={{1,0},{2,1},{5,4},{6,5},{9,8},{10,9},{13,12},{14,13},{17,16},{18,1... | collective-permute-start | bytes 2555912 | tf_op jit(solution)/shard_map/ppermute | solution.py:325
  38.7 14.8 %collective-permute-start.2 = (bf16[256,1536]{1,0:T(8,128)(2,1)}, bf16[256,1536]{1,0:T(8,128)(2,1)}, u32[]{:S(2)}, u32[]{:S(2)}) collective-permute-start(bf16[256,1536]{1,0:T(8,128)(2,1)} %collective-permute-done.refs_1_), channel_id=1, source_target_pairs={{1,2},{2,3},{5,6},{6,7},{9,10},{10,11},{13,14},{14,15},{17,18},{18... | collective-permute-start | bytes 2359304 | tf_op jit(solution)/shard_map/ppermute | solution.py:320
  59.8 20.2 %collective-permute-start.4 = (bf16[256,1536]{1,0:T(8,128)(2,1)}, bf16[256,1536]{1,0:T(8,128)(2,1)}, u32[]{:S(2)}, u32[]{:S(2)}) collective-permute-start(bf16[256,1536]{1,0:T(8,128)(2,1)} %collective-permute-done.2.refs_2_), channel_id=1, source_target_pairs={{2,3},{6,7},{10,11},{14,15},{18,19},{22,23},{26,27},{30,31}} | collective-permute-start | bytes 2359304 | tf_op jit(solution)/shard_map/ppermute | solution.py:320
  61.4 21.3 %collective-permute-start.5 = (bf16[256,1664]{0,1:T(8,128)(2,1)S(1)}, bf16[256,1664]{0,1:T(8,128)(2,1)}, u32[]{:S(2)}, u32[]{:S(2)}) collective-permute-start(bf16[256,1664]{0,1:T(8,128)(2,1)S(1)} %collective-permute-done.3), channel_id=1, source_target_pairs={{1,0},{5,4},{9,8},{13,12},{17,16},{21,20},{25,24},{29,28}} | collective-permute-start | bytes 2555912 | tf_op jit(solution)/shard_map/ppermute | solution.py:325
  82.6 471.6 %reduce-scatter.2.cloned.1.call-start = ((), (), s32[]{:S(2)}) async-start(), calls=%async_computation.3 | async-start | bytes 42467328 | tf_op jit(solution)/shard_map/reduce_scatter | solution.py:648
  83.4 53.2 %collective-permute-start.7 = (bf16[256,1664]{0,1:T(8,128)(2,1)S(1)}, bf16[256,1664]{0,1:T(8,128)(2,1)}, u32[]{:S(2)}, u32[]{:S(2)}) collective-permute-start(bf16[256,1664]{0,1:T(8,128)(2,1)S(1)} %maximum_maximum_fusion), channel_id=1, source_target_pairs={{0,2},{1,3},{4,6},{5,7},{8,10},{9,11},{12,14},{13,15},{16,18},{17,... | collective-permute-start | bytes 2555912 | tf_op jit(solution)/shard_map/ppermute | solution.py:320
  89.2 47.5 %collective-permute-start.6 = (bf16[256,1664]{0,1:T(8,128)(2,1)S(1)}, bf16[256,1664]{0,1:T(8,128)(2,1)}, u32[]{:S(2)}, u32[]{:S(2)}) collective-permute-start(bf16[256,1664]{0,1:T(8,128)(2,1)S(1)} %maximum_maximum_fusion), channel_id=1, source_target_pairs={{0,1},{1,2},{2,3},{4,5},{5,6},{6,7},{8,9},{9,10},{10,11},{12,13},{... | collective-permute-start | bytes 2555912 | tf_op jit(solution)/shard_map/ppermute | solution.py:320
  130.6 18.9 %collective-permute-start.9 = (bf16[256,1536]{1,0:T(8,128)(2,1)S(1)}, bf16[256,1536]{1,0:T(8,128)(2,1)S(1)}, u32[]{:S(2)}, u32[]{:S(2)}) collective-permute-start(bf16[256,1536]{1,0:T(8,128)(2,1)S(1)} %multiply_convert_fusion.1.normed_ref), channel_id=1, source_target_pairs={{1,0},{2,1},{3,2},{5,4},{6,5},{7,6},{9,8},{10,9},{11,10},{13,12},{... | collective-permute-start | bytes 2359304 | tf_op jit(solution)/shard_map/ppermute | solution.py:298
  132.0 18.7 %collective-permute-start.8 = (bf16[256,1536]{1,0:T(8,128)(2,1)S(1)}, bf16[256,1536]{1,0:T(8,128)(2,1)S(1)}, u32[]{:S(2)}, u32[]{:S(2)}) collective-permute-start(bf16[256,1536]{1,0:T(8,128)(2,1)S(1)} %multiply_convert_fusion.1.normed_ref), channel_id=1, source_target_pairs={{0,1},{1,2},{2,3},{4,5},{5,6},{6,7},{8,9},{9,10},{10,11},{12,13},{... | collective-permute-start | bytes 2359304 | tf_op jit(solution)/shard_map/ppermute | solution.py:296
  138.3 25.8 %collective-permute-start.13 = (bf16[256,1664]{0,1:T(8,128)(2,1)}, bf16[256,1664]{0,1:T(8,128)(2,1)S(1)}, u32[]{:S(2)}, u32[]{:S(2)}) collective-permute-start(bf16[256,1664]{0,1:T(8,128)(2,1)} %collective-permute-done.7), channel_id=1, source_target_pairs={{2,3},{6,7},{10,11},{14,15},{18,19},{22,23},{26,27},{30,31}} | collective-permute-start | bytes 2555912 | tf_op jit(solution)/shard_map/ppermute | solution.py:320
  149.5 57.6 %copy-start.8 = (bf16[256,1536]{1,0:T(8,128)(2,1)}, bf16[256,1536]{1,0:T(8,128)(2,1)S(1)}, u32[]{:S(2)}) copy-start(bf16[256,1536]{1,0:T(8,128)(2,1)S(1)} %collective-permute-done.9) | copy-start | bytes 2359300
  149.5 30.1 %collective-permute-start.10 = (bf16[256,1536]{1,0:T(8,128)(2,1)S(1)}, bf16[256,1536]{1,0:T(8,128)(2,1)S(1)}, u32[]{:S(2)}, u32[]{:S(2)}) collective-permute-start(bf16[256,1536]{1,0:T(8,128)(2,1)S(1)} %collective-permute-done.9), channel_id=1, source_target_pairs={{1,0},{2,1},{5,4},{6,5},{9,8},{10,9},{13,12},{14,13},{17,16},{18,1... | collective-permute-start | bytes 2359304 | tf_op jit(solution)/shard_map/ppermute | solution.py:298
  150.8 54.2 %copy-start.10 = (bf16[256,1536]{1,0:T(8,128)(2,1)}, bf16[256,1536]{1,0:T(8,128)(2,1)S(1)}, u32[]{:S(2)}) copy-start(bf16[256,1536]{1,0:T(8,128)(2,1)S(1)} %collective-permute-done.8) | copy-start | bytes 2359300
  150.8 30.1 %collective-permute-start.12 = (bf16[256,1536]{1,0:T(8,128)(2,1)S(1)}, bf16[256,1536]{1,0:T(8,128)(2,1)S(1)}, u32[]{:S(2)}, u32[]{:S(2)}) collective-permute-start(bf16[256,1536]{1,0:T(8,128)(2,1)S(1)} %collective-permute-done.8), channel_id=1, source_target_pairs={{1,2},{2,3},{5,6},{6,7},{9,10},{10,11},{13,14},{14,15},{17,18},{18... | collective-permute-start | bytes 2359304 | tf_op jit(solution)/shard_map/ppermute | solution.py:296
  179.5 25.4 %collective-permute-start.11 = (bf16[256,1536]{1,0:T(8,128)(2,1)S(1)}, bf16[256,1536]{1,0:T(8,128)(2,1)S(1)}, u32[]{:S(2)}, u32[]{:S(2)}) collective-permute-start(bf16[256,1536]{1,0:T(8,128)(2,1)S(1)} %collective-permute-done.10), channel_id=1, source_target_pairs={{1,0},{5,4},{9,8},{13,12},{17,16},{21,20},{25,24},{29,28}} | collective-permute-start | bytes 2359304 | tf_op jit(solution)/shard_map/ppermute | solution.py:298
  180.8 26.2 %collective-permute-start.14 = (bf16[256,1536]{1,0:T(8,128)(2,1)S(1)}, bf16[256,1536]{1,0:T(8,128)(2,1)S(1)}, u32[]{:S(2)}, u32[]{:S(2)}) collective-permute-start(bf16[256,1536]{1,0:T(8,128)(2,1)S(1)} %collective-permute-done.12), channel_id=1, source_target_pairs={{2,3},{6,7},{10,11},{14,15},{18,19},{22,23},{26,27},{30,31}} | collective-permute-start | bytes 2359304 | tf_op jit(solution)/shard_map/ppermute | solution.py:296
  286.8 14.9 %collective-permute-start.16 = (bf16[256,1664]{1,0:T(8,128)(2,1)S(1)}, bf16[256,1664]{1,0:T(8,128)(2,1)S(1)}, u32[]{:S(2)}, u32[]{:S(2)}) collective-permute-start(bf16[256,1664]{1,0:T(8,128)(2,1)S(1)} %convolution_convert_fusion.14), channel_id=1, source_target_pairs={{3,2},{7,6},{11,10},{15,14},{19,18},{23,22},{27,26},{31,30}} | collective-permute-start | bytes 2555912 | tf_op jit(solution)/shard_map/ppermute | solution.py:308
  289.2 16.6 %collective-permute-start.15 = (bf16[256,1664]{1,0:T(8,128)(2,1)S(1)}, bf16[256,1664]{1,0:T(8,128)(2,1)S(1)}, u32[]{:S(2)}, u32[]{:S(2)}) collective-permute-start(bf16[256,1664]{1,0:T(8,128)(2,1)S(1)} %convolution_convert_fusion.15), channel_id=1, source_target_pairs={{0,1},{4,5},{8,9},{12,13},{16,17},{20,21},{24,25},{28,29}} | collective-permute-start | bytes 2555912 | tf_op jit(solution)/shard_map/ppermute | solution.py:307
  307.2 11.6 %collective-permute-start.18 = (bf16[256,1664]{1,0:T(8,128)(2,1)}, bf16[256,1664]{1,0:T(8,128)(2,1)}, u32[]{:S(2)}, u32[]{:S(2)}) collective-permute-start(bf16[256,1664]{1,0:T(8,128)(2,1)} %get-tuple-element.299), channel_id=1, source_target_pairs={{2,1},{3,2},{6,5},{7,6},{10,9},{11,10},{14,13},{15,14},{18,17},{19... | collective-permute-start | bytes 2555912 | tf_op jit(solution)/shard_map/ppermute | solution.py:308
  308.7 18.2 %collective-permute-start.17 = (bf16[256,1664]{1,0:T(8,128)(2,1)}, bf16[256,1664]{1,0:T(8,128)(2,1)}, u32[]{:S(2)}, u32[]{:S(2)}) collective-permute-start(bf16[256,1664]{1,0:T(8,128)(2,1)} %get-tuple-element.300), channel_id=1, source_target_pairs={{0,1},{1,2},{4,5},{5,6},{8,9},{9,10},{12,13},{13,14},{16,17},{17,1... | collective-permute-start | bytes 2555912 | tf_op jit(solution)/shard_map/ppermute | solution.py:307
  330.4 18.3 %collective-permute-start.20 = (bf16[256,1664]{1,0:T(8,128)(2,1)S(1)}, bf16[256,1664]{1,0:T(8,128)(2,1)S(1)}, u32[]{:S(2)}, u32[]{:S(2)}) collective-permute-start(bf16[256,1664]{1,0:T(8,128)(2,1)S(1)} %add.263), channel_id=1, source_target_pairs={{1,0},{2,1},{3,2},{5,4},{6,5},{7,6},{9,8},{10,9},{11,10},{13,12},{... | collective-permute-start | bytes 2555912 | tf_op jit(solution)/shard_map/ppermute | solution.py:308
  331.7 18.2 %collective-permute-start.19 = (bf16[256,1664]{1,0:T(8,128)(2,1)S(1)}, bf16[256,1664]{1,0:T(8,128)(2,1)S(1)}, u32[]{:S(2)}, u32[]{:S(2)}) collective-permute-start(bf16[256,1664]{1,0:T(8,128)(2,1)S(1)} %add.261), channel_id=1, source_target_pairs={{0,1},{1,2},{2,3},{4,5},{5,6},{6,7},{8,9},{9,10},{10,11},{12,13},{... | collective-permute-start | bytes 2555912 | tf_op jit(solution)/shard_map/ppermute | solution.py:307
  358.3 5.0 collective-permute-start.21
  364.0 45.2 %collective-permute-start.25 = (bf16[2,96,1664]{2,1,0:T(8,128)(2,1)S(1)}, bf16[2,96,1664]{2,1,0:T(8,128)(2,1)S(1)}, u32[]{:S(2)}, u32[]{:S(2)}) collective-permute-start(bf16[2,96,1664]{2,1,0:T(8,128)(2,1)S(1)} %slice_bitcast_fusion.4), channel_id=1, source_target_pairs={{0,16},{4,20},{8,24},{12,28},{16,0},{20,4},{24,8},{28,12},{1,17},{... | collective-permute-start | bytes 1916936 | tf_op jit(solution)/shard_map/ppermute | solution.py:358
  365.3 43.9 %collective-permute-start.24 = (bf16[2,96,1664]{2,1,0:T(8,128)(2,1)S(1)}, bf16[2,96,1664]{2,1,0:T(8,128)(2,1)S(1)}, u32[]{:S(2)}, u32[]{:S(2)}) collective-permute-start(bf16[2,96,1664]{2,1,0:T(8,128)(2,1)S(1)} %slice_bitcast_fusion.6), channel_id=1, source_target_pairs={{0,8},{4,12},{8,0},{12,4},{16,24},{20,28},{24,16},{28,20},{1,9},{5... | collective-permute-start | bytes 1916936 | tf_op jit(solution)/shard_map/ppermute | solution.py:358
  366.3 43.0 %collective-permute-start.22 = (bf16[256,1536]{1,0:T(8,128)(2,1)}, bf16[256,1536]{1,0:T(8,128)(2,1)}, u32[]{:S(2)}, u32[]{:S(2)}) collective-permute-start(bf16[256,1536]{1,0:T(8,128)(2,1)} %convolution_convert_fusion.10), channel_id=1, source_target_pairs={{0,3},{1,0},{2,1},{3,2},{4,7},{5,4},{6,5},{7,6},{8,11},{9,8},{10,9... | collective-permute-start | bytes 2359304 | tf_op jit(solution)/shard_map/ppermute | solution.py:338
  371.6 37.7 %collective-permute-start.23 = (bf16[256,1536]{1,0:T(8,128)(2,1)}, bf16[256,1536]{1,0:T(8,128)(2,1)}, u32[]{:S(2)}, u32[]{:S(2)}) collective-permute-start(bf16[256,1536]{1,0:T(8,128)(2,1)} %convolution_convert_fusion.8), channel_id=1, source_target_pairs={{0,1},{1,2},{2,3},{3,0},{4,5},{5,6},{6,7},{7,4},{8,9},{9,10},{10,1... | collective-permute-start | bytes 2359304 | tf_op jit(solution)/shard_map/ppermute | solution.py:338
  409.3 14.4 %collective-permute-start.26 = (bf16[4,192,2560]{2,1,0:T(8,128)(2,1)}, bf16[4,192,2560]{2,1,0:T(8,128)(2,1)}, u32[]{:S(2)}, u32[]{:S(2)}) collective-permute-start(bf16[4,192,2560]{2,1,0:T(8,128)(2,1)} %get-tuple-element.174), channel_id=1, source_target_pairs={{0,4},{4,0},{8,12},{12,8},{16,20},{20,16},{24,28},{28,24},{1,5},{5... | collective-permute-start | bytes 11796488 | tf_op jit(solution)/shard_map/ppermute | solution.py:358
  416.7 17.3 %collective-permute-start.30 = (bf16[96,1664]{1,0:T(8,128)(2,1)S(1)}, bf16[96,1664]{1,0:T(8,128)(2,1)S(1)}, u32[]{:S(2)}, u32[]{:S(2)}) collective-permute-start(bf16[96,1664]{1,0:T(8,128)(2,1)S(1)} %slice_bitcast_fusion.10), channel_id=1, source_target_pairs={{0,8},{4,12},{8,0},{12,4},{16,24},{20,28},{24,16},{28,20},{1,9},{5... | collective-permute-start | bytes 958472 | tf_op jit(solution)/shard_map/ppermute | solution.py:358
  418.4 17.3 %collective-permute-start.29 = (bf16[96,1664]{1,0:T(8,128)(2,1)S(1)}, bf16[96,1664]{1,0:T(8,128)(2,1)S(1)}, u32[]{:S(2)}, u32[]{:S(2)}) collective-permute-start(bf16[96,1664]{1,0:T(8,128)(2,1)S(1)} %slice_bitcast_fusion.11), channel_id=1, source_target_pairs={{0,16},{4,20},{8,24},{12,28},{16,0},{20,4},{24,8},{28,12},{1,17},{... | collective-permute-start | bytes 958472 | tf_op jit(solution)/shard_map/ppermute | solution.py:358
  421.2 56.7 %collective-permute-start.31 = (bf16[256,1024]{1,0:T(8,128)(2,1)S(1)}, bf16[256,1024]{1,0:T(8,128)(2,1)S(1)}, u32[]{:S(2)}, u32[]{:S(2)}) collective-permute-start(bf16[256,1024]{1,0:T(8,128)(2,1)S(1)} %pad_maximum_fusion.3), channel_id=1, source_target_pairs={{1,0},{2,1},{3,2},{5,4},{6,5},{7,6},{9,8},{10,9},{11,10},{13,12},{... | collective-permute-start | bytes 1572872 | tf_op jit(solution)/shard_map/ppermute | solution.py:325
  427.2 48.8 %collective-permute-start.27 = (bf16[2,96,2560]{2,1,0:T(8,128)(2,1)S(1)}, bf16[2,96,2560]{2,1,0:T(8,128)(2,1)S(1)}, u32[]{:S(2)}, u32[]{:S(2)}) collective-permute-start(bf16[2,96,2560]{2,1,0:T(8,128)(2,1)S(1)} %slice_bitcast_fusion.2), channel_id=1, source_target_pairs={{0,8},{4,12},{8,0},{12,4},{16,24},{20,28},{24,16},{28,20},{1,9},{5... | collective-permute-start | bytes 2949128 | tf_op jit(solution)/shard_map/ppermute | solution.py:358
  429.0 48.7 %collective-permute-start.28 = (bf16[2,96,2560]{2,1,0:T(8,128)(2,1)S(1)}, bf16[2,96,2560]{2,1,0:T(8,128)(2,1)S(1)}, u32[]{:S(2)}, u32[]{:S(2)}) collective-permute-start(bf16[2,96,2560]{2,1,0:T(8,128)(2,1)S(1)} %slice_bitcast_fusion), channel_id=1, source_target_pairs={{0,16},{4,20},{8,24},{12,28},{16,0},{20,4},{24,8},{28,12},{1,17},{... | collective-permute-start | bytes 2949128 | tf_op jit(solution)/shard_map/ppermute | solution.py:358
  434.0 43.9 %collective-permute-start.32 = (bf16[256,1024]{1,0:T(8,128)(2,1)S(1)}, bf16[256,1024]{1,0:T(8,128)(2,1)S(1)}, u32[]{:S(2)}, u32[]{:S(2)}) collective-permute-start(bf16[256,1024]{1,0:T(8,128)(2,1)S(1)} %pad_maximum_fusion.4), channel_id=1, source_target_pairs={{2,0},{3,1},{6,4},{7,5},{10,8},{11,9},{14,12},{15,13},{18,16},{19,... | collective-permute-start | bytes 1572872 | tf_op jit(solution)/shard_map/ppermute | solution.py:325
  435.7 84.1 %collective-permute-start.36 = (bf16[256,1024]{1,0:T(8,128)(2,1)}, bf16[256,1024]{1,0:T(8,128)(2,1)}, u32[]{:S(2)}, u32[]{:S(2)}) collective-permute-start(bf16[256,1024]{1,0:T(8,128)(2,1)} %pad_maximum_fusion.5), channel_id=1, source_target_pairs={{3,0},{7,4},{11,8},{15,12},{19,16},{23,20},{27,24},{31,28}} | collective-permute-start | bytes 1572872 | tf_op jit(solution)/shard_map/ppermute | solution.py:325
  478.1 8.2 %collective-permute-start.40 = (bf16[48,1664]{1,0:T(8,128)(2,1)S(1)}, bf16[48,1664]{1,0:T(8,128)(2,1)S(1)}, u32[]{:S(2)}, u32[]{:S(2)}) collective-permute-start(bf16[48,1664]{1,0:T(8,128)(2,1)S(1)} %get-tuple-element.309), channel_id=1, source_target_pairs={{0,3},{1,0},{2,1},{3,2},{4,7},{5,4},{6,5},{7,6},{8,11},{9,8},{10,9... | collective-permute-start | bytes 479240 | tf_op jit(solution)/shard_map/ppermute | solution.py:330
  481.7 8.9 %collective-permute-start.42 = (bf16[48,1664]{1,0:T(8,128)(2,1)S(1)}, bf16[48,1664]{1,0:T(8,128)(2,1)S(1)}, u32[]{:S(2)}, u32[]{:S(2)}) collective-permute-start(bf16[48,1664]{1,0:T(8,128)(2,1)S(1)} %get-tuple-element.310), channel_id=1, source_target_pairs={{0,1},{1,2},{2,3},{3,0},{4,5},{5,6},{6,7},{7,4},{8,9},{9,10},{10,1... | collective-permute-start | bytes 479240 | tf_op jit(solution)/shard_map/ppermute | solution.py:330
  481.7 31.2 %collective-permute-start.41 = (bf16[48,1664]{1,0:T(8,128)(2,1)S(1)}, bf16[48,1664]{1,0:T(8,128)(2,1)S(1)}, u32[]{:S(2)}, u32[]{:S(2)}) collective-permute-start(bf16[48,1664]{1,0:T(8,128)(2,1)S(1)} %get-tuple-element.311), channel_id=1, source_target_pairs={{0,2},{1,3},{2,0},{3,1},{4,6},{5,7},{6,4},{7,5},{8,10},{9,11},{10,... | collective-permute-start | bytes 479240 | tf_op jit(solution)/shard_map/ppermute | solution.py:330
  484.0 33.3 %collective-permute-start.35 = (bf16[96,2560]{1,0:T(8,128)(2,1)}, bf16[96,2560]{1,0:T(8,128)(2,1)}, u32[]{:S(2)}, u32[]{:S(2)}) collective-permute-start(bf16[96,2560]{1,0:T(8,128)(2,1)} %slice_bitcast_fusion.8), channel_id=1, source_target_pairs={{0,8},{4,12},{8,0},{12,4},{16,24},{20,28},{24,16},{28,20},{1,9},{5... | collective-permute-start | bytes 1474568 | tf_op jit(solution)/shard_map/ppermute | solution.py:358
  486.3 32.2 %collective-permute-start.34 = (bf16[96,2560]{1,0:T(8,128)(2,1)}, bf16[96,2560]{1,0:T(8,128)(2,1)}, u32[]{:S(2)}, u32[]{:S(2)}) collective-permute-start(bf16[96,2560]{1,0:T(8,128)(2,1)} %slice_bitcast_fusion.9), channel_id=1, source_target_pairs={{0,16},{4,20},{8,24},{12,28},{16,0},{20,4},{24,8},{28,12},{1,17},{... | collective-permute-start | bytes 1474568 | tf_op jit(solution)/shard_map/ppermute | solution.py:358
  490.6 60.2 %collective-permute-start.33 = (bf16[256,1536]{1,0:T(8,128)(2,1)}, bf16[256,1536]{1,0:T(8,128)(2,1)}, u32[]{:S(2)}, u32[]{:S(2)}) collective-permute-start(bf16[256,1536]{1,0:T(8,128)(2,1)} %convolution_convert_fusion.9), channel_id=1, source_target_pairs={{0,2},{1,3},{2,0},{3,1},{4,6},{5,7},{6,4},{7,5},{8,10},{9,11},{10,... | collective-permute-start | bytes 2359304 | tf_op jit(solution)/shard_map/ppermute | solution.py:345
  519.9 15.3 %collective-permute-start.37 = (bf16[48,2560]{1,0:T(8,128)(2,1)S(1)}, bf16[48,2560]{1,0:T(8,128)(2,1)S(1)}, u32[]{:S(2)}, u32[]{:S(2)}) collective-permute-start(bf16[48,2560]{1,0:T(8,128)(2,1)S(1)} %get-tuple-element.296), channel_id=1, source_target_pairs={{0,3},{1,0},{2,1},{3,2},{4,7},{5,4},{6,5},{7,6},{8,11},{9,8},{10,9... | collective-permute-start | bytes 737288 | tf_op jit(solution)/shard_map/ppermute | solution.py:330
  521.1 14.1 %collective-permute-start.39 = (bf16[48,2560]{1,0:T(8,128)(2,1)S(1)}, bf16[48,2560]{1,0:T(8,128)(2,1)S(1)}, u32[]{:S(2)}, u32[]{:S(2)}) collective-permute-start(bf16[48,2560]{1,0:T(8,128)(2,1)S(1)} %get-tuple-element.297), channel_id=1, source_target_pairs={{0,1},{1,2},{2,3},{3,0},{4,5},{5,6},{6,7},{7,4},{8,9},{9,10},{10,1... | collective-permute-start | bytes 737288 | tf_op jit(solution)/shard_map/ppermute | solution.py:330
  522.0 27.6 %collective-permute-start.38 = (bf16[48,2560]{1,0:T(8,128)(2,1)S(1)}, bf16[48,2560]{1,0:T(8,128)(2,1)S(1)}, u32[]{:S(2)}, u32[]{:S(2)}) collective-permute-start(bf16[48,2560]{1,0:T(8,128)(2,1)S(1)} %get-tuple-element.298), channel_id=1, source_target_pairs={{0,2},{1,3},{2,0},{3,1},{4,6},{5,7},{6,4},{7,5},{8,10},{9,11},{10,... | collective-permute-start | bytes 737288 | tf_op jit(solution)/shard_map/ppermute | solution.py:330
  (57 other events, 446.2 us)
Sparse Core Ops, SparseCore 0:
  13.0 56.5 all-gather.2
  82.8 39.3 all-gather.4
  282.8 267.8 reduce-scatter.1

commit v4 on v3

--- a/solution.py
+++ b/solution.py
@@ -76,7 +76,7 @@
 def front_kernel(count, gain_at, me_ref, *refs):
     token_refs = refs[:count]
     wq_ref, wk_ref, wv_ref, side_ref, cos_ref, sin_ref = refs[count : count + 6]
-    normed_ref, side_out, q_ref, k_ref, v_ref, att_ref, lse_ref, bias_ref = refs[count + 6 :]
+    normed_ref, side_out, q_ref, k_ref, v_ref, att_ref, probs_ref, bias_ref = refs[count + 6 :]
     rows = token_refs[0].shape[0]
 
     @pl.when(pl.program_id(0) == 0)
@@ -98,7 +98,6 @@
     value = both[:, PAIR:].astype(BF)
     k_ref[...] = key
     v_ref[...] = value
-    lse_ref[...] = jnp.zeros_like(lse_ref)
     for head in range(2 * GROUP):
         at = slice(head * HEAD_DIM, (head + 1) * HEAD_DIM)
         kv_at = slice(head // GROUP * HEAD_DIM, (head // GROUP + 1) * HEAD_DIM)
@@ -108,7 +107,7 @@
         total = jnp.sum(weight, axis=1, keepdims=True)
         probs = (weight * (1.0 / total)).astype(BF)
         att_ref[:, at] = dot(probs, value[:, kv_at]).astype(BF)
-        lse_ref[:, head : head + 1] = peak + jnp.log(total)
+        probs_ref[head * rows : (head + 1) * rows] = probs
 
 
 def run_front(me, tokens, full, cos, sin, query_width, key_width, gain_at):
@@ -141,7 +140,7 @@
                 column(length, PAIR, 0),
                 column(length, PAIR, 0),
                 column(rows, wide, 0),
-                column(rows, PAIR, 0),
+                pl.BlockSpec((2 * GROUP * rows, length), lambda p, i: (p, 0)),
             ],
             scratch_shapes=[pltpu.VMEM((rows, length), F32)],
         ),
@@ -152,7 +151,7 @@
             jax.ShapeDtypeStruct((length, key_width), BF),
             jax.ShapeDtypeStruct((length, key_width), BF),
             jax.ShapeDtypeStruct((rows, query_width), BF),
-            jax.ShapeDtypeStruct((rows, pairs * PAIR), F32),
+            jax.ShapeDtypeStruct((pairs * 2 * GROUP * rows, length), BF),
         ],
         compiler_params=pltpu.CompilerParams(
             dimension_semantics=("arbitrary",), vmem_limit_bytes=56 * 2**20
@@ -167,28 +166,23 @@
 
 
 def back_kernel(count, me_ref, *refs):
-    branch_ref, wo_ref, q_ref, k_ref, v_ref, lse_ref, cos_ref, sin_ref, normed_ref = refs[:9]
-    dq_ref, dk_ref, dv_ref, keep_ref, send_ref, bias_ref = refs[9:]
+    branch_ref, wo_ref, q_ref, k_ref, v_ref, probs_ref, cos_ref, sin_ref, normed_ref = refs[:9]
+    dq_ref, dk_ref, dv_ref, keep_ref, send_ref = refs[9:]
     rows = branch_ref.shape[0]
-
-    @pl.when(pl.program_id(0) == 0)
-    def _():
-        bias_ref[...] = causal_bias(me_ref[0], count, rows)
-
     grad = dot(branch_ref[...], wo_ref[...], 1, 1).astype(BF)
     query, key, value = q_ref[...], k_ref[...], v_ref[...]
     dqs, dks, dvs = [], [], []
     for head in range(2 * GROUP):
         at = slice(head * HEAD_DIM, (head + 1) * HEAD_DIM)
         kv_at = slice(head // GROUP * HEAD_DIM, (head // GROUP + 1) * HEAD_DIM)
-        scores = dot(query[:, at], key[:, kv_at], 1, 1) + bias_ref[...]
-        probs = jnp.exp(scores - lse_ref[:, head : head + 1])
+        probs_low = probs_ref[head * rows : (head + 1) * rows]
+        probs = probs_low.astype(F32)
         probs_back = dot(grad[:, at], value[:, kv_at], 1, 1)
         delta = jnp.sum(probs * probs_back, axis=1, keepdims=True)
         scores_back = (probs * (probs_back - delta)).astype(BF)
         dqs.append(dot(scores_back, key[:, kv_at]) * ATT_MULT)
         dk = dot(scores_back, query[:, at], 0, 0)
-        dv = dot(probs.astype(BF), grad[:, at], 0, 0)
+        dv = dot(probs_low, grad[:, at], 0, 0)
         if head % GROUP == 0:
             dks.append(dk)
             dvs.append(dv)
@@ -239,13 +233,13 @@
     )(me, attended, branch, normed, logits, gain)
 
 
-def run_back(me, branch, out_full, query, key, value, lse, cos, sin, normed_t, slabs):
+def run_back(me, branch, out_full, query, key, value, probs, cos, sin, normed_t, slabs):
     (rows, width), (length, key_width) = branch.shape, key.shape
     count, pairs, wide = length // rows, key_width // PAIR, GROUP * PAIR
     whole = lambda shape: pl.BlockSpec(shape, lambda p, i: (0, 0))
     column = lambda r, w: pl.BlockSpec((r, w), lambda p, i: (0, p))
     flops = 2 * width * (2 * rows * query.shape[1] + 2 * length * key_width)
-    flops += 10 * rows * length * query.shape[1]
+    flops += 8 * rows * length * query.shape[1]
     return pl.pallas_call(
         functools.partial(back_kernel, count),
         grid_spec=pltpu.PrefetchScalarGridSpec(
@@ -257,7 +251,7 @@
                 column(rows, wide),
                 column(length, PAIR),
                 column(length, PAIR),
-                column(rows, PAIR),
+                pl.BlockSpec((2 * GROUP * rows, length), lambda p, i: (p, 0)),
                 whole((length, PAIR)),
                 whole((length, PAIR)),
                 whole((width, length)),
@@ -269,7 +263,6 @@
             ]
             + [pl.BlockSpec((slabs // 2, width // slabs, wide + 2 * PAIR), lambda p, i: (0, 0, p))]
             * 2,
-            scratch_shapes=[pltpu.VMEM((rows, length), F32)],
         ),
         out_shape=[
             jax.ShapeDtypeStruct(query.shape, BF),
@@ -282,11 +275,11 @@
         ),
         cost_estimate=pl.CostEstimate(
             flops=flops,
-            bytes_accessed=2 * (length * width + 2 * width * query.shape[1]),
-            transcendentals=rows * length * query.shape[1] // HEAD_DIM,
+            bytes_accessed=2 * (length * width + 2 * width * query.shape[1] + probs.size),
+            transcendentals=0,
         ),
         name="back",
-    )(me, branch, out_full, query, key, value, lse, cos, sin, normed_t)
+    )(me, branch, out_full, query, key, value, probs, cos, sin, normed_t)
 
 
 def line_gather(block, axis, count):
@@ -399,17 +392,18 @@
 
 def expert_kernel(count, total, experts, first, me_ref, *refs):
     x_refs, g_refs, p_refs = refs[:count], refs[count : 2 * count], refs[2 * count : 3 * count]
-    gate_ref, wg_ref, wu_ref, wd_ref = refs[3 * count : 3 * count + 4]
+    gate_refs, (wg_ref, wu_ref, wd_ref) = refs[3 * count : 4 * count], refs[4 * count : 4 * count + 3]
     outs = refs[-2 * count - 1 :]
     out_refs, back_refs, grads_ref = outs[:count], outs[count : 2 * count], outs[2 * count]
     capacity, width = x_refs[0].shape
-    expert = me_ref[0] * experts + first + pl.program_id(0)
+    local = first + pl.program_id(0)
+    expert = me_ref[0] * experts + local
     x = jnp.concatenate([r[...] for r in x_refs], axis=0)
     g = jnp.concatenate([r[...] for r in g_refs], axis=0)
     gate = jnp.concatenate(
         [
-            jnp.sum(p_refs[s][...].astype(F32) * gate_ref[0, s : s + 1, :], axis=1, keepdims=True)
-            for s in range(count)
+            jnp.sum(p_ref[...].astype(F32) * gate_ref[pl.ds(local, 1), :], axis=1, keepdims=True)
+            for p_ref, gate_ref in zip(p_refs, gate_refs)
         ],
         axis=0,
     )
@@ -451,7 +445,7 @@
     weight = pl.BlockSpec((1, width, hidden), lambda e, i: (first + e, 0, 0))
     rows = width // slabs
     slots = count * number * capacity
-    inputs = [*xs, *gs, *places, gates, wg, wu, wd, *earlier]
+    inputs = [*xs, *gs, *places, *gates, wg, wu, wd, *earlier]
     return pl.pallas_call(
         functools.partial(expert_kernel, count, total, experts, first),
         grid_spec=pltpu.PrefetchScalarGridSpec(
@@ -459,7 +453,7 @@
             grid=(number,),
             in_specs=[block(width)] * (2 * count)
             + [block(places[0].shape[1])] * count
-            + [pl.BlockSpec((1,) + gates.shape[1:], lambda e, i: (first + e, 0, 0))]
+            + [pl.BlockSpec(gates[0].shape, lambda e, i: (0, 0))] * count
             + [weight] * 3
             + [pl.BlockSpec(memory_space=pl.ANY)] * len(earlier),
             out_specs=[block(width)] * count
@@ -576,7 +570,7 @@
     cot_up = cot_up + [upward(side_rows, "expert", count, s) for s in (2,) if count > 2]
 
     me_ref = jnp.stack([me, lax.axis_index("dp")]).astype(jnp.int32)
-    normed_all, side, query, key, value, attended, lse = run_front(
+    normed_all, side, query, key, value, attended, probs = run_front(
         me_ref, token_blocks, full, cos, sin, query_width, key_width, expert_total
     )
     hidden = tokens.astype(F32)
@@ -624,12 +618,12 @@
         )
         gates.append(exponent / jnp.sum(exponent, axis=1, keepdims=True))
         slot_rows.append(dot(places[s], second_blocks[s]).astype(BF))
-    gate_rows = jnp.stack(
-        [lax.dynamic_slice_in_dim(g.T, me * local_experts, local_experts, 0) for g in gates],
-        axis=1,
-    )
+    gate_rows = [
+        lax.dynamic_slice_in_dim(g.T, me * local_experts, local_experts, 0) for g in gates
+    ]
     results, expert_sums = [], []
-    for first, number in ((0, local_experts),):
+    early = max(1, local_experts // 4)
+    for first, number in ((0, early), (early, local_experts - early)):
         *results, grads = run_experts(
             me_ref,
             slot_rows,
@@ -677,7 +671,7 @@
     out_stages = slab_stages(out_state, slabs)
     out_halves = next(out_stages)
     query_pre, key_pre, value_pre, *qkv_grads = run_back(
-        me_ref, branch_back, out_full, query, key, value, lse, cos, sin, normed_t, slabs
+        me_ref, branch_back, out_full, query, key, value, probs, cos, sin, normed_t, slabs
     )
     qkv_grads, key_pre, value_pre, near, out_halves = lax.optimization_barrier(
         (qkv_grads, key_pre, value_pre, near, out_halves)

time: 577 us -> 573 us (level)
  starting transfers between devices: 87.4 us -> 77.3 us
  waiting for transfers between devices: 161 us -> 155 us
    ppermute x3, starting transfers between devices: 18.6 us -> 8.89 us  [line_gather(): lax.ppermute(right[-1], axis, [(i, i + 1) for i in range(step - 1, count...]
    ppermute x3, waiting for transfers between devices: 25.8 us -> 17 us  [line_gather(): lax.ppermute(left[-1], axis, [(i, i - 1) for i in range(1, count - step +...]
    pallas_call x1 -> x2, Pallas kernels: 64.5 us -> 70.5 us  [run_experts(): pl.pallas_call(functools.partial(expert_kernel, count, total, experts, fi...]
    unnamed x127 -> x121, local copies, waits for them, and re-layouts: 22.3 us -> 21.5 us
  transfers between devices with their start and end apart: 46 -> 47, of which waited for: 20 -> 20; matrix products, arithmetic and copies ran while one was open for 24% -> 26% of each run, Pallas kernels for 13% -> 22%
where the time goes in v4:
time: 573 us; the launch traced here: 565 us
  waiting for transfers between devices  155 us (27%)
  Pallas kernels  149 us (26%)
  starting transfers between devices  77.3 us (13%)
  local copies, waits for them, and re-layouts  71 us (12%)
  matrix products  59.9 us (10%)
  other arithmetic  36.6 us (6%)
  between operations  15.6 us (3%)
    pallas_call x2, Pallas kernels, run_experts(): pl.pallas_call(functools.partial(expert_kernel, count, total, experts, fi...  70.5 us
    dot_general x28, matrix products, dot(): lax.dot_general(a, b, (((ca,), (cb,)), ((), ())), preferred_element_type=...  59.9 us
    ppermute x10, waiting for transfers between devices, trade(): lax.ppermute(send, 'dp', [(i, i ^ 1 << bit) for i in range(slabs)])  51.3 us
    ppermute x6, waiting for transfers between devices, send_parts(): lax.ppermute(parts[s], axis, [(i, (i + count - s) % count) for i in range...  50 us
    pallas_call x1, Pallas kernels, run_back(): pl.pallas_call(functools.partial(back_kernel, count), grid_spec=pltpu.Pre...  35.1 us
    pallas_call x1, Pallas kernels, run_front(): pl.pallas_call(functools.partial(front_kernel, count, gain_at), grid_spec...  33.9 us
    optimization_barrier x2, local copies, waits for them, and re-layouts, body(): lax.optimization_barrier((up, down, turned, weights))  26.1 us
    unnamed x121, local copies, waits for them, and re-layouts  21.5 us
  transfers between devices with their start and end apart: 47, of which 20 were waited for; matrix products, arithmetic and copies ran while one was open for 26% of the time, Pallas kernels for 22%

profile of v4, /device:TPU:0, one launch (start us, length us, event | category | flops | bytes accessed | tf_op | source)
XLA Modules:
  0.0 564.7 jit_solution(15971718476069978770)
XLA Ops:
  9.7 3.2 concatenate.40
  15.0 6.5 %collective-permute-start = (bf16[256,1536]{1,0:T(8,128)(2,1)S(1)}, bf16[256,1536]{1,0:T(8,128)(2,1)}, u32[]{:S(2)}, u32[]{:S(2)}) collective-permute-start(bf16[256,1536]{1,0:T(8,128)(2,1)S(1)} %copy-done.11), channel_id=1, source_target_pairs={{0,1},{1,2},{2,3},{4,5},{5,6},{6,7},{8,9},{9,10},{10,11},{12,13},{... | collective-permute-start | bytes 2359304 | tf_op jit(solution)/shard_map/ppermute | solution.py:313
  21.4 13.2 %copy.239 = bf16[1536,8,512]{2,0,1:T(8,128)(2,1)} copy(bf16[1536,8,512]{2,1,0:T(8,128)(2,1)} %param.22) | data formatting | bytes 25165824 | tf_op args[9]
  34.6 2.7 collective-permute-done.refs_1_
  39.5 13.3 %copy.238 = bf16[1536,8,512]{2,0,1:T(8,128)(2,1)} copy(bf16[1536,8,512]{2,1,0:T(8,128)(2,1)} %param.23) | data formatting | bytes 25165824 | tf_op jit(solution)/shard_map/optimization_barrier | solution.py:560
  52.8 7.2 %collective-permute-done.3 = bf16[256,1664]{0,1:T(8,128)(2,1)} collective-permute-done((bf16[256,1664]{0,1:T(8,128)(2,1)S(1)}, bf16[256,1664]{0,1:T(8,128)(2,1)}, u32[]{:S(2)}, u32[]{:S(2)}) %collective-permute-start.3) | collective-permute-done | bytes 852000 | tf_op jit(solution)/shard_map/ppermute | solution.py:318
  67.3 12.8 %copy.237 = bf16[1536,8,512]{2,0,1:T(8,128)(2,1)} copy(bf16[1536,8,512]{2,1,0:T(8,128)(2,1)} %param.24) | data formatting | bytes 25165824 | tf_op jit(solution)/shard_map/optimization_barrier | solution.py:560
  80.2 2.7 collective-permute-done.5
  84.1 6.4 %collective-permute-start.7 = (bf16[256,1664]{0,1:T(8,128)(2,1)S(1)}, bf16[256,1664]{0,1:T(8,128)(2,1)}, u32[]{:S(2)}, u32[]{:S(2)}) collective-permute-start(bf16[256,1664]{0,1:T(8,128)(2,1)S(1)} %maximum_maximum_fusion), channel_id=1, source_target_pairs={{0,2},{1,3},{4,6},{5,7},{8,10},{9,11},{12,14},{13,15},{16,18},{17,... | collective-permute-start | bytes 2555912 | tf_op jit(solution)/shard_map/ppermute | solution.py:313
  90.5 2.7 collective-permute-start.6
  93.4 33.9 %front.1 = (bf16[1024,1536]{1,0:T(8,128)(2,1)}, f32[128,1536]{1,0:T(8,128)}, bf16[256,1536]{1,0:T(8,128)(2,1)}, bf16[1024,512]{1,0:T(8,128)(2,1)}, bf16[1024,512...) custom-call(s32[2]{0:T(128)} %pad_add_fusion.me_ref, bf16[256,1536]{1,0:T(8,128)(2,1)} %refs_0_, ...), custom_call_target="tpu_custom_call" | custom-call | flops 6039797760 | bytes 22806528 | tf_op jit(solution)/shard_map/front/pallas_call | solution.py:120
  128.9 4.1 multiply_reduce_fusion.2
  135.1 5.4 collective-permute-start.8
  149.9 2.8 collective-permute-done.9
  160.0 2.5 convolution_convert_fusion.3.refs_4_
  162.5 2.4 convolution_convert_fusion.7.refs_0_
  165.6 2.4 convolution_convert_fusion.refs_7_
  168.1 2.4 convolution_convert_fusion.1.refs_6_
  170.5 2.5 convolution_convert_fusion.2.refs_5_
  178.2 3.8 convolution_convert_fusion.5.refs_2_
  182.7 14.2 %collective-permute-done.11 = bf16[256,1536]{1,0:T(8,128)(2,1)S(1)} collective-permute-done((bf16[256,1536]{1,0:T(8,128)(2,1)}, bf16[256,1536]{1,0:T(8,128)(2,1)S(1)}, u32[]{:S(2)}, u32[]{:S(2)}) %collective-permute-start.11) | collective-permute-done | bytes 786464 | tf_op jit(solution)/shard_map/ppermute | solution.py:291
  203.3 3.9 convolution_convert_fusion.4.refs_3_
  207.2 3.5 convolution_convert_fusion.6.refs_1_
  210.7 20.6 %experts.2 = (bf16[896,1536]{1,0:T(8,128)(2,1)}, bf16[896,1536]{1,0:T(8,128)(2,1)}, bf16[896,1536]{1,0:T(8,128)(2,1)}, bf16[896,1536]{1,0:T(8,128)(2,1)}, bf16[8...) custom-call(s32[2]{0:T(128)} %pad_add_fusion.me_ref, ...), custom_call_target="tpu_custom_call" | custom-call | flops 12683575296 | bytes 29884416 | tf_op jit(solution)/shard_map/experts/pallas_call | solution.py:449
  231.9 49.9 %experts.3 = (bf16[896,1536]{1,0:T(8,128)(2,1)}, bf16[896,1536]{1,0:T(8,128)(2,1)}, bf16[896,1536]{1,0:T(8,128)(2,1)}, bf16[896,1536]{1,0:T(8,128)(2,1)}, bf16[8...) custom-call(s32[2]{0:T(128)} %pad_add_fusion.me_ref, ...), custom_call_target="tpu_custom_call", output_to_operand_aliasing={{0}: (20, {}), {1}: (21, {}), {2}: (22, {}), {3}: (23, {}),... | custom-call | flops 38050725888 | bytes 89653248 | tf_op jit(solution)/shard_map/experts/pallas_call | solution.py:449
  282.8 3.3 convolution_convert_fusion.14
  299.1 5.7 %collective-permute-done.15 = bf16[256,1664]{1,0:T(8,128)(2,1)S(1)} collective-permute-done((bf16[256,1664]{1,0:T(8,128)(2,1)S(1)}, bf16[256,1664]{1,0:T(8,128)(2,1)S(1)}, u32[]{:S(2)}, u32[]{:S(2)}) %collective-permute-start.15) | collective-permute-done | bytes 852000 | tf_op jit(solution)/shard_map/ppermute | solution.py:300
  307.7 5.0 collective-permute-start.17
  312.8 4.7 copy.217
  317.5 8.5 %collective-permute-done.17 = bf16[256,1664]{1,0:T(8,128)(2,1)} collective-permute-done((bf16[256,1664]{1,0:T(8,128)(2,1)}, bf16[256,1664]{1,0:T(8,128)(2,1)}, u32[]{:S(2)}, u32[]{:S(2)}) %collective-permute-start.17) | collective-permute-done | bytes 852000 | tf_op jit(solution)/shard_map/ppermute | solution.py:300
  330.8 6.3 %collective-permute-start.19 = (bf16[256,1664]{1,0:T(8,128)(2,1)S(1)}, bf16[256,1664]{1,0:T(8,128)(2,1)S(1)}, u32[]{:S(2)}, u32[]{:S(2)}) collective-permute-start(bf16[256,1664]{1,0:T(8,128)(2,1)S(1)} %add.263), channel_id=1, source_target_pairs={{0,1},{1,2},{2,3},{4,5},{5,6},{6,7},{8,9},{9,10},{10,11},{12,13},{... | collective-permute-start | bytes 2555912 | tf_op jit(solution)/shard_map/ppermute | solution.py:300
  338.3 8.8 %collective-permute-done.20 = bf16[256,1664]{1,0:T(8,128)(2,1)S(1)} collective-permute-done((bf16[256,1664]{1,0:T(8,128)(2,1)S(1)}, bf16[256,1664]{1,0:T(8,128)(2,1)S(1)}, u32[]{:S(2)}, u32[]{:S(2)}) %collective-permute-start.20) | collective-permute-done | bytes 852000 | tf_op jit(solution)/shard_map/ppermute | solution.py:301
  352.4 4.4 out_grad.1
  356.8 5.0 collective-permute-done.21
  365.1 4.3 collective-permute-start.22
  369.4 35.1 %back.1 = (bf16[256,1536]{1,0:T(8,128)(2,1)}, bf16[1024,512]{1,0:T(8,128)(2,1)}, bf16[1024,512]{1,0:T(8,128)(2,1)}, bf16[4,192,2560]{2,1,0:T(8,128)(2,1)}, bf16[4,192,2560]{2,1,0:T(8,128)(2,1)}) custom-call(s32[2]{0:T(128)} %pad_add_fusion.me_ref, bf16[256,1536]{1,0:T(8,128)(2,1)} %copy-done.2, bf16[1536,1536]{1,0:T(8,128)(2,1)} %all-gather.5.cloned.1.call-done.refs_1_, ...), custom_call_target="tpu_custom_call" | custom-call | flops 8858370048 | bytes 25165824 | tf_op jit(solution)/shard_map/back/pallas_call | solution.py:243
  406.9 5.2 fusion
  418.3 3.1 add.275
  423.7 5.7 %collective-permute-done.30 = bf16[96,1664]{1,0:T(8,128)(2,1)S(1)} collective-permute-done((bf16[96,1664]{1,0:T(8,128)(2,1)S(1)}, bf16[96,1664]{1,0:T(8,128)(2,1)S(1)}, u32[]{:S(2)}, u32[]{:S(2)}) %collective-permute-start.30) | collective-permute-done | bytes 319520 | tf_op jit(solution)/shard_map/ppermute | solution.py:351
  432.6 38.8 %collective-permute-done.27 = bf16[2,96,2560]{2,1,0:T(8,128)(2,1)S(1)} collective-permute-done((bf16[2,96,2560]{2,1,0:T(8,128)(2,1)S(1)}, bf16[2,96,2560]{2,1,0:T(8,128)(2,1)S(1)}, u32[]{:S(2)}, u32[]{:S(2)}) %collective-permute-start.27) | collective-permute-done | bytes 983072 | tf_op jit(solution)/shard_map/ppermute | solution.py:351
  473.2 3.8 collective-permute-start.40
  482.4 3.5 collective-permute-done.42
  486.1 22.0 %collective-permute-done.41 = bf16[48,1664]{1,0:T(8,128)(2,1)S(1)} collective-permute-done((bf16[48,1664]{1,0:T(8,128)(2,1)S(1)}, bf16[48,1664]{1,0:T(8,128)(2,1)S(1)}, u32[]{:S(2)}, u32[]{:S(2)}) %collective-permute-start.41) | collective-permute-done | bytes 159776 | tf_op jit(solution)/shard_map/ppermute | solution.py:323
  517.3 3.4 fusion.11
  522.1 10.2 %collective-permute-done.37 = bf16[48,2560]{1,0:T(8,128)(2,1)S(1)} collective-permute-done((bf16[48,2560]{1,0:T(8,128)(2,1)S(1)}, bf16[48,2560]{1,0:T(8,128)(2,1)S(1)}, u32[]{:S(2)}, u32[]{:S(2)}) %collective-permute-start.37) | collective-permute-done | bytes 245792 | tf_op jit(solution)/shard_map/ppermute | solution.py:323
  532.3 12.5 %collective-permute-done.38 = bf16[48,2560]{1,0:T(8,128)(2,1)S(1)} collective-permute-done((bf16[48,2560]{1,0:T(8,128)(2,1)S(1)}, bf16[48,2560]{1,0:T(8,128)(2,1)S(1)}, u32[]{:S(2)}, u32[]{:S(2)}) %collective-permute-start.38) | collective-permute-done | bytes 245792 | tf_op jit(solution)/shard_map/ppermute | solution.py:323
  546.5 3.0 add_convert_fusion
  552.8 4.9 owned.1
  (311 shorter events, 116.6 us)
Async XLA Ops:
  7.2 75.7 %all-gather.3.cloned.1.call-start = ((), (), s32[]{:S(2)}) async-start(), calls=%async_computation.2 | async-start | bytes 9289728 | tf_op jit(solution)/shard_map/all_gather | solution.py:543
  12.9 116.0 %all-gather.5.cloned.1.call-start = ((), (), s32[]{:S(2)}) async-start(), calls=%async_computation.3 | async-start | bytes 5308416 | tf_op jit(solution)/shard_map/all_gather | solution.py:567
  13.6 79.6 %copy-start.7 = (bf16[256,1664]{0,1:T(8,128)(2,1)}, bf16[256,1664]{0,1:T(8,128)(2,1)S(1)}, u32[]{:S(2)}) copy-start(bf16[256,1664]{0,1:T(8,128)(2,1)S(1)} %maximum_maximum_fusion) | copy-start | bytes 2555908
  13.6 23.9 %collective-permute-start.1 = (bf16[256,1664]{0,1:T(8,128)(2,1)S(1)}, bf16[256,1664]{0,1:T(8,128)(2,1)S(1)}, u32[]{:S(2)}, u32[]{:S(2)}) collective-permute-start(bf16[256,1664]{0,1:T(8,128)(2,1)S(1)} %maximum_maximum_fusion), channel_id=1, source_target_pairs={{1,0},{2,1},{3,2},{5,4},{6,5},{7,6},{9,8},{10,9},{11,10},{13,12},{... | collective-permute-start | bytes 2555912 | tf_op jit(solution)/shard_map/ppermute | solution.py:318
  15.0 22.3 %collective-permute-start = (bf16[256,1536]{1,0:T(8,128)(2,1)S(1)}, bf16[256,1536]{1,0:T(8,128)(2,1)}, u32[]{:S(2)}, u32[]{:S(2)}) collective-permute-start(bf16[256,1536]{1,0:T(8,128)(2,1)S(1)} %copy-done.11), channel_id=1, source_target_pairs={{0,1},{1,2},{2,3},{4,5},{5,6},{6,7},{8,9},{9,10},{10,11},{12,13},{... | collective-permute-start | bytes 2359304 | tf_op jit(solution)/shard_map/ppermute | solution.py:313
  37.5 22.4 %collective-permute-start.3 = (bf16[256,1664]{0,1:T(8,128)(2,1)S(1)}, bf16[256,1664]{0,1:T(8,128)(2,1)}, u32[]{:S(2)}, u32[]{:S(2)}) collective-permute-start(bf16[256,1664]{0,1:T(8,128)(2,1)S(1)} %collective-permute-done.1), channel_id=1, source_target_pairs={{1,0},{2,1},{5,4},{6,5},{9,8},{10,9},{13,12},{14,13},{17,16},{18,1... | collective-permute-start | bytes 2555912 | tf_op jit(solution)/shard_map/ppermute | solution.py:318
  38.8 14.0 %collective-permute-start.2 = (bf16[256,1536]{1,0:T(8,128)(2,1)}, bf16[256,1536]{1,0:T(8,128)(2,1)S(1)}, u32[]{:S(2)}, u32[]{:S(2)}) collective-permute-start(bf16[256,1536]{1,0:T(8,128)(2,1)} %collective-permute-done.refs_1_), channel_id=1, source_target_pairs={{1,2},{2,3},{5,6},{6,7},{9,10},{10,11},{13,14},{14,15},{17,18},{18... | collective-permute-start | bytes 2359304 | tf_op jit(solution)/shard_map/ppermute | solution.py:313
  60.0 20.2 %collective-permute-start.4 = (bf16[256,1536]{1,0:T(8,128)(2,1)S(1)}, bf16[256,1536]{1,0:T(8,128)(2,1)}, u32[]{:S(2)}, u32[]{:S(2)}) collective-permute-start(bf16[256,1536]{1,0:T(8,128)(2,1)S(1)} %collective-permute-done.2.refs_2_), channel_id=1, source_target_pairs={{2,3},{6,7},{10,11},{14,15},{18,19},{22,23},{26,27},{30,31}} | collective-permute-start | bytes 2359304 | tf_op jit(solution)/shard_map/ppermute | solution.py:313
  61.5 21.4 %collective-permute-start.5 = (bf16[256,1664]{0,1:T(8,128)(2,1)}, bf16[256,1664]{0,1:T(8,128)(2,1)}, u32[]{:S(2)}, u32[]{:S(2)}) collective-permute-start(bf16[256,1664]{0,1:T(8,128)(2,1)} %collective-permute-done.3), channel_id=1, source_target_pairs={{1,0},{5,4},{9,8},{13,12},{17,16},{21,20},{25,24},{29,28}} | collective-permute-start | bytes 2555912 | tf_op jit(solution)/shard_map/ppermute | solution.py:318
  82.9 466.6 %reduce-scatter.3.cloned.1.call-start = ((), (), s32[]{:S(2)}) async-start(), calls=%async_computation.4 | async-start | bytes 10616832 | tf_op jit(solution)/shard_map/reduce_scatter | solution.py:642
  84.1 56.4 %collective-permute-start.7 = (bf16[256,1664]{0,1:T(8,128)(2,1)S(1)}, bf16[256,1664]{0,1:T(8,128)(2,1)}, u32[]{:S(2)}, u32[]{:S(2)}) collective-permute-start(bf16[256,1664]{0,1:T(8,128)(2,1)S(1)} %maximum_maximum_fusion), channel_id=1, source_target_pairs={{0,2},{1,3},{4,6},{5,7},{8,10},{9,11},{12,14},{13,15},{16,18},{17,... | collective-permute-start | bytes 2555912 | tf_op jit(solution)/shard_map/ppermute | solution.py:313
  90.5 50.0 %collective-permute-start.6 = (bf16[256,1664]{0,1:T(8,128)(2,1)S(1)}, bf16[256,1664]{0,1:T(8,128)(2,1)}, u32[]{:S(2)}, u32[]{:S(2)}) collective-permute-start(bf16[256,1664]{0,1:T(8,128)(2,1)S(1)} %maximum_maximum_fusion), channel_id=1, source_target_pairs={{0,1},{1,2},{2,3},{4,5},{5,6},{6,7},{8,9},{9,10},{10,11},{12,13},{... | collective-permute-start | bytes 2555912 | tf_op jit(solution)/shard_map/ppermute | solution.py:313
  133.8 18.9 %collective-permute-start.9 = (bf16[256,1536]{1,0:T(8,128)(2,1)S(1)}, bf16[256,1536]{1,0:T(8,128)(2,1)}, u32[]{:S(2)}, u32[]{:S(2)}) collective-permute-start(bf16[256,1536]{1,0:T(8,128)(2,1)S(1)} %multiply_convert_fusion.1.normed_ref), channel_id=1, source_target_pairs={{1,0},{2,1},{3,2},{5,4},{6,5},{7,6},{9,8},{10,9},{11,10},{13,12},{... | collective-permute-start | bytes 2359304 | tf_op jit(solution)/shard_map/ppermute | solution.py:291
  135.1 18.9 %collective-permute-start.8 = (bf16[256,1536]{1,0:T(8,128)(2,1)S(1)}, bf16[256,1536]{1,0:T(8,128)(2,1)}, u32[]{:S(2)}, u32[]{:S(2)}) collective-permute-start(bf16[256,1536]{1,0:T(8,128)(2,1)S(1)} %multiply_convert_fusion.1.normed_ref), channel_id=1, source_target_pairs={{0,1},{1,2},{2,3},{4,5},{5,6},{6,7},{8,9},{9,10},{10,11},{12,13},{... | collective-permute-start | bytes 2359304 | tf_op jit(solution)/shard_map/ppermute | solution.py:289
  143.6 12.2 %collective-permute-start.13 = (bf16[256,1664]{0,1:T(8,128)(2,1)}, bf16[256,1664]{0,1:T(8,128)(2,1)}, u32[]{:S(2)}, u32[]{:S(2)}) collective-permute-start(bf16[256,1664]{0,1:T(8,128)(2,1)} %collective-permute-done.7), channel_id=1, source_target_pairs={{2,3},{6,7},{10,11},{14,15},{18,19},{22,23},{26,27},{30,31}} | collective-permute-start | bytes 2555912 | tf_op jit(solution)/shard_map/ppermute | solution.py:313
  152.8 20.2 %collective-permute-start.10 = (bf16[256,1536]{1,0:T(8,128)(2,1)}, bf16[256,1536]{1,0:T(8,128)(2,1)}, u32[]{:S(2)}, u32[]{:S(2)}) collective-permute-start(bf16[256,1536]{1,0:T(8,128)(2,1)} %collective-permute-done.9), channel_id=1, source_target_pairs={{1,0},{2,1},{5,4},{6,5},{9,8},{10,9},{13,12},{14,13},{17,16},{18,1... | collective-permute-start | bytes 2359304 | tf_op jit(solution)/shard_map/ppermute | solution.py:291
  154.1 20.2 %collective-permute-start.12 = (bf16[256,1536]{1,0:T(8,128)(2,1)}, bf16[256,1536]{1,0:T(8,128)(2,1)}, u32[]{:S(2)}, u32[]{:S(2)}) collective-permute-start(bf16[256,1536]{1,0:T(8,128)(2,1)} %collective-permute-done.8), channel_id=1, source_target_pairs={{1,2},{2,3},{5,6},{6,7},{9,10},{10,11},{13,14},{14,15},{17,18},{18... | collective-permute-start | bytes 2359304 | tf_op jit(solution)/shard_map/ppermute | solution.py:289
  173.0 23.9 %collective-permute-start.11 = (bf16[256,1536]{1,0:T(8,128)(2,1)}, bf16[256,1536]{1,0:T(8,128)(2,1)S(1)}, u32[]{:S(2)}, u32[]{:S(2)}) collective-permute-start(bf16[256,1536]{1,0:T(8,128)(2,1)} %collective-permute-done.10), channel_id=1, source_target_pairs={{1,0},{5,4},{9,8},{13,12},{17,16},{21,20},{25,24},{29,28}} | collective-permute-start | bytes 2359304 | tf_op jit(solution)/shard_map/ppermute | solution.py:291
  174.3 25.3 %collective-permute-start.14 = (bf16[256,1536]{1,0:T(8,128)(2,1)}, bf16[256,1536]{1,0:T(8,128)(2,1)}, u32[]{:S(2)}, u32[]{:S(2)}) collective-permute-start(bf16[256,1536]{1,0:T(8,128)(2,1)} %collective-permute-done.12), channel_id=1, source_target_pairs={{2,3},{6,7},{10,11},{14,15},{18,19},{22,23},{26,27},{30,31}} | collective-permute-start | bytes 2359304 | tf_op jit(solution)/shard_map/ppermute | solution.py:289
  231.4 318.1 %reduce-scatter.5.cloned.1.call-start = ((), (), s32[]{:S(2)}) async-start(), calls=%async_computation.5 | async-start | bytes 31850496 | tf_op jit(solution)/shard_map/reduce_scatter | solution.py:642
  286.1 13.0 %collective-permute-start.16 = (bf16[256,1664]{1,0:T(8,128)(2,1)S(1)}, bf16[256,1664]{1,0:T(8,128)(2,1)S(1)}, u32[]{:S(2)}, u32[]{:S(2)}) collective-permute-start(bf16[256,1664]{1,0:T(8,128)(2,1)S(1)} %convolution_convert_fusion.14), channel_id=1, source_target_pairs={{3,2},{7,6},{11,10},{15,14},{19,18},{23,22},{27,26},{31,30}} | collective-permute-start | bytes 2555912 | tf_op jit(solution)/shard_map/ppermute | solution.py:301
  288.2 16.7 %collective-permute-start.15 = (bf16[256,1664]{1,0:T(8,128)(2,1)S(1)}, bf16[256,1664]{1,0:T(8,128)(2,1)S(1)}, u32[]{:S(2)}, u32[]{:S(2)}) collective-permute-start(bf16[256,1664]{1,0:T(8,128)(2,1)S(1)} %convolution_convert_fusion.15), channel_id=1, source_target_pairs={{0,1},{4,5},{8,9},{12,13},{16,17},{20,21},{24,25},{28,29}} | collective-permute-start | bytes 2555912 | tf_op jit(solution)/shard_map/ppermute | solution.py:300
  306.1 11.4 %collective-permute-start.18 = (bf16[256,1664]{1,0:T(8,128)(2,1)}, bf16[256,1664]{1,0:T(8,128)(2,1)}, u32[]{:S(2)}, u32[]{:S(2)}) collective-permute-start(bf16[256,1664]{1,0:T(8,128)(2,1)} %get-tuple-element.317), channel_id=1, source_target_pairs={{2,1},{3,2},{6,5},{7,6},{10,9},{11,10},{14,13},{15,14},{18,17},{19... | collective-permute-start | bytes 2555912 | tf_op jit(solution)/shard_map/ppermute | solution.py:301
  307.7 18.3 %collective-permute-start.17 = (bf16[256,1664]{1,0:T(8,128)(2,1)}, bf16[256,1664]{1,0:T(8,128)(2,1)}, u32[]{:S(2)}, u32[]{:S(2)}) collective-permute-start(bf16[256,1664]{1,0:T(8,128)(2,1)} %get-tuple-element.318), channel_id=1, source_target_pairs={{0,1},{1,2},{4,5},{5,6},{8,9},{9,10},{12,13},{13,14},{16,17},{17,1... | collective-permute-start | bytes 2555912 | tf_op jit(solution)/shard_map/ppermute | solution.py:300
  329.5 17.6 %collective-permute-start.20 = (bf16[256,1664]{1,0:T(8,128)(2,1)S(1)}, bf16[256,1664]{1,0:T(8,128)(2,1)S(1)}, u32[]{:S(2)}, u32[]{:S(2)}) collective-permute-start(bf16[256,1664]{1,0:T(8,128)(2,1)S(1)} %add.265), channel_id=1, source_target_pairs={{1,0},{2,1},{3,2},{5,4},{6,5},{7,6},{9,8},{10,9},{11,10},{13,12},{... | collective-permute-start | bytes 2555912 | tf_op jit(solution)/shard_map/ppermute | solution.py:301
  330.8 17.5 %collective-permute-start.19 = (bf16[256,1664]{1,0:T(8,128)(2,1)S(1)}, bf16[256,1664]{1,0:T(8,128)(2,1)S(1)}, u32[]{:S(2)}, u32[]{:S(2)}) collective-permute-start(bf16[256,1664]{1,0:T(8,128)(2,1)S(1)} %add.263), channel_id=1, source_target_pairs={{0,1},{1,2},{2,3},{4,5},{5,6},{6,7},{8,9},{9,10},{10,11},{12,13},{... | collective-permute-start | bytes 2555912 | tf_op jit(solution)/shard_map/ppermute | solution.py:300
  356.8 5.0 collective-permute-start.21
  362.5 42.0 %collective-permute-start.25 = (bf16[2,96,1664]{2,1,0:T(8,128)(2,1)S(1)}, bf16[2,96,1664]{2,1,0:T(8,128)(2,1)S(1)}, u32[]{:S(2)}, u32[]{:S(2)}) collective-permute-start(bf16[2,96,1664]{2,1,0:T(8,128)(2,1)S(1)} %slice_bitcast_fusion.4), channel_id=1, source_target_pairs={{0,16},{4,20},{8,24},{12,28},{16,0},{20,4},{24,8},{28,12},{1,17},{... | collective-permute-start | bytes 1916936 | tf_op jit(solution)/shard_map/ppermute | solution.py:351
  363.8 40.7 %collective-permute-start.24 = (bf16[2,96,1664]{2,1,0:T(8,128)(2,1)S(1)}, bf16[2,96,1664]{2,1,0:T(8,128)(2,1)S(1)}, u32[]{:S(2)}, u32[]{:S(2)}) collective-permute-start(bf16[2,96,1664]{2,1,0:T(8,128)(2,1)S(1)} %slice_bitcast_fusion.6), channel_id=1, source_target_pairs={{0,8},{4,12},{8,0},{12,4},{16,24},{20,28},{24,16},{28,20},{1,9},{5... | collective-permute-start | bytes 1916936 | tf_op jit(solution)/shard_map/ppermute | solution.py:351
  365.1 39.5 %collective-permute-start.22 = (bf16[256,1536]{1,0:T(8,128)(2,1)}, bf16[256,1536]{1,0:T(8,128)(2,1)}, u32[]{:S(2)}, u32[]{:S(2)}) collective-permute-start(bf16[256,1536]{1,0:T(8,128)(2,1)} %convolution_convert_fusion.10), channel_id=1, source_target_pairs={{0,3},{1,0},{2,1},{3,2},{4,7},{5,4},{6,5},{7,6},{8,11},{9,8},{10,9... | collective-permute-start | bytes 2359304 | tf_op jit(solution)/shard_map/ppermute | solution.py:331
  369.4 35.2 %collective-permute-start.23 = (bf16[256,1536]{1,0:T(8,128)(2,1)}, bf16[256,1536]{1,0:T(8,128)(2,1)}, u32[]{:S(2)}, u32[]{:S(2)}) collective-permute-start(bf16[256,1536]{1,0:T(8,128)(2,1)} %convolution_convert_fusion.8), channel_id=1, source_target_pairs={{0,1},{1,2},{2,3},{3,0},{4,5},{5,6},{6,7},{7,4},{8,9},{9,10},{10,1... | collective-permute-start | bytes 2359304 | tf_op jit(solution)/shard_map/ppermute | solution.py:331
  404.7 13.7 %collective-permute-start.26 = (bf16[4,192,2560]{2,1,0:T(8,128)(2,1)}, bf16[4,192,2560]{2,1,0:T(8,128)(2,1)}, u32[]{:S(2)}, u32[]{:S(2)}) collective-permute-start(bf16[4,192,2560]{2,1,0:T(8,128)(2,1)} %get-tuple-element.191), channel_id=1, source_target_pairs={{0,4},{4,0},{8,12},{12,8},{16,20},{20,16},{24,28},{28,24},{1,5},{5... | collective-permute-start | bytes 11796488 | tf_op jit(solution)/shard_map/ppermute | solution.py:351
  412.1 17.3 %collective-permute-start.30 = (bf16[96,1664]{1,0:T(8,128)(2,1)S(1)}, bf16[96,1664]{1,0:T(8,128)(2,1)S(1)}, u32[]{:S(2)}, u32[]{:S(2)}) collective-permute-start(bf16[96,1664]{1,0:T(8,128)(2,1)S(1)} %slice_bitcast_fusion.10), channel_id=1, source_target_pairs={{0,8},{4,12},{8,0},{12,4},{16,24},{20,28},{24,16},{28,20},{1,9},{5... | collective-permute-start | bytes 958472 | tf_op jit(solution)/shard_map/ppermute | solution.py:351
  413.7 17.3 %collective-permute-start.29 = (bf16[96,1664]{1,0:T(8,128)(2,1)S(1)}, bf16[96,1664]{1,0:T(8,128)(2,1)S(1)}, u32[]{:S(2)}, u32[]{:S(2)}) collective-permute-start(bf16[96,1664]{1,0:T(8,128)(2,1)S(1)} %slice_bitcast_fusion.11), channel_id=1, source_target_pairs={{0,16},{4,20},{8,24},{12,28},{16,0},{20,4},{24,8},{28,12},{1,17},{... | collective-permute-start | bytes 958472 | tf_op jit(solution)/shard_map/ppermute | solution.py:351
  416.2 56.9 %collective-permute-start.31 = (bf16[256,1024]{1,0:T(8,128)(2,1)S(1)}, bf16[256,1024]{1,0:T(8,128)(2,1)S(1)}, u32[]{:S(2)}, u32[]{:S(2)}) collective-permute-start(bf16[256,1024]{1,0:T(8,128)(2,1)S(1)} %pad_maximum_fusion.2), channel_id=1, source_target_pairs={{1,0},{2,1},{3,2},{5,4},{6,5},{7,6},{9,8},{10,9},{11,10},{13,12},{... | collective-permute-start | bytes 1572872 | tf_op jit(solution)/shard_map/ppermute | solution.py:318
  421.6 49.7 %collective-permute-start.27 = (bf16[2,96,2560]{2,1,0:T(8,128)(2,1)S(1)}, bf16[2,96,2560]{2,1,0:T(8,128)(2,1)S(1)}, u32[]{:S(2)}, u32[]{:S(2)}) collective-permute-start(bf16[2,96,2560]{2,1,0:T(8,128)(2,1)S(1)} %slice_bitcast_fusion.2), channel_id=1, source_target_pairs={{0,8},{4,12},{8,0},{12,4},{16,24},{20,28},{24,16},{28,20},{1,9},{5... | collective-permute-start | bytes 2949128 | tf_op jit(solution)/shard_map/ppermute | solution.py:351
  423.6 49.3 %collective-permute-start.28 = (bf16[2,96,2560]{2,1,0:T(8,128)(2,1)S(1)}, bf16[2,96,2560]{2,1,0:T(8,128)(2,1)S(1)}, u32[]{:S(2)}, u32[]{:S(2)}) collective-permute-start(bf16[2,96,2560]{2,1,0:T(8,128)(2,1)S(1)} %slice_bitcast_fusion), channel_id=1, source_target_pairs={{0,16},{4,20},{8,24},{12,28},{16,0},{20,4},{24,8},{28,12},{1,17},{... | collective-permute-start | bytes 2949128 | tf_op jit(solution)/shard_map/ppermute | solution.py:351
  429.4 43.7 %collective-permute-start.32 = (bf16[256,1024]{1,0:T(8,128)(2,1)S(1)}, bf16[256,1024]{1,0:T(8,128)(2,1)S(1)}, u32[]{:S(2)}, u32[]{:S(2)}) collective-permute-start(bf16[256,1024]{1,0:T(8,128)(2,1)S(1)} %pad_maximum_fusion.3), channel_id=1, source_target_pairs={{2,0},{3,1},{6,4},{7,5},{10,8},{11,9},{14,12},{15,13},{18,16},{19,... | collective-permute-start | bytes 1572872 | tf_op jit(solution)/shard_map/ppermute | solution.py:318
  431.0 84.0 %collective-permute-start.36 = (bf16[256,1024]{1,0:T(8,128)(2,1)}, bf16[256,1024]{1,0:T(8,128)(2,1)}, u32[]{:S(2)}, u32[]{:S(2)}) collective-permute-start(bf16[256,1024]{1,0:T(8,128)(2,1)} %pad_maximum_fusion.4), channel_id=1, source_target_pairs={{3,0},{7,4},{11,8},{15,12},{19,16},{23,20},{27,24},{31,28}} | collective-permute-start | bytes 1572872 | tf_op jit(solution)/shard_map/ppermute | solution.py:318
  473.2 8.4 %collective-permute-start.40 = (bf16[48,1664]{1,0:T(8,128)(2,1)S(1)}, bf16[48,1664]{1,0:T(8,128)(2,1)S(1)}, u32[]{:S(2)}, u32[]{:S(2)}) collective-permute-start(bf16[48,1664]{1,0:T(8,128)(2,1)S(1)} %get-tuple-element.327), channel_id=1, source_target_pairs={{0,3},{1,0},{2,1},{3,2},{4,7},{5,4},{6,5},{7,6},{8,11},{9,8},{10,9... | collective-permute-start | bytes 479240 | tf_op jit(solution)/shard_map/ppermute | solution.py:323
  477.0 8.9 %collective-permute-start.42 = (bf16[48,1664]{1,0:T(8,128)(2,1)S(1)}, bf16[48,1664]{1,0:T(8,128)(2,1)S(1)}, u32[]{:S(2)}, u32[]{:S(2)}) collective-permute-start(bf16[48,1664]{1,0:T(8,128)(2,1)S(1)} %get-tuple-element.328), channel_id=1, source_target_pairs={{0,1},{1,2},{2,3},{3,0},{4,5},{5,6},{6,7},{7,4},{8,9},{9,10},{10,1... | collective-permute-start | bytes 479240 | tf_op jit(solution)/shard_map/ppermute | solution.py:323
  477.0 31.1 %collective-permute-start.41 = (bf16[48,1664]{1,0:T(8,128)(2,1)S(1)}, bf16[48,1664]{1,0:T(8,128)(2,1)S(1)}, u32[]{:S(2)}, u32[]{:S(2)}) collective-permute-start(bf16[48,1664]{1,0:T(8,128)(2,1)S(1)} %get-tuple-element.329), channel_id=1, source_target_pairs={{0,2},{1,3},{2,0},{3,1},{4,6},{5,7},{6,4},{7,5},{8,10},{9,11},{10,... | collective-permute-start | bytes 479240 | tf_op jit(solution)/shard_map/ppermute | solution.py:323
  479.3 33.3 %collective-permute-start.35 = (bf16[96,2560]{1,0:T(8,128)(2,1)}, bf16[96,2560]{1,0:T(8,128)(2,1)}, u32[]{:S(2)}, u32[]{:S(2)}) collective-permute-start(bf16[96,2560]{1,0:T(8,128)(2,1)} %slice_bitcast_fusion.8), channel_id=1, source_target_pairs={{0,8},{4,12},{8,0},{12,4},{16,24},{20,28},{24,16},{28,20},{1,9},{5... | collective-permute-start | bytes 1474568 | tf_op jit(solution)/shard_map/ppermute | solution.py:351
  481.6 32.1 %collective-permute-start.34 = (bf16[96,2560]{1,0:T(8,128)(2,1)}, bf16[96,2560]{1,0:T(8,128)(2,1)}, u32[]{:S(2)}, u32[]{:S(2)}) collective-permute-start(bf16[96,2560]{1,0:T(8,128)(2,1)} %slice_bitcast_fusion.9), channel_id=1, source_target_pairs={{0,16},{4,20},{8,24},{12,28},{16,0},{20,4},{24,8},{28,12},{1,17},{... | collective-permute-start | bytes 1474568 | tf_op jit(solution)/shard_map/ppermute | solution.py:351
  485.9 60.2 %collective-permute-start.33 = (bf16[256,1536]{1,0:T(8,128)(2,1)}, bf16[256,1536]{1,0:T(8,128)(2,1)}, u32[]{:S(2)}, u32[]{:S(2)}) collective-permute-start(bf16[256,1536]{1,0:T(8,128)(2,1)} %convolution_convert_fusion.9), channel_id=1, source_target_pairs={{0,2},{1,3},{2,0},{3,1},{4,6},{5,7},{6,4},{7,5},{8,10},{9,11},{10,... | collective-permute-start | bytes 2359304 | tf_op jit(solution)/shard_map/ppermute | solution.py:338
  515.2 17.1 %collective-permute-start.37 = (bf16[48,2560]{1,0:T(8,128)(2,1)S(1)}, bf16[48,2560]{1,0:T(8,128)(2,1)S(1)}, u32[]{:S(2)}, u32[]{:S(2)}) collective-permute-start(bf16[48,2560]{1,0:T(8,128)(2,1)S(1)} %get-tuple-element.314), channel_id=1, source_target_pairs={{0,3},{1,0},{2,1},{3,2},{4,7},{5,4},{6,5},{7,6},{8,11},{9,8},{10,9... | collective-permute-start | bytes 737288 | tf_op jit(solution)/shard_map/ppermute | solution.py:323
  516.4 15.9 %collective-permute-start.39 = (bf16[48,2560]{1,0:T(8,128)(2,1)S(1)}, bf16[48,2560]{1,0:T(8,128)(2,1)S(1)}, u32[]{:S(2)}, u32[]{:S(2)}) collective-permute-start(bf16[48,2560]{1,0:T(8,128)(2,1)S(1)} %get-tuple-element.315), channel_id=1, source_target_pairs={{0,1},{1,2},{2,3},{3,0},{4,5},{5,6},{6,7},{7,4},{8,9},{9,10},{10,1... | collective-permute-start | bytes 737288 | tf_op jit(solution)/shard_map/ppermute | solution.py:323
  517.2 27.6 %collective-permute-start.38 = (bf16[48,2560]{1,0:T(8,128)(2,1)S(1)}, bf16[48,2560]{1,0:T(8,128)(2,1)S(1)}, u32[]{:S(2)}, u32[]{:S(2)}) collective-permute-start(bf16[48,2560]{1,0:T(8,128)(2,1)S(1)} %get-tuple-element.316), channel_id=1, source_target_pairs={{0,2},{1,3},{2,0},{3,1},{4,6},{5,7},{6,4},{7,5},{8,10},{9,11},{10,... | collective-permute-start | bytes 737288 | tf_op jit(solution)/shard_map/ppermute | solution.py:323
  (55 other events, 430.9 us)
Sparse Core Ops, SparseCore 0:
  13.0 56.5 all-gather.2
  83.0 40.0 all-gather.4
  231.5 84.8 reduce-scatter.2
  320.0 218.4 reduce-scatter.4
